TPU v7x, 32 devices: a whole 2x2x4 slice. The times are simulated.
32 devices in a mesh: row: 4 (over z), col: 4 (over y, core), layer: 2 (over x).
Axes of the slice: x: 2, y: 2, z: 4, core: 2. Of those that a mesh axis runs over, the one named last changes fastest.
Arguments:
- density: bfloat16 [16, 13, 256, 256], P(('row', 'col')), as said below
- pattern: int32 [16, 13], P(('row', 'col')), may hold values from 0 to 1, as said below
Outputs:
- purified: float32 [16, 13, 256, 256], P(('row', 'col'), None, None, 'layer')
Inputs may be any that keep to these rules, and one draw needn't show every extreme that they name: pattern[i, 6 + d] = pattern[i + d mod 16, 6 - d], and pattern[i, 6] = 1. density[i, 6 + d] is the transpose of density[i + d mod 16, 6 - d], and it is zero where pattern is 0.
All inputs are finite; a program needn't handle non-finite values.
Results may differ from a plain program's by a relative error of at most 0.0039.
The roundings to bfloat16 on the way count: a program that leaves them out, or rounds other values in their place, can miss the bound.
Values may be sent and summed in bfloat16 or wider, within the bound.
No kernel may reach another device: no remote copies, remote signals or barrier semaphores. Data moves between devices by JAX's collectives and lax.ppermute only.
A program may use at most 64 MiB of HBM per device.

v0:
```python
from functools import reduce

import jax
import jax.numpy as jnp
from jax import lax
from jax.sharding import PartitionSpec as P


def shifted(array, axis, by):
    peers = lax.axis_size(axis)
    return lax.ppermute(array, axis, [(i, (i + by) % peers) for i in range(peers)])


def band_product(factor, neighbour_rows, half):
    band = 2 * half + 1
    collected = [[] for position in range(band)]
    for offset in range(-half, half + 1):
        right_rows = neighbour_rows(offset)
        if offset >= 0:
            first = offset
            source = right_rows[:, : band - offset]
        else:
            first = 0
            source = right_rows[:, -offset:]
        product = jnp.einsum(
            "rab,rdbc->rdac", factor[:, half + offset], source, preferred_element_type=jnp.float32
        )
        for column in range(product.shape[1]):
            collected[first + column].append(product[:, column])
    return jnp.stack(
        [
            reduce(lambda first_item, second_item: first_item + second_item, items)
            for items in collected
        ],
        axis=1,
    )


def body(density, pattern):
    n_layer = lax.axis_size("layer")
    layer_index = lax.axis_index("layer")
    brows = density.shape[0]
    band = density.shape[1]
    block = density.shape[2]
    half = band // 2
    width = block // n_layer
    reach = (half + brows - 1) // brows
    slab = lax.dynamic_slice_in_dim(density, layer_index * width, width, 3)
    before = []
    after = []
    for distance in range(reach, 0, -1):
        before.append(shifted(slab, ("row", "col"), distance))
    for distance in range(1, reach + 1):
        after.append(shifted(slab, ("row", "col"), -distance))
    pieces = before + [slab] + after
    centre = reach * brows

    def neighbour_rows(offset):
        return pieces[centre + offset]

    keep = pattern.astype(jnp.float32)[:, :, None, None]
    square = band_product(density, neighbour_rows, half) * keep
    square_half = square.astype(jnp.bfloat16)
    square_rows = lax.all_gather(square_half, "layer", axis=3, tiled=True)
    cube = band_product(square_rows, neighbour_rows, half) * keep
    return 3.0 * square - 2.0 * cube


def solution(mesh):
    return jax.shard_map(
        body,
        mesh=mesh,
        in_specs=(P(("row", "col"), None, None, None), P(("row", "col"), None)),
        out_specs=P(("row", "col"), None, None, "layer"),
        check_vma=False,
    )
```

profile of v0, /device:TPU:0, one launch (start us, length us, event | category | flops | bytes accessed | tf_op | source)
XLA Modules:
  0.0 301.7 jit_solution(17502194435136577396)
XLA Ops:
  6.5 1.3 constant_dynamic-slice_fusion
  7.9 1.3 copy.44
  9.1 2.4 collective-permute-start.3
  11.6 1.6 collective-permute-start.2
  13.1 1.6 collective-permute-start.1
  14.8 2.2 collective-permute-start.9
  17.0 0.8 collective-permute-start.8
  17.8 13.7 %collective-permute-done.3 = bf16[1,13,256,128]{2,3,1,0:T(8,128)(2,1)S(1)} collective-permute-done((bf16[1,13,256,128]{2,3,1,0:T(8,128)(2,1)}, bf16[1,13,256,128]{2,3,1,0:T(8,128)(2,1)S(1)}, u32[]{:S(2)}, u32[]{:S(2)}) %collective-permute-start.3) | collective-permute-done | bytes 852000 | tf_op jit(solution)/shard_map/ppermute | solution.py:11
  31.5 3.7 %collective-permute-start.4 = (bf16[1,13,256,128]{2,3,1,0:T(8,128)(2,1)}, bf16[1,13,256,128]{2,3,1,0:T(8,128)(2,1)S(1)}, u32[]{:S(2)}, u32[]{:S(2)}) collective-permute-start(bf16[1,13,256,128]{2,3,1,0:T(8,128)(2,1)} %copy.44), channel_id=1, source_target_pairs={{0,4},{2,6},{4,8},{6,10},{8,12},{10,14},{12,16},{14,18},{16,20},{1... | collective-permute-start | bytes 2555912 | tf_op jit(solution)/shard_map/ppermute | solution.py:11
  35.2 0.4 convolution_bitcast_fusion.1
  35.7 19.1 %collective-permute-start.7 = (bf16[1,13,256,128]{2,3,1,0:T(8,128)(2,1)S(1)}, bf16[1,13,256,128]{2,3,1,0:T(8,128)(2,1)S(1)}, u32[]{:S(2)}, u32[]{:S(2)}) collective-permute-start(bf16[1,13,256,128]{2,3,1,0:T(8,128)(2,1)S(1)} %copy-done.23), channel_id=1, source_target_pairs={{0,28},{2,30},{4,0},{6,2},{8,4},{10,6},{12,8},{14,10},{16,12},{18,... | collective-permute-start | bytes 2555912 | tf_op jit(solution)/shard_map/ppermute | solution.py:11
  54.8 0.4 convolution_bitcast_fusion.13
  55.2 34.6 %collective-permute-done.1 = bf16[1,13,256,128]{2,3,1,0:T(8,128)(2,1)S(1)} collective-permute-done((bf16[1,13,256,128]{2,3,1,0:T(8,128)(2,1)}, bf16[1,13,256,128]{2,3,1,0:T(8,128)(2,1)S(1)}, u32[]{:S(2)}, u32[]{:S(2)}) %collective-permute-start.1) | collective-permute-done | bytes 852000 | tf_op jit(solution)/shard_map/ppermute | solution.py:11
  89.7 0.3 convolution_bitcast_fusion.17
  90.1 19.6 %collective-permute-start.6 = (bf16[1,13,256,128]{2,3,1,0:T(8,128)(2,1)S(1)}, bf16[1,13,256,128]{2,3,1,0:T(8,128)(2,1)S(1)}, u32[]{:S(2)}, u32[]{:S(2)}) collective-permute-start(bf16[1,13,256,128]{2,3,1,0:T(8,128)(2,1)S(1)} %copy-done.23), channel_id=1, source_target_pairs={{0,30},{2,0},{4,2},{6,4},{8,6},{10,8},{12,10},{14,12},{16,14},{18,... | collective-permute-start | bytes 2555912 | tf_op jit(solution)/shard_map/ppermute | solution.py:11
  109.7 0.3 convolution_bitcast_fusion.16
  110.1 0.3 convolution_bitcast_fusion.21
  110.5 0.4 convolution_bitcast_fusion.12
  111.0 12.7 %collective-permute-done.4 = bf16[1,13,256,128]{2,3,1,0:T(8,128)(2,1)S(1)} collective-permute-done((bf16[1,13,256,128]{2,3,1,0:T(8,128)(2,1)}, bf16[1,13,256,128]{2,3,1,0:T(8,128)(2,1)S(1)}, u32[]{:S(2)}, u32[]{:S(2)}) %collective-permute-start.4) | collective-permute-done | bytes 852000 | tf_op jit(solution)/shard_map/ppermute | solution.py:11
  123.7 30.4 %collective-permute-start.10 = (bf16[1,13,256,128]{2,3,1,0:T(8,128)(2,1)S(1)}, bf16[1,13,256,128]{2,3,1,0:T(8,128)(2,1)S(1)}, u32[]{:S(2)}, u32[]{:S(2)}) collective-permute-start(bf16[1,13,256,128]{2,3,1,0:T(8,128)(2,1)S(1)} %copy-done.23), channel_id=1, source_target_pairs={{0,22},{2,24},{4,26},{6,28},{8,30},{10,0},{12,2},{14,4},{16,6},{18... | collective-permute-start | bytes 2555912 | tf_op jit(solution)/shard_map/ppermute | solution.py:11
  154.2 0.4 convolution_bitcast_fusion.9
  154.6 2.6 collective-permute-start.11
  157.1 0.4 convolution_bitcast_fusion.8
  157.5 0.4 convolution_bitcast_fusion.5
  157.9 0.4 convolution_bitcast_fusion.4
  158.3 14.7 %collective-permute-done = bf16[1,13,256,128]{2,3,1,0:T(8,128)(2,1)S(1)} collective-permute-done((bf16[1,13,256,128]{2,3,1,0:T(8,128)(2,1)S(1)}, bf16[1,13,256,128]{2,3,1,0:T(8,128)(2,1)S(1)}, u32[]{:S(2)}, u32[]{:S(2)}) %collective-permute-start) | collective-permute-done | bytes 852000 | tf_op jit(solution)/shard_map/ppermute | solution.py:11
  173.0 0.3 convolution_bitcast_fusion.25
  173.5 0.5 copy-done.21
  174.0 1.4 convolution_bitcast_fusion.20
  175.7 33.4 %collective-permute-done.11 = bf16[1,13,256,128]{2,3,1,0:T(8,128)(2,1)S(1)} collective-permute-done((bf16[1,13,256,128]{2,3,1,0:T(8,128)(2,1)S(1)}, bf16[1,13,256,128]{2,3,1,0:T(8,128)(2,1)S(1)}, u32[]{:S(2)}, u32[]{:S(2)}) %collective-permute-start.11) | collective-permute-done | bytes 852000 | tf_op jit(solution)/shard_map/ppermute | solution.py:11
  209.1 1.3 convolution_bitcast_fusion.24
  210.5 0.1 fusion.21
  211.1 1.1 multiply_convert_fusion
  212.3 65.3 %all-gather.2.cloned.1.call-done = bf16[1,13,256,256]{2,3,1,0:T(8,128)(2,1)} async-done(((bf16[1,13,256,128]{2,3,1,0:T(8,128)(2,1)}), bf16[1,13,256,256]{2,3,1,0:T(8,128)(2,1)}) %all-gather.2.cloned.1.call-update) | async-done | bytes 1703952 | tf_op jit(solution)/shard_map/all_gather | solution.py:64
  277.6 1.6 convolution_bitcast_fusion.7
  279.3 1.4 convolution_bitcast_fusion.11
  280.7 0.1 copy-done.10
  280.8 0.3 convolution_bitcast_fusion.15
  281.1 0.3 convolution_bitcast_fusion.19
  281.4 0.6 copy-done.22
  282.0 0.3 convolution_bitcast_fusion.23
  282.3 0.4 convolution_bitcast_fusion.3
  282.6 0.5 convolution_bitcast_fusion
  283.2 0.6 copy-done.2
  283.8 0.4 convolution_bitcast_fusion.2
  284.3 0.7 copy-done.4
  284.9 0.3 convolution_bitcast_fusion.6
  285.4 0.7 copy-done.7
  286.1 0.3 convolution_bitcast_fusion.10
  286.4 0.1 fusion.11
  286.5 0.7 copy-done.12
  287.3 0.3 convolution_bitcast_fusion.14
  287.6 0.1 fusion.10
  287.7 0.7 copy-done.18
  288.4 0.3 convolution_bitcast_fusion.18
  288.7 0.1 fusion.9
  288.8 0.7 copy-done.20
  289.6 0.3 convolution_bitcast_fusion.22
  289.9 0.1 fusion.8
  290.0 0.1 fusion.7
  290.1 0.1 fusion.6
  290.2 0.1 fusion.5
  290.6 1.6 multiply_subtract_fusion
  292.2 2.7 copy.17
  (71 shorter events, 1.8 us)
Async XLA Ops:
  6.5 271.1 %all-gather.2.cloned.1.call-start = ((), (), s32[]{:S(2)}) async-start(), calls=%async_computation | async-start | bytes 2555904 | tf_op jit(solution)/shard_map/all_gather | solution.py:64
  6.5 11.3 %copy-start.24 = (s32[1,13]{1,0:T(1,128)S(1)}, s32[1,13]{1,0:T(1,128)}, u32[]{:S(2)}) copy-start(s32[1,13]{1,0:T(1,128)} %param.3) | copy-start | bytes 160
  6.5 28.7 %copy-start = (bf16[1,13,256,256]{3,2,1,0:T(8,128)(2,1)S(1)}, bf16[1,13,256,256]{3,2,1,0:T(8,128)(2,1)}, u32[]{:S(2)}) copy-start(bf16[1,13,256,256]{3,2,1,0:T(8,128)(2,1)} %param.2) | copy-start | bytes 5111812
  9.1 26.5 %copy-start.23 = (bf16[1,13,256,128]{2,3,1,0:T(8,128)(2,1)S(1)}, bf16[1,13,256,128]{2,3,1,0:T(8,128)(2,1)}, u32[]{:S(2)}) copy-start(bf16[1,13,256,128]{2,3,1,0:T(8,128)(2,1)} %copy.44) | copy-start | bytes 2555908
  9.1 22.4 %collective-permute-start.3 = (bf16[1,13,256,128]{2,3,1,0:T(8,128)(2,1)}, bf16[1,13,256,128]{2,3,1,0:T(8,128)(2,1)S(1)}, u32[]{:S(2)}, u32[]{:S(2)}) collective-permute-start(bf16[1,13,256,128]{2,3,1,0:T(8,128)(2,1)} %copy.44), channel_id=1, source_target_pairs={{0,6},{2,8},{4,10},{6,12},{8,14},{10,16},{12,18},{14,20},{16,22},{... | collective-permute-start | bytes 2555912 | tf_op jit(solution)/shard_map/ppermute | solution.py:11
  11.6 24.1 %collective-permute-start.2 = (bf16[1,13,256,128]{2,3,1,0:T(8,128)(2,1)}, bf16[1,13,256,128]{2,3,1,0:T(8,128)(2,1)S(1)}, u32[]{:S(2)}, u32[]{:S(2)}) collective-permute-start(bf16[1,13,256,128]{2,3,1,0:T(8,128)(2,1)} %copy.44), channel_id=1, source_target_pairs={{0,8},{2,10},{4,12},{6,14},{8,16},{10,18},{12,20},{14,22},{16,24},... | collective-permute-start | bytes 2555912 | tf_op jit(solution)/shard_map/ppermute | solution.py:11
  13.1 76.6 %collective-permute-start.1 = (bf16[1,13,256,128]{2,3,1,0:T(8,128)(2,1)}, bf16[1,13,256,128]{2,3,1,0:T(8,128)(2,1)S(1)}, u32[]{:S(2)}, u32[]{:S(2)}) collective-permute-start(bf16[1,13,256,128]{2,3,1,0:T(8,128)(2,1)} %copy.44), channel_id=1, source_target_pairs={{0,10},{2,12},{4,14},{6,16},{8,18},{10,20},{12,22},{14,24},{16,26}... | collective-permute-start | bytes 2555912 | tf_op jit(solution)/shard_map/ppermute | solution.py:11
  14.8 75.3 %collective-permute-start.9 = (bf16[1,13,256,128]{2,3,1,0:T(8,128)(2,1)}, bf16[1,13,256,128]{2,3,1,0:T(8,128)(2,1)S(1)}, u32[]{:S(2)}, u32[]{:S(2)}) collective-permute-start(bf16[1,13,256,128]{2,3,1,0:T(8,128)(2,1)} %copy.44), channel_id=1, source_target_pairs={{0,24},{2,26},{4,28},{6,30},{8,0},{10,2},{12,4},{14,6},{16,8},{18,... | collective-permute-start | bytes 2555912 | tf_op jit(solution)/shard_map/ppermute | solution.py:11
  17.0 93.0 %collective-permute-start.8 = (bf16[1,13,256,128]{2,3,1,0:T(8,128)(2,1)}, bf16[1,13,256,128]{2,3,1,0:T(8,128)(2,1)S(1)}, u32[]{:S(2)}, u32[]{:S(2)}) collective-permute-start(bf16[1,13,256,128]{2,3,1,0:T(8,128)(2,1)} %copy.44), channel_id=1, source_target_pairs={{0,26},{2,28},{4,30},{6,0},{8,2},{10,4},{12,6},{14,8},{16,10},{18,... | collective-permute-start | bytes 2555912 | tf_op jit(solution)/shard_map/ppermute | solution.py:11
  31.5 23.6 %copy-start.8 = (bf16[1,13,256,128]{2,3,1,0:T(8,128)(2,1)}, bf16[1,13,256,128]{2,3,1,0:T(8,128)(2,1)S(1)}, u32[]{:S(2)}) copy-start(bf16[1,13,256,128]{2,3,1,0:T(8,128)(2,1)S(1)} %collective-permute-done.3) | copy-start | bytes 2555908
  31.5 92.2 %collective-permute-start.4 = (bf16[1,13,256,128]{2,3,1,0:T(8,128)(2,1)}, bf16[1,13,256,128]{2,3,1,0:T(8,128)(2,1)S(1)}, u32[]{:S(2)}, u32[]{:S(2)}) collective-permute-start(bf16[1,13,256,128]{2,3,1,0:T(8,128)(2,1)} %copy.44), channel_id=1, source_target_pairs={{0,4},{2,6},{4,8},{6,10},{8,12},{10,14},{12,16},{14,18},{16,20},{1... | collective-permute-start | bytes 2555912 | tf_op jit(solution)/shard_map/ppermute | solution.py:11
  35.7 54.4 %copy-start.13 = (bf16[1,13,256,128]{2,3,1,0:T(8,128)(2,1)}, bf16[1,13,256,128]{2,3,1,0:T(8,128)(2,1)S(1)}, u32[]{:S(2)}) copy-start(bf16[1,13,256,128]{2,3,1,0:T(8,128)(2,1)S(1)} %collective-permute-done.2) | copy-start | bytes 2555908
  35.7 118.9 %collective-permute-start.7 = (bf16[1,13,256,128]{2,3,1,0:T(8,128)(2,1)S(1)}, bf16[1,13,256,128]{2,3,1,0:T(8,128)(2,1)S(1)}, u32[]{:S(2)}, u32[]{:S(2)}) collective-permute-start(bf16[1,13,256,128]{2,3,1,0:T(8,128)(2,1)S(1)} %copy-done.23), channel_id=1, source_target_pairs={{0,28},{2,30},{4,0},{6,2},{8,4},{10,6},{12,8},{14,10},{16,12},{18,... | collective-permute-start | bytes 2555912 | tf_op jit(solution)/shard_map/ppermute | solution.py:11
  89.7 20.4 %copy-start.15 = (bf16[1,13,256,128]{2,3,1,0:T(8,128)(2,1)}, bf16[1,13,256,128]{2,3,1,0:T(8,128)(2,1)S(1)}, u32[]{:S(2)}) copy-start(bf16[1,13,256,128]{2,3,1,0:T(8,128)(2,1)S(1)} %collective-permute-done.1) | copy-start | bytes 2555908
  89.7 67.8 %collective-permute-start.5 = (bf16[1,13,256,128]{2,3,1,0:T(8,128)(2,1)S(1)}, bf16[1,13,256,128]{2,3,1,0:T(8,128)(2,1)S(1)}, u32[]{:S(2)}, u32[]{:S(2)}) collective-permute-start(bf16[1,13,256,128]{2,3,1,0:T(8,128)(2,1)S(1)} %copy-done.23), channel_id=1, source_target_pairs={{0,2},{2,4},{4,6},{6,8},{8,10},{10,12},{12,14},{14,16},{16,18},{18... | collective-permute-start | bytes 2555912 | tf_op jit(solution)/shard_map/ppermute | solution.py:11
  90.1 20.4 %copy-start.11 = (bf16[1,13,256,128]{2,3,1,0:T(8,128)(2,1)}, bf16[1,13,256,128]{2,3,1,0:T(8,128)(2,1)S(1)}, u32[]{:S(2)}) copy-start(bf16[1,13,256,128]{2,3,1,0:T(8,128)(2,1)S(1)} %collective-permute-done.9) | copy-start | bytes 2555908
  90.1 67.8 %collective-permute-start.6 = (bf16[1,13,256,128]{2,3,1,0:T(8,128)(2,1)S(1)}, bf16[1,13,256,128]{2,3,1,0:T(8,128)(2,1)S(1)}, u32[]{:S(2)}, u32[]{:S(2)}) collective-permute-start(bf16[1,13,256,128]{2,3,1,0:T(8,128)(2,1)S(1)} %copy-done.23), channel_id=1, source_target_pairs={{0,30},{2,0},{4,2},{6,4},{8,6},{10,8},{12,10},{14,12},{16,14},{18,... | collective-permute-start | bytes 2555912 | tf_op jit(solution)/shard_map/ppermute | solution.py:11
  110.1 0.9 copy-start.6
  110.1 62.9 %collective-permute-start = (bf16[1,13,256,128]{2,3,1,0:T(8,128)(2,1)S(1)}, bf16[1,13,256,128]{2,3,1,0:T(8,128)(2,1)S(1)}, u32[]{:S(2)}, u32[]{:S(2)}) collective-permute-start(bf16[1,13,256,128]{2,3,1,0:T(8,128)(2,1)S(1)} %copy-done.23), channel_id=1, source_target_pairs={{0,12},{2,14},{4,16},{6,18},{8,20},{10,22},{12,24},{14,26},{16,28}... | collective-permute-start | bytes 2555912 | tf_op jit(solution)/shard_map/ppermute | solution.py:11
  123.7 30.8 %copy-start.5 = (bf16[1,13,256,128]{2,3,1,0:T(8,128)(2,1)}, bf16[1,13,256,128]{2,3,1,0:T(8,128)(2,1)S(1)}, u32[]{:S(2)}) copy-start(bf16[1,13,256,128]{2,3,1,0:T(8,128)(2,1)S(1)} %collective-permute-done.4) | copy-start | bytes 2555908
  123.7 50.3 %collective-permute-start.10 = (bf16[1,13,256,128]{2,3,1,0:T(8,128)(2,1)S(1)}, bf16[1,13,256,128]{2,3,1,0:T(8,128)(2,1)S(1)}, u32[]{:S(2)}, u32[]{:S(2)}) collective-permute-start(bf16[1,13,256,128]{2,3,1,0:T(8,128)(2,1)S(1)} %copy-done.23), channel_id=1, source_target_pairs={{0,22},{2,24},{4,26},{6,28},{8,30},{10,0},{12,2},{14,4},{16,6},{18... | collective-permute-start | bytes 2555912 | tf_op jit(solution)/shard_map/ppermute | solution.py:11
  154.6 3.3 %copy-start.3 = (bf16[1,13,256,128]{2,3,1,0:T(8,128)(2,1)}, bf16[1,13,256,128]{2,3,1,0:T(8,128)(2,1)S(1)}, u32[]{:S(2)}) copy-start(bf16[1,13,256,128]{2,3,1,0:T(8,128)(2,1)S(1)} %collective-permute-done.7) | copy-start | bytes 2555908
  154.6 54.6 %collective-permute-start.11 = (bf16[1,13,256,128]{2,3,1,0:T(8,128)(2,1)S(1)}, bf16[1,13,256,128]{2,3,1,0:T(8,128)(2,1)S(1)}, u32[]{:S(2)}, u32[]{:S(2)}) collective-permute-start(bf16[1,13,256,128]{2,3,1,0:T(8,128)(2,1)S(1)} %copy-done.23), channel_id=1, source_target_pairs={{0,20},{2,22},{4,24},{6,26},{8,28},{10,30},{12,0},{14,2},{16,4},{1... | collective-permute-start | bytes 2555912 | tf_op jit(solution)/shard_map/ppermute | solution.py:11
  157.9 15.4 %copy-start.1 = (bf16[1,13,256,128]{2,3,1,0:T(8,128)(2,1)}, bf16[1,13,256,128]{2,3,1,0:T(8,128)(2,1)S(1)}, u32[]{:S(2)}) copy-start(bf16[1,13,256,128]{2,3,1,0:T(8,128)(2,1)S(1)} %collective-permute-done.6) | copy-start | bytes 2555908
  173.0 0.9 copy-start.21
  174.0 1.5 copy-start.17
  209.1 1.5 copy-start.19
  277.6 1.6 copy-start.9
  277.6 3.0 %copy-start.14 = (bf16[1,13,256,128]{2,3,1,0:T(8,128)(2,1)S(1)}, bf16[1,13,256,128]{2,3,1,0:T(8,128)(2,1)}, u32[]{:S(2)}) copy-start(bf16[1,13,256,128]{2,3,1,0:T(8,128)(2,1)} %copy-done.13) | copy-start | bytes 2555908
  279.2 1.5 copy-start.10
  279.3 1.8 copy-start.16
  280.8 1.2 copy-start.22
  282.6 1.2 copy-start.2
  283.8 1.2 copy-start.4
  284.9 1.2 copy-start.7
  286.1 1.2 copy-start.12
  287.3 1.2 copy-start.18
  288.4 1.2 copy-start.20
Sparse Core Ops, SparseCore 0:
  212.4 65.1 all-gather.1
where the time goes:
time: 302 us
  waiting for transfers between devices  175 us (58%)
  starting transfers between devices  84.1 us (28%)
  between operations  13.8 us (5%)
  matrix products  13.3 us (4%)
  local copies, waits for them, and re-layouts  10.7 us (4%)
  other arithmetic  5.25 us (2%)
    ppermute x12, waiting for transfers between devices, shifted(): lax.ppermute(array, axis, [(i, (i + by) % peers) for i in range(peers)])  109 us
    ppermute x12, starting transfers between devices, shifted(): lax.ppermute(array, axis, [(i, (i + by) % peers) for i in range(peers)])  84.1 us
    all_gather x1, waiting for transfers between devices, body(): square_rows = lax.all_gather(square_half, 'layer', axis=3, tiled=True)  65.3 us
    dot_general x26, matrix products, band_product(): jnp.einsum('rab,rdbc->rdac', factor[:, half + offset], source, preferred_...  13.3 us
    unnamed x51, local copies, waits for them, and re-layouts  6.71 us
  transfers between devices with their start and end apart: 13, of which 6 were waited for; matrix products, arithmetic and copies ran while one was open for 2% of the time, Pallas kernels for 0%

commit v1 on v0

v1 whole, which is shorter than its diff:
```python
import jax
import jax.numpy as jnp
from jax import lax
from jax.experimental import pallas as pl
from jax.experimental.pallas import tpu as pltpu
from jax.sharding import PartitionSpec as P

HALF = 6
BAND = 2 * HALF + 1
FORWARD = ((0, 1, 2, 3, 4, 5, -3, -5), (0, 1, 2, 3), (0, 1))
BACKWARD = ((0, 1, 2, 3, 4, -4, -5, -6), (0, 1, 2, -6), (0, 0))
SIZES = tuple(len(part) for part in FORWARD)
FETCHED = sum(SIZES)
LANES = 128
FRAME = range(-HALF, HALF + 1)


def places():
    held = {}
    for offset in FRAME:
        held[0, offset] = offset + HALF
    for offset in FRAME:
        held.setdefault((1, 1 + offset), BAND + offset + HALF)
    slot = 2 * BAND
    for other in (False, True):
        for parts, way in ((FORWARD, 1), (BACKWARD, -1)):
            for step, part in enumerate(parts):
                for offset in part:
                    row = way * 2 * (step + 1)
                    column = row + way * offset
                    if other:
                        row, column = 1 - row, 1 - column
                    if (row, column) not in held and (column, row) not in held:
                        held[row, column] = slot
                    slot += 1
    return held


HELD = places()


def terms(column):
    plain = []
    turned = []
    for row in FRAME:
        if abs(row - column) <= HALF:
            if (row, column) in HELD:
                plain.append((row, HELD[row, column]))
            else:
                turned.append((row, HELD[column, row]))
    return plain, turned


def column_product(left, plain_block, turned_block, column):
    plain, turned = terms(column)
    total = None
    if plain:
        total = jnp.dot(
            jnp.concatenate([left(row) for row, slot in plain], axis=1),
            jnp.concatenate([plain_block(slot) for row, slot in plain], axis=0),
            preferred_element_type=jnp.float32,
        )
    if turned:
        other = lax.dot_general(
            jnp.concatenate([left(row) for row, slot in turned], axis=1),
            jnp.concatenate([turned_block(slot) for row, slot in turned], axis=1),
            (((1,), (1,)), ((), ())),
            preferred_element_type=jnp.float32,
        )
        total = other if total is None else total + other
    return total


def pack_kernel(index, density, first, second, third, sems):
    copies = []
    place = 0
    for out in (first, second, third):
        for item in range(out.shape[1]):
            copies.append(
                pltpu.make_async_copy(
                    density.at[0, index[place]], out.at[0, item], sems.at[place]
                )
            )
            place += 1
    for copy in copies:
        copy.start()
    for copy in copies:
        copy.wait()


def pack(density, index):
    block = density.shape[2]
    return pl.pallas_call(
        pack_kernel,
        out_shape=[
            jax.ShapeDtypeStruct((1, size, block, block), density.dtype) for size in SIZES
        ],
        in_specs=[
            pl.BlockSpec(memory_space=pltpu.SMEM),
            pl.BlockSpec(memory_space=pl.ANY),
        ],
        out_specs=[pl.BlockSpec(memory_space=pl.ANY)] * len(SIZES),
        scratch_shapes=[pltpu.SemaphoreType.DMA((FETCHED,))],
        name="pack",
    )(index, density)


def purify_kernel(where, keep, own, beside, *refs):
    sources, (out, slots, rounded, square, result, in_sems, out_sems) = refs[:12], refs[12:]
    way = where[0]
    kind = where[1]
    part = where[2]
    copies = []

    def bring(source, target):
        copies.append(pltpu.make_async_copy(source, target, in_sems.at[len(copies)]))

    for offset in FRAME:
        bring(own.at[0, HALF + way * offset], slots.at[offset + HALF])
        bring(beside.at[0, HALF + way * offset], slots.at[BAND + offset + HALF])
    for group in range(2):
        base = 2 * BAND + group * 2 * FETCHED
        start = 0
        for step, size in enumerate(SIZES):
            near = sources[group * 6 + step]
            far = sources[group * 6 + 3 + step]
            bring(near.at[0], slots.at[pl.ds(base + kind * FETCHED + start, size)])
            bring(far.at[0], slots.at[pl.ds(base + (1 - kind) * FETCHED + start, size)])
            start += size
    for copy in copies:
        copy.start()
    for copy in copies:
        copy.wait()

    lanes = pl.ds(pl.multiple_of(part * LANES, LANES), LANES)
    for column in FRAME:
        total = column_product(
            lambda row: slots[row + HALF], lambda slot: slots[slot], lambda slot: slots[slot], column
        )
        total = total * keep[0, HALF + way * column].astype(jnp.float32)
        rounded[column + HALF] = total.astype(jnp.bfloat16)
        mine = total[:, :LANES]
        for piece in range(1, total.shape[1] // LANES):
            mine = jnp.where(part == piece, total[:, piece * LANES : (piece + 1) * LANES], mine)
        square[column + HALF] = mine
    written = []
    for column in FRAME:
        total = column_product(
            lambda row: rounded[row + HALF],
            lambda slot: slots[slot, :, lanes],
            lambda slot: slots[slot, lanes, :],
            column,
        )
        total = total * keep[0, HALF + way * column].astype(jnp.float32)
        result[column + HALF] = 3.0 * square[column + HALF] - 2.0 * total
        copy = pltpu.make_async_copy(
            result.at[column + HALF], out.at[0, HALF + way * column], out_sems.at[column + HALF]
        )
        copy.start()
        written.append(copy)
    for copy in written:
        copy.wait()


def purify(where, keep, own, beside, fetched):
    block = own.shape[2]
    copies = 2 * BAND + len(fetched)
    return pl.pallas_call(
        purify_kernel,
        out_shape=jax.ShapeDtypeStruct((1, BAND, block, LANES), jnp.float32),
        in_specs=[pl.BlockSpec(memory_space=pltpu.SMEM)] * 2
        + [pl.BlockSpec(memory_space=pl.ANY)] * (2 + len(fetched)),
        out_specs=pl.BlockSpec(memory_space=pl.ANY),
        scratch_shapes=[
            pltpu.VMEM((2 * BAND + 4 * FETCHED, block, block), jnp.bfloat16),
            pltpu.VMEM((BAND, block, block), jnp.bfloat16),
            pltpu.VMEM((BAND, block, LANES), jnp.float32),
            pltpu.VMEM((BAND, block, LANES), jnp.float32),
            pltpu.SemaphoreType.DMA((copies,)),
            pltpu.SemaphoreType.DMA((BAND,)),
        ],
        compiler_params=pltpu.CompilerParams(vmem_limit_bytes=48 * 2**20),
        cost_estimate=pl.CostEstimate(
            flops=6 * 127 * block**3, bytes_accessed=14 * 2**20, transcendentals=0
        ),
        name="purify",
    )(where, keep, own, beside, *fetched)


def body(density, pattern):
    axes = ("row", "col", "layer")
    rows = lax.axis_size(("row", "col"))
    layers = lax.axis_size("layer")
    width = density.shape[2] // layers
    row = lax.axis_index(("row", "col"))
    layer = lax.axis_index("layer")
    way = 1 - 2 * (row % 2)
    kind = layer % 2

    def fetch(array, step):
        pairs = []
        for source in range(rows):
            for plane in range(layers):
                shift = 2 * step * (1 - 2 * (source % 2)) * (1 - 2 * (plane % 2))
                pairs.append((source * layers + plane, (source - shift) % rows * layers + plane))
        return lax.ppermute(array, axes, pairs)

    def swap_layers(array):
        return lax.ppermute(array, "layer", [(plane, plane ^ 1) for plane in range(layers)])

    def swap_cores(array):
        peers = lax.axis_size("col")
        return lax.ppermute(array, "col", [(peer, peer ^ 1) for peer in range(peers)])

    lists = jnp.where(
        kind == 0,
        jnp.array([offset for part in FORWARD for offset in part], jnp.int32),
        -jnp.array([offset for part in BACKWARD for offset in part], jnp.int32),
    )
    parts = pack(density, HALF + way * lists)
    beside = swap_cores(density)
    near = [fetch(part, step + 1) for step, part in enumerate(parts)]
    far = [swap_layers(part) for part in near]
    fetched = near + far + [swap_cores(part) for part in near + far]
    where = jnp.stack([way, kind, layer * width // LANES]).astype(jnp.int32)
    out = purify(where, pattern, density, beside, fetched)
    if width < LANES:
        out = lax.dynamic_slice_in_dim(out, layer * width % LANES, width, 3)
    return out


def solution(mesh):
    return jax.shard_map(
        body,
        mesh=mesh,
        in_specs=(P(("row", "col"), None, None, None), P(("row", "col"), None)),
        out_specs=P(("row", "col"), None, None, "layer"),
        check_vma=False,
    )
```

time: 302 us -> 150 us (0.50)
  waiting for transfers between devices: 175 us -> 55.9 us
  Pallas kernels: 0 us -> 71.1 us
  starting transfers between devices: 84.1 us -> 14.5 us
  between operations: 13.8 us -> 0.05 us
  matrix products: 13.3 us -> 0 us
  local copies, waits for them, and re-layouts: 10.7 us -> 4.96 us
  other arithmetic: 5.25 us -> 1.26 us
    pallas_call x0 -> x2, Pallas kernels: none -> 71.1 us  [the longest x1 57.5 us: pack(): pl.pallas_call(pack_kernel, out_shape=[jax.ShapeDtypeStruct((1, size, blo...]
    ppermute x12 -> x13, starting transfers between devices: 84.1 us -> 14.5 us  [the longest x3 10.9 us: fetch(): return lax.ppermute(array, axes, pairs)]
    all_gather x1 -> x0, waiting for transfers between devices: 65.3 us -> none  [body(): square_rows = lax.all_gather(square_half, 'layer', axis=3, tiled=True)]
    ppermute x12 -> x13, waiting for transfers between devices: 109 us -> 55.9 us  [the longest x3 38.8 us: fetch(): return lax.ppermute(array, axes, pairs)]
    dot_general x26 -> x0, matrix products: 13.3 us -> none  [band_product(): jnp.einsum('rab,rdbc->rdac', factor[:, half + offset], source, preferred_...]
    unnamed x51 -> x14, local copies, waits for them, and re-layouts: 6.71 us -> 4.96 us
  transfers between devices with their start and end apart: 13 -> 13, of which waited for: 6 -> 6; matrix products, arithmetic and copies ran while one was open for 2% -> 0% of each run, Pallas kernels for 0% -> 0%
where the time goes in v1:
time: 150 us; the launch traced here: 148 us
  Pallas kernels  71.1 us (47%)
  waiting for transfers between devices  55.9 us (37%)
  starting transfers between devices  14.5 us (10%)
  local copies, waits for them, and re-layouts  4.96 us (3%)
    pallas_call x1, Pallas kernels, pack(): pl.pallas_call(pack_kernel, out_shape=[jax.ShapeDtypeStruct((1, size, blo...  57.5 us
    ppermute x3, waiting for transfers between devices, fetch(): return lax.ppermute(array, axes, pairs)  38.8 us
    ppermute x3, waiting for transfers between devices, swap_layers(): lax.ppermute(array, 'layer', [(plane, plane ^ 1) for plane in range(layer...  14.3 us
    pallas_call x1, Pallas kernels, purify(): pl.pallas_call(purify_kernel, out_shape=jax.ShapeDtypeStruct((1, BAND, bl...  13.6 us
    ppermute x3, starting transfers between devices, fetch(): return lax.ppermute(array, axes, pairs)  10.9 us
    unnamed x14, local copies, waits for them, and re-layouts  4.96 us
  transfers between devices with their start and end apart: 13, of which 6 were waited for; matrix products, arithmetic and copies ran while one was open for 0% of the time, Pallas kernels for 0%

profile of v1, /device:TPU:0, one launch (start us, length us, event | category | flops | bytes accessed | tf_op | source)
XLA Modules:
  0.0 147.8 jit_solution(8326132518040935280)
XLA Ops:
  0.0 0.0 copy-start.6
  0.0 1.2 fusion.1.index
  1.2 57.5 %pack.1 = (bf16[1,8,256,256]{3,2,1,0:T(8,128)(2,1)}, bf16[1,4,256,256]{3,2,1,0:T(8,128)(2,1)}, bf16[1,2,256,256]{3,2,1,0:T(8,128)(2,1)}) custom-call(s32[14]{0:T(128)} %fusion.1.index, bf16[1,13,256,256]{3,2,1,0:T(8,128)(2,1)} %own.1), custom_call_target="tpu_custom_call" | custom-call | tf_op jit(solution)/shard_map/pack/pallas_call | solution.py:93
  58.7 6.1 %collective-permute-start.1 = (bf16[1,8,256,256]{3,2,1,0:T(8,128)(2,1)}, bf16[1,8,256,256]{3,2,1,0:T(8,128)(2,1)S(1)}, u32[]{:S(2)}, u32[]{:S(2)}) collective-permute-start(bf16[1,8,256,256]{3,2,1,0:T(8,128)(2,1)} %get-tuple-element.8), channel_id=1, source_target_pairs={{0,28},{1,5},{2,6},{3,31},{4,0},{5,9},{6,10},{7,3},{8,4},{9,13},{1... | collective-permute-start | bytes 3145736 | tf_op jit(solution)/shard_map/ppermute | solution.py:206
  64.7 21.2 %collective-permute-done.1.refs_0_ = bf16[1,8,256,256]{3,2,1,0:T(8,128)(2,1)S(1)} collective-permute-done((bf16[1,8,256,256]{3,2,1,0:T(8,128)(2,1)}, bf16[1,8,256,256]{3,2,1,0:T(8,128)(2,1)S(1)}, u32[]{:S(2)}, u32[]{:S(2)}) %collective-permute-start.1) | collective-permute-done | bytes 1048608 | tf_op jit(solution)/shard_map/ppermute | solution.py:206
  85.9 0.9 collective-permute-start.4
  86.8 0.0 collective-permute-start
  86.8 3.8 %collective-permute-start.2 = (bf16[1,4,256,256]{3,2,1,0:T(8,128)(2,1)}, bf16[1,4,256,256]{3,2,1,0:T(8,128)(2,1)S(1)}, u32[]{:S(2)}, u32[]{:S(2)}) collective-permute-start(bf16[1,4,256,256]{3,2,1,0:T(8,128)(2,1)} %get-tuple-element.9), channel_id=1, source_target_pairs={{0,24},{1,9},{2,10},{3,27},{4,28},{5,13},{6,14},{7,31},{8,0},{9,17... | collective-permute-start | bytes 1572872 | tf_op jit(solution)/shard_map/ppermute | solution.py:206
  90.7 1.0 collective-permute-start.3
  91.7 17.6 %collective-permute-done.3.refs_2_ = bf16[1,2,256,256]{3,2,1,0:T(8,128)(2,1)S(1)} collective-permute-done((bf16[1,2,256,256]{3,2,1,0:T(8,128)(2,1)}, bf16[1,2,256,256]{3,2,1,0:T(8,128)(2,1)S(1)}, u32[]{:S(2)}, u32[]{:S(2)}) %collective-permute-start.3) | collective-permute-done | bytes 262176 | tf_op jit(solution)/shard_map/ppermute | solution.py:206
  109.3 0.0 collective-permute-start.9
  109.3 0.0 collective-permute-start.6
  109.3 0.0 collective-permute-done.2.refs_1_
  109.3 2.0 %collective-permute-start.5 = (bf16[1,4,256,256]{3,2,1,0:T(8,128)(2,1)S(1)}, bf16[1,4,256,256]{3,2,1,0:T(8,128)(2,1)S(1)}, u32[]{:S(2)}, u32[]{:S(2)}) collective-permute-start(bf16[1,4,256,256]{3,2,1,0:T(8,128)(2,1)S(1)} %collective-permute-done.2.refs_1_), channel_id=1, source_target_pairs={{0,1},{1,0},{2,3},{3,2},{4,5},{5,4},{6,7},{7,6},{8,9},{9,8},{10,11... | collective-permute-start | bytes 1572872 | tf_op jit(solution)/shard_map/ppermute | solution.py:209
  111.3 0.0 collective-permute-done.9.refs_8_
  111.3 0.0 copy-start
  111.3 0.7 copy-done
  112.0 0.0 collective-permute-start.7
  112.0 0.0 collective-permute-done.4.refs_3_
  112.0 0.5 collective-permute-start.10
  112.5 5.9 %collective-permute-done.6.refs_5_ = bf16[1,2,256,256]{3,2,1,0:T(8,128)(2,1)S(1)} collective-permute-done((bf16[1,2,256,256]{3,2,1,0:T(8,128)(2,1)S(1)}, bf16[1,2,256,256]{3,2,1,0:T(8,128)(2,1)S(1)}, u32[]{:S(2)}, u32[]{:S(2)}) %collective-permute-start.6) | collective-permute-done | bytes 262176 | tf_op jit(solution)/shard_map/ppermute | solution.py:209
  118.4 0.0 collective-permute-start.12
  118.4 0.0 copy-start.2
  118.4 0.7 copy-done.2
  119.1 0.8 collective-permute-done.12.refs_11_
  119.9 0.0 copy-start.4
  119.9 0.7 copy-done.4
  120.6 0.1 collective-permute-start.8
  120.8 8.5 %collective-permute-done.5.refs_4_ = bf16[1,4,256,256]{3,2,1,0:T(8,128)(2,1)S(1)} collective-permute-done((bf16[1,4,256,256]{3,2,1,0:T(8,128)(2,1)S(1)}, bf16[1,4,256,256]{3,2,1,0:T(8,128)(2,1)S(1)}, u32[]{:S(2)}, u32[]{:S(2)}) %collective-permute-start.5) | collective-permute-done | bytes 524320 | tf_op jit(solution)/shard_map/ppermute | solution.py:209
  129.2 0.0 collective-permute-start.11
  129.2 0.1 pad_add_fusion.where
  129.3 0.0 collective-permute-done.8.refs_7_
  129.3 2.0 %collective-permute-done.11.refs_10_ = bf16[1,4,256,256]{3,2,1,0:T(8,128)(2,1)} collective-permute-done((bf16[1,4,256,256]{3,2,1,0:T(8,128)(2,1)S(1)}, bf16[1,4,256,256]{3,2,1,0:T(8,128)(2,1)}, u32[]{:S(2)}, u32[]{:S(2)}) %collective-permute-start.11) | collective-permute-done | bytes 524320 | tf_op jit(solution)/shard_map/ppermute | solution.py:213
  131.3 0.0 collective-permute-done.beside
  131.3 0.0 collective-permute-done.7.refs_6_
  131.3 0.0 collective-permute-done.10.refs_9_
  131.3 0.0 copy-done.6
  131.3 0.0 copy-start.1
  131.3 0.9 copy-done.1
  132.2 0.0 copy-start.3
  132.2 0.9 copy-done.3
  133.2 0.0 copy-start.5
  133.2 0.9 copy-done.5
  134.1 13.6 %purify.1 = f32[1,13,256,128]{3,2,1,0:T(8,128)} custom-call(s32[3]{0:T(128)S(1)} %pad_add_fusion.where, s32[1,13]{1,0:T(1,128)S(1)} %copy-done.6, bf16[1,13,256,256]{3,2,1,0:T(8,128)(2,1)} %own.1, bf16[1,13,256,256]{3,2,1,0:T(8,128)(2,1)} %collective-permute-done.beside, bf16[1,8,256,256]{3,2,1,0:T(8,128)(2,1)S(1)} %collective-permute-done.1.refs_0_, ...), custom_call_target="tpu_custom_call" | custom-call | flops 12784238592 | bytes 14680064 | tf_op jit(solution)/shard_map/purify/pallas_call | solution.py:168
Async XLA Ops:
  0.0 131.3 %copy-start.6 = (s32[1,13]{1,0:T(1,128)S(1)}, s32[1,13]{1,0:T(1,128)}, u32[]{:S(2)}) copy-start(s32[1,13]{1,0:T(1,128)} %keep.1) | copy-start | bytes 160
  58.7 27.2 %collective-permute-start.1 = (bf16[1,8,256,256]{3,2,1,0:T(8,128)(2,1)}, bf16[1,8,256,256]{3,2,1,0:T(8,128)(2,1)S(1)}, u32[]{:S(2)}, u32[]{:S(2)}) collective-permute-start(bf16[1,8,256,256]{3,2,1,0:T(8,128)(2,1)} %get-tuple-element.8), channel_id=1, source_target_pairs={{0,28},{1,5},{2,6},{3,31},{4,0},{5,9},{6,10},{7,3},{8,4},{9,13},{1... | collective-permute-start | bytes 3145736 | tf_op jit(solution)/shard_map/ppermute | solution.py:206
  85.9 26.1 %collective-permute-start.4 = (bf16[1,8,256,256]{3,2,1,0:T(8,128)(2,1)S(1)}, bf16[1,8,256,256]{3,2,1,0:T(8,128)(2,1)S(1)}, u32[]{:S(2)}, u32[]{:S(2)}) collective-permute-start(bf16[1,8,256,256]{3,2,1,0:T(8,128)(2,1)S(1)} %collective-permute-done.1.refs_0_), channel_id=1, source_target_pairs={{0,1},{1,0},{2,3},{3,2},{4,5},{5,4},{6,7},{7,6},{8,9},{9,8},{10,11... | collective-permute-start | bytes 3145736 | tf_op jit(solution)/shard_map/ppermute | solution.py:209
  86.8 44.5 %collective-permute-start = (bf16[1,13,256,256]{3,2,1,0:T(8,128)(2,1)}, bf16[1,13,256,256]{3,2,1,0:T(8,128)(2,1)}, u32[]{:S(2)}, u32[]{:S(2)}) collective-permute-start(bf16[1,13,256,256]{3,2,1,0:T(8,128)(2,1)} %own.1), channel_id=1, source_target_pairs={{0,2},{2,0},{4,6},{6,4},{1,3},{3,1},{5,7},{7,5},{8,10},{10,8},{12,... | collective-permute-start | bytes 5111816 | tf_op jit(solution)/shard_map/ppermute | solution.py:213
  86.8 22.4 %collective-permute-start.2 = (bf16[1,4,256,256]{3,2,1,0:T(8,128)(2,1)}, bf16[1,4,256,256]{3,2,1,0:T(8,128)(2,1)S(1)}, u32[]{:S(2)}, u32[]{:S(2)}) collective-permute-start(bf16[1,4,256,256]{3,2,1,0:T(8,128)(2,1)} %get-tuple-element.9), channel_id=1, source_target_pairs={{0,24},{1,9},{2,10},{3,27},{4,28},{5,13},{6,14},{7,31},{8,0},{9,17... | collective-permute-start | bytes 1572872 | tf_op jit(solution)/shard_map/ppermute | solution.py:206
  90.7 18.6 %collective-permute-start.3 = (bf16[1,2,256,256]{3,2,1,0:T(8,128)(2,1)}, bf16[1,2,256,256]{3,2,1,0:T(8,128)(2,1)S(1)}, u32[]{:S(2)}, u32[]{:S(2)}) collective-permute-start(bf16[1,2,256,256]{3,2,1,0:T(8,128)(2,1)} %get-tuple-element.10), channel_id=1, source_target_pairs={{0,20},{1,13},{2,14},{3,23},{4,24},{5,17},{6,18},{7,27},{8,28},{9,... | collective-permute-start | bytes 786440 | tf_op jit(solution)/shard_map/ppermute | solution.py:206
  109.3 2.0 %collective-permute-start.9 = (bf16[1,2,256,256]{3,2,1,0:T(8,128)(2,1)S(1)}, bf16[1,2,256,256]{3,2,1,0:T(8,128)(2,1)S(1)}, u32[]{:S(2)}, u32[]{:S(2)}) collective-permute-start(bf16[1,2,256,256]{3,2,1,0:T(8,128)(2,1)S(1)} %collective-permute-done.3.refs_2_), channel_id=1, source_target_pairs={{0,2},{2,0},{4,6},{6,4},{1,3},{3,1},{5,7},{7,5},{8,10},{10,8},{12,... | collective-permute-start | bytes 786440 | tf_op jit(solution)/shard_map/ppermute | solution.py:213
  109.3 9.1 %collective-permute-start.6 = (bf16[1,2,256,256]{3,2,1,0:T(8,128)(2,1)S(1)}, bf16[1,2,256,256]{3,2,1,0:T(8,128)(2,1)S(1)}, u32[]{:S(2)}, u32[]{:S(2)}) collective-permute-start(bf16[1,2,256,256]{3,2,1,0:T(8,128)(2,1)S(1)} %collective-permute-done.3.refs_2_), channel_id=1, source_target_pairs={{0,1},{1,0},{2,3},{3,2},{4,5},{5,4},{6,7},{7,6},{8,9},{9,8},{10,11... | collective-permute-start | bytes 786440 | tf_op jit(solution)/shard_map/ppermute | solution.py:209
  109.3 20.0 %collective-permute-start.5 = (bf16[1,4,256,256]{3,2,1,0:T(8,128)(2,1)S(1)}, bf16[1,4,256,256]{3,2,1,0:T(8,128)(2,1)S(1)}, u32[]{:S(2)}, u32[]{:S(2)}) collective-permute-start(bf16[1,4,256,256]{3,2,1,0:T(8,128)(2,1)S(1)} %collective-permute-done.2.refs_1_), channel_id=1, source_target_pairs={{0,1},{1,0},{2,3},{3,2},{4,5},{5,4},{6,7},{7,6},{8,9},{9,8},{10,11... | collective-permute-start | bytes 1572872 | tf_op jit(solution)/shard_map/ppermute | solution.py:209
  111.3 0.7 copy-start
  112.0 19.3 %collective-permute-start.7 = (bf16[1,8,256,256]{3,2,1,0:T(8,128)(2,1)S(1)}, bf16[1,8,256,256]{3,2,1,0:T(8,128)(2,1)}, u32[]{:S(2)}, u32[]{:S(2)}) collective-permute-start(bf16[1,8,256,256]{3,2,1,0:T(8,128)(2,1)S(1)} %collective-permute-done.1.refs_0_), channel_id=1, source_target_pairs={{0,2},{2,0},{4,6},{6,4},{1,3},{3,1},{5,7},{7,5},{8,10},{10,8},{12,... | collective-permute-start | bytes 3145736 | tf_op jit(solution)/shard_map/ppermute | solution.py:213
  112.0 19.3 %collective-permute-start.10 = (bf16[1,8,256,256]{3,2,1,0:T(8,128)(2,1)S(1)}, bf16[1,8,256,256]{3,2,1,0:T(8,128)(2,1)}, u32[]{:S(2)}, u32[]{:S(2)}) collective-permute-start(bf16[1,8,256,256]{3,2,1,0:T(8,128)(2,1)S(1)} %collective-permute-done.4.refs_3_), channel_id=1, source_target_pairs={{0,2},{2,0},{4,6},{6,4},{1,3},{3,1},{5,7},{7,5},{8,10},{10,8},{12,... | collective-permute-start | bytes 3145736 | tf_op jit(solution)/shard_map/ppermute | solution.py:213
  118.4 1.5 %collective-permute-start.12 = (bf16[1,2,256,256]{3,2,1,0:T(8,128)(2,1)S(1)}, bf16[1,2,256,256]{3,2,1,0:T(8,128)(2,1)S(1)}, u32[]{:S(2)}, u32[]{:S(2)}) collective-permute-start(bf16[1,2,256,256]{3,2,1,0:T(8,128)(2,1)S(1)} %collective-permute-done.6.refs_5_), channel_id=1, source_target_pairs={{0,2},{2,0},{4,6},{6,4},{1,3},{3,1},{5,7},{7,5},{8,10},{10,8},{12,... | collective-permute-start | bytes 786440 | tf_op jit(solution)/shard_map/ppermute | solution.py:213
  118.4 0.7 copy-start.2
  119.9 0.7 copy-start.4
  120.6 8.7 %collective-permute-start.8 = (bf16[1,4,256,256]{3,2,1,0:T(8,128)(2,1)S(1)}, bf16[1,4,256,256]{3,2,1,0:T(8,128)(2,1)}, u32[]{:S(2)}, u32[]{:S(2)}) collective-permute-start(bf16[1,4,256,256]{3,2,1,0:T(8,128)(2,1)S(1)} %collective-permute-done.2.refs_1_), channel_id=1, source_target_pairs={{0,2},{2,0},{4,6},{6,4},{1,3},{3,1},{5,7},{7,5},{8,10},{10,8},{12,... | collective-permute-start | bytes 1572872 | tf_op jit(solution)/shard_map/ppermute | solution.py:213
  129.2 2.0 %collective-permute-start.11 = (bf16[1,4,256,256]{3,2,1,0:T(8,128)(2,1)S(1)}, bf16[1,4,256,256]{3,2,1,0:T(8,128)(2,1)}, u32[]{:S(2)}, u32[]{:S(2)}) collective-permute-start(bf16[1,4,256,256]{3,2,1,0:T(8,128)(2,1)S(1)} %collective-permute-done.5.refs_4_), channel_id=1, source_target_pairs={{0,2},{2,0},{4,6},{6,4},{1,3},{3,1},{5,7},{7,5},{8,10},{10,8},{12,... | collective-permute-start | bytes 1572872 | tf_op jit(solution)/shard_map/ppermute | solution.py:213
  131.3 1.0 copy-start.1
  132.2 0.9 copy-start.3
  133.2 0.9 copy-start.5

commit v2 on v1

--- a/solution.py
+++ b/solution.py
@@ -99,7 +99,7 @@
             pl.BlockSpec(memory_space=pltpu.SMEM),
             pl.BlockSpec(memory_space=pl.ANY),
         ],
-        out_specs=[pl.BlockSpec(memory_space=pl.ANY)] * len(SIZES),
+        out_specs=[pl.BlockSpec(memory_space=pltpu.VMEM)] * len(SIZES),
         scratch_shapes=[pltpu.SemaphoreType.DMA((FETCHED,))],
         name="pack",
     )(index, density)

time: 150 us -> 95.7 us (0.64)
  Pallas kernels: 71.1 us -> 17.2 us
    pallas_call x1, Pallas kernels: 57.5 us -> 3.52 us  [pack(): pl.pallas_call(pack_kernel, out_shape=[jax.ShapeDtypeStruct((1, size, blo...]
where the time goes in v2:
time: 95.7 us; the launch traced here: 93.8 us
  waiting for transfers between devices  55.9 us (58%)
  Pallas kernels  17.2 us (18%)
  starting transfers between devices  14.5 us (15%)
  local copies, waits for them, and re-layouts  4.96 us (5%)
  other arithmetic  1.26 us (1%)
    ppermute x3, waiting for transfers between devices, fetch(): return lax.ppermute(array, axes, pairs)  38.8 us
    ppermute x3, waiting for transfers between devices, swap_layers(): lax.ppermute(array, 'layer', [(plane, plane ^ 1) for plane in range(layer...  14.3 us
    pallas_call x1, Pallas kernels, purify(): pl.pallas_call(purify_kernel, out_shape=jax.ShapeDtypeStruct((1, BAND, bl...  13.6 us
    ppermute x3, starting transfers between devices, fetch(): return lax.ppermute(array, axes, pairs)  10.9 us
    unnamed x14, local copies, waits for them, and re-layouts  4.96 us
    pallas_call x1, Pallas kernels, pack(): pl.pallas_call(pack_kernel, out_shape=[jax.ShapeDtypeStruct((1, size, blo...  3.52 us
    ppermute x3, starting transfers between devices, swap_layers(): lax.ppermute(array, 'layer', [(plane, plane ^ 1) for plane in range(layer...  2.92 us
    ppermute x7, waiting for transfers between devices, swap_cores(): lax.ppermute(array, 'col', [(peer, peer ^ 1) for peer in range(peers)])  2.8 us
  transfers between devices with their start and end apart: 13, of which 6 were waited for; matrix products, arithmetic and copies ran while one was open for 0% of the time, Pallas kernels for 0%

profile of v2, /device:TPU:0, one launch (start us, length us, event | category | flops | bytes accessed | tf_op | source)
XLA Modules:
  0.0 93.8 jit_solution(1369027658043232104)
XLA Ops:
  0.0 0.0 copy-start.6
  0.0 1.2 %fusion.1.index = s32[14]{0:T(128)} fusion(s32[14]{0:T(128)} %constant.53.clone, s32[14]{0:T(128)} %constant.57, pred[]{:T(512)S(6)} %eq.6, s32[]{:T(128)} %sub.7), kind=kLoop, calls=%fused_computation.2 | loop fusion | flops 42 | bytes 173 | tf_op jit(solution)/shard_map/add | solution.py:220
  1.2 3.5 %pack.1 = (bf16[1,8,256,256]{3,2,1,0:T(8,128)(2,1)}, bf16[1,4,256,256]{3,2,1,0:T(8,128)(2,1)}, bf16[1,2,256,256]{3,2,1,0:T(8,128)(2,1)}) custom-call(s32[14]{0:T(128)} %fusion.1.index, bf16[1,13,256,256]{3,2,1,0:T(8,128)(2,1)} %own.1), custom_call_target="tpu_custom_call" | custom-call | tf_op jit(solution)/shard_map/pack/pallas_call | solution.py:93
  4.7 6.1 %collective-permute-start.1 = (bf16[1,8,256,256]{3,2,1,0:T(8,128)(2,1)}, bf16[1,8,256,256]{3,2,1,0:T(8,128)(2,1)S(1)}, u32[]{:S(2)}, u32[]{:S(2)}) collective-permute-start(bf16[1,8,256,256]{3,2,1,0:T(8,128)(2,1)} %get-tuple-element.8), channel_id=1, source_target_pairs={{0,28},{1,5},{2,6},{3,31},{4,0},{5,9},{6,10},{7,3},{8,4},{9,13},{1... | collective-permute-start | bytes 3145736 | tf_op jit(solution)/shard_map/ppermute | solution.py:206
  10.8 21.2 %collective-permute-done.1.refs_0_ = bf16[1,8,256,256]{3,2,1,0:T(8,128)(2,1)S(1)} collective-permute-done((bf16[1,8,256,256]{3,2,1,0:T(8,128)(2,1)}, bf16[1,8,256,256]{3,2,1,0:T(8,128)(2,1)S(1)}, u32[]{:S(2)}, u32[]{:S(2)}) %collective-permute-start.1) | collective-permute-done | bytes 1048608 | tf_op jit(solution)/shard_map/ppermute | solution.py:206
  32.0 0.9 collective-permute-start.4
  32.9 0.0 collective-permute-start
  32.9 3.9 %collective-permute-start.2 = (bf16[1,4,256,256]{3,2,1,0:T(8,128)(2,1)}, bf16[1,4,256,256]{3,2,1,0:T(8,128)(2,1)S(1)}, u32[]{:S(2)}, u32[]{:S(2)}) collective-permute-start(bf16[1,4,256,256]{3,2,1,0:T(8,128)(2,1)} %get-tuple-element.9), channel_id=1, source_target_pairs={{0,24},{1,9},{2,10},{3,27},{4,28},{5,13},{6,14},{7,31},{8,0},{9,17... | collective-permute-start | bytes 1572872 | tf_op jit(solution)/shard_map/ppermute | solution.py:206
  36.7 1.0 %collective-permute-start.3 = (bf16[1,2,256,256]{3,2,1,0:T(8,128)(2,1)}, bf16[1,2,256,256]{3,2,1,0:T(8,128)(2,1)S(1)}, u32[]{:S(2)}, u32[]{:S(2)}) collective-permute-start(bf16[1,2,256,256]{3,2,1,0:T(8,128)(2,1)} %get-tuple-element.10), channel_id=1, source_target_pairs={{0,20},{1,13},{2,14},{3,23},{4,24},{5,17},{6,18},{7,27},{8,28},{9,... | collective-permute-start | bytes 786440 | tf_op jit(solution)/shard_map/ppermute | solution.py:206
  37.7 17.6 %collective-permute-done.3.refs_2_ = bf16[1,2,256,256]{3,2,1,0:T(8,128)(2,1)S(1)} collective-permute-done((bf16[1,2,256,256]{3,2,1,0:T(8,128)(2,1)}, bf16[1,2,256,256]{3,2,1,0:T(8,128)(2,1)S(1)}, u32[]{:S(2)}, u32[]{:S(2)}) %collective-permute-start.3) | collective-permute-done | bytes 262176 | tf_op jit(solution)/shard_map/ppermute | solution.py:206
  55.3 0.0 collective-permute-start.9
  55.3 0.0 collective-permute-start.6
  55.3 0.0 collective-permute-done.2.refs_1_
  55.3 2.0 %collective-permute-start.5 = (bf16[1,4,256,256]{3,2,1,0:T(8,128)(2,1)S(1)}, bf16[1,4,256,256]{3,2,1,0:T(8,128)(2,1)S(1)}, u32[]{:S(2)}, u32[]{:S(2)}) collective-permute-start(bf16[1,4,256,256]{3,2,1,0:T(8,128)(2,1)S(1)} %collective-permute-done.2.refs_1_), channel_id=1, source_target_pairs={{0,1},{1,0},{2,3},{3,2},{4,5},{5,4},{6,7},{7,6},{8,9},{9,8},{10,11... | collective-permute-start | bytes 1572872 | tf_op jit(solution)/shard_map/ppermute | solution.py:209
  57.3 0.0 collective-permute-done.9.refs_8_
  57.3 0.0 copy-start
  57.3 0.7 copy-done
  58.0 0.0 collective-permute-start.7
  58.0 0.0 collective-permute-done.4.refs_3_
  58.0 0.5 collective-permute-start.10
  58.6 5.9 %collective-permute-done.6.refs_5_ = bf16[1,2,256,256]{3,2,1,0:T(8,128)(2,1)S(1)} collective-permute-done((bf16[1,2,256,256]{3,2,1,0:T(8,128)(2,1)S(1)}, bf16[1,2,256,256]{3,2,1,0:T(8,128)(2,1)S(1)}, u32[]{:S(2)}, u32[]{:S(2)}) %collective-permute-start.6) | collective-permute-done | bytes 262176 | tf_op jit(solution)/shard_map/ppermute | solution.py:209
  64.4 0.0 collective-permute-start.12
  64.4 0.0 copy-start.2
  64.4 0.7 copy-done.2
  65.1 0.8 collective-permute-done.12.refs_11_
  65.9 0.0 copy-start.4
  65.9 0.7 copy-done.4
  66.7 0.1 collective-permute-start.8
  66.8 8.5 %collective-permute-done.5.refs_4_ = bf16[1,4,256,256]{3,2,1,0:T(8,128)(2,1)S(1)} collective-permute-done((bf16[1,4,256,256]{3,2,1,0:T(8,128)(2,1)S(1)}, bf16[1,4,256,256]{3,2,1,0:T(8,128)(2,1)S(1)}, u32[]{:S(2)}, u32[]{:S(2)}) %collective-permute-start.5) | collective-permute-done | bytes 524320 | tf_op jit(solution)/shard_map/ppermute | solution.py:209
  75.3 0.0 collective-permute-start.11
  75.3 0.1 pad_add_fusion.where
  75.4 0.0 collective-permute-done.8.refs_7_
  75.4 2.0 %collective-permute-done.11.refs_10_ = bf16[1,4,256,256]{3,2,1,0:T(8,128)(2,1)} collective-permute-done((bf16[1,4,256,256]{3,2,1,0:T(8,128)(2,1)S(1)}, bf16[1,4,256,256]{3,2,1,0:T(8,128)(2,1)}, u32[]{:S(2)}, u32[]{:S(2)}) %collective-permute-start.11) | collective-permute-done | bytes 524320 | tf_op jit(solution)/shard_map/ppermute | solution.py:213
  77.3 0.0 collective-permute-done.beside
  77.3 0.0 collective-permute-done.7.refs_6_
  77.3 0.0 collective-permute-done.10.refs_9_
  77.3 0.0 copy-done.6
  77.3 0.0 copy-start.1
  77.4 0.9 %copy-done.1 = bf16[1,2,256,256]{3,2,1,0:T(8,128)(2,1)S(1)} copy-done((bf16[1,2,256,256]{3,2,1,0:T(8,128)(2,1)S(1)}, bf16[1,2,256,256]{3,2,1,0:T(8,128)(2,1)}, u32[]{:S(2)}) %copy-start.1) | copy-done | bytes 262168
  78.3 0.0 copy-start.3
  78.3 0.9 %copy-done.3 = bf16[1,2,256,256]{3,2,1,0:T(8,128)(2,1)S(1)} copy-done((bf16[1,2,256,256]{3,2,1,0:T(8,128)(2,1)S(1)}, bf16[1,2,256,256]{3,2,1,0:T(8,128)(2,1)}, u32[]{:S(2)}) %copy-start.3) | copy-done | bytes 262168
  79.2 0.0 copy-start.5
  79.2 0.9 %copy-done.5 = bf16[1,2,256,256]{3,2,1,0:T(8,128)(2,1)S(1)} copy-done((bf16[1,2,256,256]{3,2,1,0:T(8,128)(2,1)S(1)}, bf16[1,2,256,256]{3,2,1,0:T(8,128)(2,1)}, u32[]{:S(2)}) %copy-start.5) | copy-done | bytes 262168
  80.2 13.6 %purify.1 = f32[1,13,256,128]{3,2,1,0:T(8,128)} custom-call(s32[3]{0:T(128)S(1)} %pad_add_fusion.where, s32[1,13]{1,0:T(1,128)S(1)} %copy-done.6, bf16[1,13,256,256]{3,2,1,0:T(8,128)(2,1)} %own.1, bf16[1,13,256,256]{3,2,1,0:T(8,128)(2,1)} %collective-permute-done.beside, bf16[1,8,256,256]{3,2,1,0:T(8,128)(2,1)S(1)} %collective-permute-done.1.refs_0_, ...), custom_call_target="tpu_custom_call" | custom-call | flops 12784238592 | bytes 14680064 | tf_op jit(solution)/shard_map/purify/pallas_call | solution.py:168
Async XLA Ops:
  0.0 77.3 %copy-start.6 = (s32[1,13]{1,0:T(1,128)S(1)}, s32[1,13]{1,0:T(1,128)}, u32[]{:S(2)}) copy-start(s32[1,13]{1,0:T(1,128)} %keep.1) | copy-start | bytes 160
  4.7 27.2 %collective-permute-start.1 = (bf16[1,8,256,256]{3,2,1,0:T(8,128)(2,1)}, bf16[1,8,256,256]{3,2,1,0:T(8,128)(2,1)S(1)}, u32[]{:S(2)}, u32[]{:S(2)}) collective-permute-start(bf16[1,8,256,256]{3,2,1,0:T(8,128)(2,1)} %get-tuple-element.8), channel_id=1, source_target_pairs={{0,28},{1,5},{2,6},{3,31},{4,0},{5,9},{6,10},{7,3},{8,4},{9,13},{1... | collective-permute-start | bytes 3145736 | tf_op jit(solution)/shard_map/ppermute | solution.py:206
  32.0 26.1 %collective-permute-start.4 = (bf16[1,8,256,256]{3,2,1,0:T(8,128)(2,1)S(1)}, bf16[1,8,256,256]{3,2,1,0:T(8,128)(2,1)S(1)}, u32[]{:S(2)}, u32[]{:S(2)}) collective-permute-start(bf16[1,8,256,256]{3,2,1,0:T(8,128)(2,1)S(1)} %collective-permute-done.1.refs_0_), channel_id=1, source_target_pairs={{0,1},{1,0},{2,3},{3,2},{4,5},{5,4},{6,7},{7,6},{8,9},{9,8},{10,11... | collective-permute-start | bytes 3145736 | tf_op jit(solution)/shard_map/ppermute | solution.py:209
  32.9 44.5 %collective-permute-start = (bf16[1,13,256,256]{3,2,1,0:T(8,128)(2,1)}, bf16[1,13,256,256]{3,2,1,0:T(8,128)(2,1)}, u32[]{:S(2)}, u32[]{:S(2)}) collective-permute-start(bf16[1,13,256,256]{3,2,1,0:T(8,128)(2,1)} %own.1), channel_id=1, source_target_pairs={{0,2},{2,0},{4,6},{6,4},{1,3},{3,1},{5,7},{7,5},{8,10},{10,8},{12,... | collective-permute-start | bytes 5111816 | tf_op jit(solution)/shard_map/ppermute | solution.py:213
  32.9 22.4 %collective-permute-start.2 = (bf16[1,4,256,256]{3,2,1,0:T(8,128)(2,1)}, bf16[1,4,256,256]{3,2,1,0:T(8,128)(2,1)S(1)}, u32[]{:S(2)}, u32[]{:S(2)}) collective-permute-start(bf16[1,4,256,256]{3,2,1,0:T(8,128)(2,1)} %get-tuple-element.9), channel_id=1, source_target_pairs={{0,24},{1,9},{2,10},{3,27},{4,28},{5,13},{6,14},{7,31},{8,0},{9,17... | collective-permute-start | bytes 1572872 | tf_op jit(solution)/shard_map/ppermute | solution.py:206
  36.7 18.6 %collective-permute-start.3 = (bf16[1,2,256,256]{3,2,1,0:T(8,128)(2,1)}, bf16[1,2,256,256]{3,2,1,0:T(8,128)(2,1)S(1)}, u32[]{:S(2)}, u32[]{:S(2)}) collective-permute-start(bf16[1,2,256,256]{3,2,1,0:T(8,128)(2,1)} %get-tuple-element.10), channel_id=1, source_target_pairs={{0,20},{1,13},{2,14},{3,23},{4,24},{5,17},{6,18},{7,27},{8,28},{9,... | collective-permute-start | bytes 786440 | tf_op jit(solution)/shard_map/ppermute | solution.py:206
  55.3 2.0 %collective-permute-start.9 = (bf16[1,2,256,256]{3,2,1,0:T(8,128)(2,1)S(1)}, bf16[1,2,256,256]{3,2,1,0:T(8,128)(2,1)S(1)}, u32[]{:S(2)}, u32[]{:S(2)}) collective-permute-start(bf16[1,2,256,256]{3,2,1,0:T(8,128)(2,1)S(1)} %collective-permute-done.3.refs_2_), channel_id=1, source_target_pairs={{0,2},{2,0},{4,6},{6,4},{1,3},{3,1},{5,7},{7,5},{8,10},{10,8},{12,... | collective-permute-start | bytes 786440 | tf_op jit(solution)/shard_map/ppermute | solution.py:213
  55.3 9.1 %collective-permute-start.6 = (bf16[1,2,256,256]{3,2,1,0:T(8,128)(2,1)S(1)}, bf16[1,2,256,256]{3,2,1,0:T(8,128)(2,1)S(1)}, u32[]{:S(2)}, u32[]{:S(2)}) collective-permute-start(bf16[1,2,256,256]{3,2,1,0:T(8,128)(2,1)S(1)} %collective-permute-done.3.refs_2_), channel_id=1, source_target_pairs={{0,1},{1,0},{2,3},{3,2},{4,5},{5,4},{6,7},{7,6},{8,9},{9,8},{10,11... | collective-permute-start | bytes 786440 | tf_op jit(solution)/shard_map/ppermute | solution.py:209
  55.3 20.0 %collective-permute-start.5 = (bf16[1,4,256,256]{3,2,1,0:T(8,128)(2,1)S(1)}, bf16[1,4,256,256]{3,2,1,0:T(8,128)(2,1)S(1)}, u32[]{:S(2)}, u32[]{:S(2)}) collective-permute-start(bf16[1,4,256,256]{3,2,1,0:T(8,128)(2,1)S(1)} %collective-permute-done.2.refs_1_), channel_id=1, source_target_pairs={{0,1},{1,0},{2,3},{3,2},{4,5},{5,4},{6,7},{7,6},{8,9},{9,8},{10,11... | collective-permute-start | bytes 1572872 | tf_op jit(solution)/shard_map/ppermute | solution.py:209
  57.3 0.7 copy-start
  58.0 19.3 %collective-permute-start.7 = (bf16[1,8,256,256]{3,2,1,0:T(8,128)(2,1)S(1)}, bf16[1,8,256,256]{3,2,1,0:T(8,128)(2,1)}, u32[]{:S(2)}, u32[]{:S(2)}) collective-permute-start(bf16[1,8,256,256]{3,2,1,0:T(8,128)(2,1)S(1)} %collective-permute-done.1.refs_0_), channel_id=1, source_target_pairs={{0,2},{2,0},{4,6},{6,4},{1,3},{3,1},{5,7},{7,5},{8,10},{10,8},{12,... | collective-permute-start | bytes 3145736 | tf_op jit(solution)/shard_map/ppermute | solution.py:213
  58.0 19.3 %collective-permute-start.10 = (bf16[1,8,256,256]{3,2,1,0:T(8,128)(2,1)S(1)}, bf16[1,8,256,256]{3,2,1,0:T(8,128)(2,1)}, u32[]{:S(2)}, u32[]{:S(2)}) collective-permute-start(bf16[1,8,256,256]{3,2,1,0:T(8,128)(2,1)S(1)} %collective-permute-done.4.refs_3_), channel_id=1, source_target_pairs={{0,2},{2,0},{4,6},{6,4},{1,3},{3,1},{5,7},{7,5},{8,10},{10,8},{12,... | collective-permute-start | bytes 3145736 | tf_op jit(solution)/shard_map/ppermute | solution.py:213
  64.4 1.5 %collective-permute-start.12 = (bf16[1,2,256,256]{3,2,1,0:T(8,128)(2,1)S(1)}, bf16[1,2,256,256]{3,2,1,0:T(8,128)(2,1)S(1)}, u32[]{:S(2)}, u32[]{:S(2)}) collective-permute-start(bf16[1,2,256,256]{3,2,1,0:T(8,128)(2,1)S(1)} %collective-permute-done.6.refs_5_), channel_id=1, source_target_pairs={{0,2},{2,0},{4,6},{6,4},{1,3},{3,1},{5,7},{7,5},{8,10},{10,8},{12,... | collective-permute-start | bytes 786440 | tf_op jit(solution)/shard_map/ppermute | solution.py:213
  64.4 0.7 copy-start.2
  65.9 0.7 copy-start.4
  66.7 8.7 %collective-permute-start.8 = (bf16[1,4,256,256]{3,2,1,0:T(8,128)(2,1)S(1)}, bf16[1,4,256,256]{3,2,1,0:T(8,128)(2,1)}, u32[]{:S(2)}, u32[]{:S(2)}) collective-permute-start(bf16[1,4,256,256]{3,2,1,0:T(8,128)(2,1)S(1)} %collective-permute-done.2.refs_1_), channel_id=1, source_target_pairs={{0,2},{2,0},{4,6},{6,4},{1,3},{3,1},{5,7},{7,5},{8,10},{10,8},{12,... | collective-permute-start | bytes 1572872 | tf_op jit(solution)/shard_map/ppermute | solution.py:213
  75.3 2.0 %collective-permute-start.11 = (bf16[1,4,256,256]{3,2,1,0:T(8,128)(2,1)S(1)}, bf16[1,4,256,256]{3,2,1,0:T(8,128)(2,1)}, u32[]{:S(2)}, u32[]{:S(2)}) collective-permute-start(bf16[1,4,256,256]{3,2,1,0:T(8,128)(2,1)S(1)} %collective-permute-done.5.refs_4_), channel_id=1, source_target_pairs={{0,2},{2,0},{4,6},{6,4},{1,3},{3,1},{5,7},{7,5},{8,10},{10,8},{12,... | collective-permute-start | bytes 1572872 | tf_op jit(solution)/shard_map/ppermute | solution.py:213
  77.3 1.0 %copy-start.1 = (bf16[1,2,256,256]{3,2,1,0:T(8,128)(2,1)S(1)}, bf16[1,2,256,256]{3,2,1,0:T(8,128)(2,1)}, u32[]{:S(2)}) copy-start(bf16[1,2,256,256]{3,2,1,0:T(8,128)(2,1)} %copy-done) | copy-start | bytes 786436
  78.3 0.9 %copy-start.3 = (bf16[1,2,256,256]{3,2,1,0:T(8,128)(2,1)S(1)}, bf16[1,2,256,256]{3,2,1,0:T(8,128)(2,1)}, u32[]{:S(2)}) copy-start(bf16[1,2,256,256]{3,2,1,0:T(8,128)(2,1)} %copy-done.2) | copy-start | bytes 786436
  79.2 0.9 %copy-start.5 = (bf16[1,2,256,256]{3,2,1,0:T(8,128)(2,1)S(1)}, bf16[1,2,256,256]{3,2,1,0:T(8,128)(2,1)}, u32[]{:S(2)}) copy-start(bf16[1,2,256,256]{3,2,1,0:T(8,128)(2,1)} %copy-done.4) | copy-start | bytes 786436

commit v3 on v2

v3 whole, which is shorter than its diff:
```python
import jax
import jax.numpy as jnp
from jax import lax
from jax.experimental import pallas as pl
from jax.experimental.pallas import tpu as pltpu
from jax.sharding import PartitionSpec as P

HALF = 6
BAND = 2 * HALF + 1
FORWARD = ((0, 1, 2, 3, 4, 5, -3, -5), (0, 1, 2, 3), (0, 1))
BACKWARD = ((0, 1, 2, 3, 4, -4, -5, -6), (0, 1, 2, -6), (0, 0))
SIZES = tuple(len(part) for part in FORWARD)
WHOLE, MIDDLE, OUTER = SIZES
PART = WHOLE // 2
STARTS = (0, WHOLE, WHOLE + MIDDLE)
FETCHED = sum(SIZES)
LANES = 128
FRAME = range(-HALF, HALF + 1)


def places():
    held = {}
    for offset in FRAME:
        held[0, offset] = offset + HALF
    for offset in FRAME:
        held.setdefault((1, 1 + offset), BAND + offset + HALF)
    slot = 2 * BAND
    for other in (False, True):
        for parts, way in ((FORWARD, 1), (BACKWARD, -1)):
            for step, part in enumerate(parts):
                for offset in part:
                    row = way * 2 * (step + 1)
                    column = row + way * offset
                    if other:
                        row, column = 1 - row, 1 - column
                    if (row, column) not in held and (column, row) not in held:
                        held[row, column] = slot
                    slot += 1
    return held


HELD = places()
def stage(slot):
    if slot < 2 * BAND:
        return 0
    return 1 if (slot - 2 * BAND) % FETCHED >= WHOLE else 2


def terms(column, stages=(0, 1, 2)):
    plain = {}
    turned = {}
    for row in FRAME:
        if abs(row - column) <= HALF:
            if (row, column) in HELD:
                slot, group = HELD[row, column], plain
            else:
                slot, group = HELD[column, row], turned
            if stage(slot) in stages:
                group[row] = slot
    return plain, turned


def pairs():
    def shared(one, two):
        return sum(len(first.keys() & other.keys()) for first, other in zip(terms(one), terms(two)))

    def best(left):
        if len(left) < 2:
            return 0, [left] if left else []
        choices = []
        for place in range(1, len(left)):
            count, rest = best(left[1:place] + left[place + 1 :])
            choices.append((count + shared(left[0], left[place]), [(left[0], left[place])] + rest))
        if len(left) % 2:
            count, rest = best(left[1:])
            choices.append((count, [(left[0],)] + rest))
        return max(choices, key=lambda choice: choice[0])

    return best(tuple(FRAME))[1]


PAIRS = pairs()


def product(lefts, blocks, turned):
    return lax.dot_general(
        jnp.concatenate(lefts, axis=1),
        jnp.concatenate(blocks, axis=1 if turned else 0),
        (((1,), (1 if turned else 0,)), ((), ())),
        preferred_element_type=jnp.float32,
    )


def column_product(left, block, column, stages):
    total = None
    for turned, group in enumerate(terms(column, stages)):
        if group:
            part = product(
                [left(row) for row in group], [block(slot) for slot in group.values()], turned
            )
            total = part if total is None else total + part
    return total


def part_products(left, part, columns):
    totals = [None] * len(columns)

    def add(place, value):
        totals[place] = value if totals[place] is None else totals[place] + value

    for turned in (0, 1):
        groups = [terms(column)[turned] for column in columns]
        both = [row for row in groups[0] if all(row in group for group in groups)]
        if len(columns) > 1 and both:
            blocks = [
                jnp.concatenate([part(group[row], turned) for group in groups], axis=0 if turned else 1)
                for row in both
            ]
            value = product([left(row) for row in both], blocks, turned)
            for place in range(len(columns)):
                add(place, value[:, place * LANES : (place + 1) * LANES])
        for place, group in enumerate(groups):
            alone = [row for row in group if len(columns) == 1 or row not in both]
            if alone:
                blocks = [part(group[row], turned) for row in alone]
                add(place, product([left(row) for row in alone], blocks, turned))
    return totals


def position():
    row = lax.axis_index(("row", "col"))
    return 1 - 2 * (row % 2), lax.axis_index("layer") % 2, (row + row // 2) % 2


def pack_kernel(density, diag, middle, outer, pure):
    way, layer_kind, row_kind = position()

    def bring(out, item, forward, backward, backwards):
        index = HALF + way * jnp.where(backwards == 0, forward, -backward)
        out[0, item] = density[0, index]

    for item in range(PART):
        forward = jnp.where(layer_kind == 0, FORWARD[0][item], FORWARD[0][PART + item])
        backward = jnp.where(layer_kind == 0, BACKWARD[0][item], BACKWARD[0][PART + item])
        bring(diag, item, forward, backward, row_kind)
    for out, step in ((middle, 1), (outer, 2)):
        for item in range(SIZES[step]):
            bring(out, item, FORWARD[step][item], BACKWARD[step][item], layer_kind)
    for item in range(WHOLE):
        bring(pure, item, FORWARD[0][item], BACKWARD[0][item], 1 - row_kind)


def frame_row(way, array):
    return lambda offset: array[0, HALF + way * offset]


def first_kernel(own, beside, sums):
    way, layer_kind, row_kind = position()
    left = frame_row(way, own)
    right = frame_row(way, beside)
    for column in FRAME:
        block = lambda slot: left(slot - HALF) if slot < BAND else right(slot - BAND - HALF)
        sums[column + HALF] = column_product(left, block, column, (0,))


def second_kernel(own, *refs):
    sources, (before, sums, far, sems) = refs[:8], refs[8:]
    way, layer_kind, row_kind = position()
    copies = []
    for group in range(2):
        for step, start in ((1, 0), (2, MIDDLE)):
            for place in range(2):
                source = sources[group * 4 + (step - 1) * 2 + place]
                kind = layer_kind if place == 0 else 1 - layer_kind
                base = (group * 2 + kind) * (MIDDLE + OUTER) + start
                copies.append(
                    pltpu.make_async_copy(
                        source.at[0], far.at[pl.ds(base, SIZES[step])], sems.at[len(copies)]
                    )
                )
    for copy in copies:
        copy.start()
    for copy in copies:
        copy.wait()
    left = frame_row(way, own)
    for column in FRAME:
        block = lambda slot: far[far_place(slot)]
        total = column_product(left, block, column, (1,))
        sums[column + HALF] = before[column + HALF] + (0.0 if total is None else total)


def far_place(slot):
    group, item = divmod(slot - 2 * BAND, FETCHED)
    return group * (MIDDLE + OUTER) + item - WHOLE


def last_kernel(keep, own, beside, far, *refs):
    sources, refs = refs[:6], refs[6:]
    before, out, following, rounded, square, result, sems, out_sems = refs
    way, layer_kind, row_kind = position()
    part = lax.axis_index("layer") * (own.shape[2] // lax.axis_size("layer")) // LANES
    copies = []

    def bring(source, first, size):
        copies.append(
            pltpu.make_async_copy(
                source.at[0], following.at[pl.ds(first, size)], sems.at[len(copies)]
            )
        )

    for group in range(2):
        pure, near, remote = sources[group * 3 : group * 3 + 3]
        kind = row_kind if group == 0 else 1 - row_kind
        bring(pure, (group * 2 + kind) * WHOLE, WHOLE)
        base = (group * 2 + 1 - kind) * WHOLE
        bring(near, base + layer_kind * PART, PART)
        bring(remote, base + (1 - layer_kind) * PART, PART)
    for copy in copies:
        copy.start()
    for copy in copies:
        copy.wait()

    left = frame_row(way, own)

    def next_place(slot):
        group, item = divmod(slot - 2 * BAND, FETCHED)
        return group * WHOLE + item

    for column in FRAME:
        total = column_product(left, lambda slot: following[next_place(slot)], column, (2,))
        total = before[column + HALF] + (0.0 if total is None else total)
        total = total * keep[0, HALF + way * column].astype(jnp.float32)
        rounded[column + HALF] = total.astype(jnp.bfloat16)
        mine = total[:, :LANES]
        for piece in range(1, total.shape[1] // LANES):
            mine = jnp.where(part == piece, total[:, piece * LANES : (piece + 1) * LANES], mine)
        square[column + HALF] = mine

    lanes = pl.ds(pl.multiple_of(part * LANES, LANES), LANES)

    def piece(slot, turned):
        if slot < BAND:
            array, index = own, (0, HALF + way * (slot - HALF))
        elif slot < 2 * BAND:
            array, index = beside, (0, HALF + way * (slot - BAND - HALF))
        elif stage(slot) == 1:
            array, index = far, (far_place(slot),)
        else:
            array, index = following, (next_place(slot),)
        return array[(*index, lanes, slice(None)) if turned else (*index, slice(None), lanes)]

    written = []
    for columns in PAIRS:
        totals = part_products(lambda row: rounded[row + HALF], piece, columns)
        for column, total in zip(columns, totals):
            total = total * keep[0, HALF + way * column].astype(jnp.float32)
            result[column + HALF] = 3.0 * square[column + HALF] - 2.0 * total
            copy = pltpu.make_async_copy(
                result.at[column + HALF], out.at[0, HALF + way * column], out_sems.at[column + HALF]
            )
            copy.start()
            written.append(copy)
    for copy in written:
        copy.wait()


SCALARS = pl.BlockSpec(memory_space=pltpu.SMEM)
ANYWHERE = pl.BlockSpec(memory_space=pl.ANY)
VECTOR = pl.BlockSpec(memory_space=pltpu.VMEM)


def call(kernel, name, shapes, in_specs, out_specs, scratch, products, limit):
    cost = pl.CostEstimate(
        flops=2 * products * 256**3, bytes_accessed=4 * 2**20, transcendentals=0
    )
    return pl.pallas_call(
        kernel,
        out_shape=shapes,
        in_specs=in_specs,
        out_specs=out_specs,
        scratch_shapes=scratch,
        compiler_params=pltpu.CompilerParams(vmem_limit_bytes=limit * 2**20),
        cost_estimate=cost,
        name=name,
    )


def pack(density):
    block = density.shape[2]
    sizes = (PART, MIDDLE, OUTER, WHOLE)
    shapes = [jax.ShapeDtypeStruct((1, size, block, block), density.dtype) for size in sizes]
    return call(pack_kernel, "pack", shapes, [VECTOR], [VECTOR] * len(sizes), [], 1, 8)(density)


def first(own, beside):
    block = own.shape[2]
    shape = jax.ShapeDtypeStruct((BAND, block, block), jnp.float32)
    return call(first_kernel, "first", shape, [VECTOR] * 2, VECTOR, [], 46, 16)(own, beside)


def second(own, far, before):
    block = own.shape[2]
    shapes = [
        jax.ShapeDtypeStruct((BAND, block, block), jnp.float32),
        jax.ShapeDtypeStruct((4 * (MIDDLE + OUTER), block, block), own.dtype),
    ]
    return call(
        second_kernel,
        "second",
        shapes,
        [VECTOR] + [ANYWHERE] * 8 + [VECTOR],
        [VECTOR] * 2,
        [pltpu.SemaphoreType.DMA((8,))],
        30,
        24,
    )(own, *far, before)


def last(keep, own, beside, far, following, before):
    block = own.shape[2]
    shape = jax.ShapeDtypeStruct((1, BAND, block, LANES), jnp.float32)
    return call(
        last_kernel,
        "last",
        shape,
        [SCALARS] + [VECTOR] * 3 + [ANYWHERE] * 6 + [VECTOR],
        ANYWHERE,
        [
            pltpu.VMEM((4 * WHOLE, block, block), own.dtype),
            pltpu.VMEM((BAND, block, block), own.dtype),
            pltpu.VMEM((BAND, block, LANES), jnp.float32),
            pltpu.VMEM((BAND, block, LANES), jnp.float32),
            pltpu.SemaphoreType.DMA((6,)),
            pltpu.SemaphoreType.DMA((BAND,)),
        ],
        120,
        32,
    )(keep, own, beside, far, *following, before)


def after(*arrays):
    return lax.optimization_barrier(arrays)


def body(density, pattern):
    axes = ("row", "col", "layer")
    rows = lax.axis_size(("row", "col"))
    layers = lax.axis_size("layer")
    width = density.shape[2] // layers

    def fetch(array, step):
        pairs = []
        for source in range(rows):
            for plane in range(layers):
                shift = 2 * step * (1 - 2 * (source % 2)) * (1 - 2 * (plane % 2))
                pairs.append((source * layers + plane, (source - shift) % rows * layers + plane))
        return lax.ppermute(array, axes, pairs)

    def fetch_diag(array):
        pairs = []
        for source in range(rows):
            shift = 2 if source // 2 % 2 else -2
            pairs.append((source, (source + shift) % rows))
        return lax.ppermute(array, ("row", "col"), pairs)

    def swap(array, axis, distance):
        peers = lax.axis_size(axis)
        return lax.ppermute(array, axis, [(peer, peer ^ distance) for peer in range(peers)])

    swap_cores = lambda array: swap(array, "col", 1)
    swap_layers = lambda array: swap(array, "layer", 1)

    beside = swap_cores(density)
    diag, middle, outer, pure = pack(density)
    diag = fetch_diag(diag)
    middle = fetch(middle, 2)
    outer = fetch(outer, 3)
    pure = swap(pure, "col", 2)
    sums = first(density, beside)
    sums, middle = after(sums, middle)
    far_middle = swap_layers(middle)
    other_middle = swap_cores(middle)
    middle, outer = after(middle, outer)
    far_outer = swap_layers(outer)
    other_outer = swap_cores(outer)
    outer, diag = after(outer, diag)
    far_diag = swap_layers(diag)
    other_diag = swap_cores(diag)
    diag, far_middle, far_outer, pure = after(diag, far_middle, far_outer, pure)
    other_far_middle = swap_cores(far_middle)
    other_far_outer = swap_cores(far_outer)
    other_pure = swap_cores(pure)
    far = [middle, far_middle, outer, far_outer]
    far = far + [other_middle, other_far_middle, other_outer, other_far_outer]
    sums, far = second(density, far, sums)
    other_far_diag = swap_cores(far_diag)
    following = [pure, diag, far_diag, other_pure, other_diag, other_far_diag]
    out = last(pattern, density, beside, far, following, sums)
    if width < LANES:
        layer = lax.axis_index("layer")
        out = lax.dynamic_slice_in_dim(out, layer * width % LANES, width, 3)
    return out


def solution(mesh):
    return jax.shard_map(
        body,
        mesh=mesh,
        in_specs=(P(("row", "col"), None, None, None), P(("row", "col"), None)),
        out_specs=P(("row", "col"), None, None, "layer"),
        check_vma=False,
    )
```

time: 95.7 us -> 67.5 us (0.71)
  the two profiles are of different devices: /device:TPU:0 before, /device:TPU:19 now
where the time goes in v3:
time: 67.5 us; the launch traced here: 67.3 us
  waiting for transfers between devices  33.1 us (49%)
  starting transfers between devices  21.2 us (31%)
  Pallas kernels  10 us (15%)
  local copies, waits for them, and re-layouts  2.92 us (4%)
    ppermute x12, starting transfers between devices, swap(): lax.ppermute(array, axis, [(peer, peer ^ distance) for peer in range(peer...  16.6 us
    ppermute x2, waiting for transfers between devices, fetch(): return lax.ppermute(array, axes, pairs)  16.2 us
    ppermute x12, waiting for transfers between devices, swap(): lax.ppermute(array, axis, [(peer, peer ^ distance) for peer in range(peer...  10.5 us
    pallas_call x1, Pallas kernels, last(): call(last_kernel, 'last', shape, [SCALARS] + [VECTOR] * 3 + [ANYWHERE] *...  6.55 us
    ppermute x1, waiting for transfers between devices, fetch_diag(): return lax.ppermute(array, ('row', 'col'), pairs)  6.34 us
    ppermute x2, starting transfers between devices, fetch(): return lax.ppermute(array, axes, pairs)  3.37 us
    unnamed x8, local copies, waits for them, and re-layouts  2.92 us
    pallas_call x1, Pallas kernels, first(): call(first_kernel, 'first', shape, [VECTOR] * 2, VECTOR, [], 46, 16)  1.74 us
  transfers between devices with their start and end apart: 15, of which 6 were waited for; matrix products, arithmetic and copies ran while one was open for 0% of the time, Pallas kernels for 5%

profile of v3, /device:TPU:19, one launch (start us, length us, event | category | flops | bytes accessed | tf_op | source)
XLA Modules:
  0.0 67.3 jit_solution(5257106251719472194)
XLA Ops:
  0.0 0.7 %collective-permute-start = (bf16[1,13,256,256]{3,2,1,0:T(8,128)(2,1)}, bf16[1,13,256,256]{3,2,1,0:T(8,128)(2,1)S(1)}, u32[]{:S(2)}, u32[]{:S(2)}) collective-permute-start(bf16[1,13,256,256]{3,2,1,0:T(8,128)(2,1)} %own.5), channel_id=1, source_target_pairs={{0,2},{2,0},{4,6},{6,4},{1,3},{3,1},{5,7},{7,5},{8,10},{10,8},{12,... | collective-permute-start | bytes 5111816 | tf_op jit(solution)/shard_map/ppermute | solution.py:368
  0.7 0.0 copy-start
  0.7 1.5 %copy-done = bf16[1,13,256,256]{3,2,1,0:T(8,128)(2,1)S(1)} copy-done((bf16[1,13,256,256]{3,2,1,0:T(8,128)(2,1)S(1)}, bf16[1,13,256,256]{3,2,1,0:T(8,128)(2,1)}, u32[]{:S(2)}) %copy-start) | copy-done | bytes 1703960
  2.1 0.2 pack.1
  2.3 0.2 collective-permute-start.1
  2.5 1.2 %collective-permute-start.6 = (bf16[1,8,256,256]{3,2,1,0:T(8,128)(2,1)S(1)}, bf16[1,8,256,256]{3,2,1,0:T(8,128)(2,1)S(1)}, u32[]{:S(2)}, u32[]{:S(2)}) collective-permute-start(bf16[1,8,256,256]{3,2,1,0:T(8,128)(2,1)S(1)} %get-tuple-element.28), channel_id=1, source_target_pairs={{0,4},{2,6},{4,0},{6,2},{1,5},{3,7},{5,1},{7,3},{8,12},{10,14},{12... | collective-permute-start | bytes 3145736 | tf_op jit(solution)/shard_map/ppermute | solution.py:368
  3.8 3.2 %collective-permute-start.2 = (bf16[1,2,256,256]{3,2,1,0:T(8,128)(2,1)S(1)}, bf16[1,2,256,256]{3,2,1,0:T(8,128)(2,1)S(1)}, u32[]{:S(2)}, u32[]{:S(2)}) collective-permute-start(bf16[1,2,256,256]{3,2,1,0:T(8,128)(2,1)S(1)} %get-tuple-element.23), channel_id=1, source_target_pairs={{0,20},{1,13},{2,14},{3,23},{4,24},{5,17},{6,18},{7,27},{8,28},{9,... | collective-permute-start | bytes 786440 | tf_op jit(solution)/shard_map/ppermute | solution.py:357
  6.9 1.2 %collective-permute-start.3 = (bf16[1,4,256,256]{3,2,1,0:T(8,128)(2,1)S(1)}, bf16[1,4,256,256]{3,2,1,0:T(8,128)(2,1)S(1)}, u32[]{:S(2)}, u32[]{:S(2)}) collective-permute-start(bf16[1,4,256,256]{3,2,1,0:T(8,128)(2,1)S(1)} %get-tuple-element.26), channel_id=1, source_target_pairs={{0,28},{2,30},{4,8},{6,10},{8,4},{10,6},{12,16},{14,18},{16,12},{1... | collective-permute-start | bytes 1572872 | tf_op jit(solution)/shard_map/ppermute | solution.py:364
  8.1 0.0 collective-permute-done.beside
  8.1 0.0 copy-start.1
  8.1 1.5 %copy-done.1 = bf16[1,13,256,256]{3,2,1,0:T(8,128)(2,1)S(1)} copy-done((bf16[1,13,256,256]{3,2,1,0:T(8,128)(2,1)S(1)}, bf16[1,13,256,256]{3,2,1,0:T(8,128)(2,1)}, u32[]{:S(2)}) %copy-start.1) | copy-done | bytes 1703960
  9.6 0.0 copy-start.2
  9.6 1.7 %first.1.refs_8_ = f32[13,256,256]{2,1,0:T(8,128)S(1)} custom-call(bf16[1,13,256,256]{3,2,1,0:T(8,128)(2,1)S(1)} %copy-done.1, bf16[1,13,256,256]{3,2,1,0:T(8,128)(2,1)S(1)} %collective-permute-done.beside), custom_call_target="tpu_custom_call" | custom-call | flops 1543503872 | bytes 4194304 | tf_op jit(solution)/shard_map/first/pallas_call | solution.py:298
  11.4 0.0 copy-start.3
  11.4 10.4 %collective-permute-done.1.refs_0_ = bf16[1,4,256,256]{3,2,1,0:T(8,128)(2,1)S(1)} collective-permute-done((bf16[1,4,256,256]{3,2,1,0:T(8,128)(2,1)S(1)}, bf16[1,4,256,256]{3,2,1,0:T(8,128)(2,1)S(1)}, u32[]{:S(2)}, u32[]{:S(2)}) %collective-permute-start.1) | collective-permute-done | bytes 524320 | tf_op jit(solution)/shard_map/ppermute | solution.py:357
  21.8 0.0 collective-permute-start.4
  21.8 5.8 %collective-permute-done.2.refs_2_ = bf16[1,2,256,256]{3,2,1,0:T(8,128)(2,1)S(1)} collective-permute-done((bf16[1,2,256,256]{3,2,1,0:T(8,128)(2,1)S(1)}, bf16[1,2,256,256]{3,2,1,0:T(8,128)(2,1)S(1)}, u32[]{:S(2)}, u32[]{:S(2)}) %collective-permute-start.2) | collective-permute-done | bytes 262176 | tf_op jit(solution)/shard_map/ppermute | solution.py:357
  27.6 0.0 collective-permute-start.5
  27.6 6.3 %collective-permute-done.3.refs_1_ = bf16[1,4,256,256]{3,2,1,0:T(8,128)(2,1)S(1)} collective-permute-done((bf16[1,4,256,256]{3,2,1,0:T(8,128)(2,1)S(1)}, bf16[1,4,256,256]{3,2,1,0:T(8,128)(2,1)S(1)}, u32[]{:S(2)}, u32[]{:S(2)}) %collective-permute-start.3) | collective-permute-done | bytes 524320 | tf_op jit(solution)/shard_map/ppermute | solution.py:364
  33.9 3.0 %collective-permute-start.11 = (bf16[1,4,256,256]{3,2,1,0:T(8,128)(2,1)S(1)}, bf16[1,4,256,256]{3,2,1,0:T(8,128)(2,1)S(1)}, u32[]{:S(2)}, u32[]{:S(2)}) collective-permute-start(bf16[1,4,256,256]{3,2,1,0:T(8,128)(2,1)S(1)} %collective-permute-done.3.refs_1_), channel_id=1, source_target_pairs={{0,1},{1,0},{2,3},{3,2},{4,5},{5,4},{6,7},{7,6},{8,9},{9,8},{10,11... | collective-permute-start | bytes 1572872 | tf_op jit(solution)/shard_map/ppermute | solution.py:368
  36.9 5.7 %collective-permute-done.6.refs_0_ = bf16[1,8,256,256]{3,2,1,0:T(8,128)(2,1)S(1)} collective-permute-done((bf16[1,8,256,256]{3,2,1,0:T(8,128)(2,1)S(1)}, bf16[1,8,256,256]{3,2,1,0:T(8,128)(2,1)S(1)}, u32[]{:S(2)}, u32[]{:S(2)}) %collective-permute-start.6) | collective-permute-done | bytes 1048608 | tf_op jit(solution)/shard_map/ppermute | solution.py:368
  42.6 0.0 collective-permute-done.5.refs_3_
  42.6 0.0 collective-permute-done.4.refs_1_
  42.6 9.0 %collective-permute-start.12 = (bf16[1,8,256,256]{3,2,1,0:T(8,128)(2,1)S(1)}, bf16[1,8,256,256]{3,2,1,0:T(8,128)(2,1)S(1)}, u32[]{:S(2)}, u32[]{:S(2)}) collective-permute-start(bf16[1,8,256,256]{3,2,1,0:T(8,128)(2,1)S(1)} %collective-permute-done.6.refs_0_), channel_id=1, source_target_pairs={{0,2},{2,0},{4,6},{6,4},{1,3},{3,1},{5,7},{7,5},{8,10},{10,8},{12,... | collective-permute-start | bytes 3145736 | tf_op jit(solution)/shard_map/ppermute | solution.py:368
  51.6 0.0 collective-permute-start.7
  51.6 0.5 collective-permute-start.9
  52.1 0.0 collective-permute-start.8
  52.1 2.9 %collective-permute-done.9.refs_6_ = bf16[1,2,256,256]{3,2,1,0:T(8,128)(2,1)S(1)} collective-permute-done((bf16[1,2,256,256]{3,2,1,0:T(8,128)(2,1)S(1)}, bf16[1,2,256,256]{3,2,1,0:T(8,128)(2,1)S(1)}, u32[]{:S(2)}, u32[]{:S(2)}) %collective-permute-start.9) | collective-permute-done | bytes 262176 | tf_op jit(solution)/shard_map/ppermute | solution.py:368
  55.0 0.4 collective-permute-start.13
  55.4 0.0 collective-permute-done.11.refs_2_
  55.4 1.8 %collective-permute-start.14 = (bf16[1,4,256,256]{3,2,1,0:T(8,128)(2,1)S(1)}, bf16[1,4,256,256]{3,2,1,0:T(8,128)(2,1)S(1)}, u32[]{:S(2)}, u32[]{:S(2)}) collective-permute-start(bf16[1,4,256,256]{3,2,1,0:T(8,128)(2,1)S(1)} %collective-permute-done.11.refs_2_), channel_id=1, source_target_pairs={{0,2},{2,0},{4,6},{6,4},{1,3},{3,1},{5,7},{7,5},{8,10},{10,8},{12,... | collective-permute-start | bytes 1572872 | tf_op jit(solution)/shard_map/ppermute | solution.py:368
  57.2 0.0 collective-permute-done.7.refs_4_
  57.2 0.0 collective-permute-start.10
  57.2 1.9 %collective-permute-done.10.refs_7_ = bf16[1,2,256,256]{3,2,1,0:T(8,128)(2,1)S(1)} collective-permute-done((bf16[1,2,256,256]{3,2,1,0:T(8,128)(2,1)S(1)}, bf16[1,2,256,256]{3,2,1,0:T(8,128)(2,1)S(1)}, u32[]{:S(2)}, u32[]{:S(2)}) %collective-permute-start.10) | collective-permute-done | bytes 262176 | tf_op jit(solution)/shard_map/ppermute | solution.py:368
  59.1 0.0 collective-permute-done.8.refs_5_
  59.1 0.0 copy-done.2
  59.1 1.5 %second.1 = (f32[13,256,256]{2,1,0:T(8,128)S(1)}, bf16[24,256,256]{2,1,0:T(8,128)(2,1)S(1)}) custom-call(bf16[1,13,256,256]{3,2,1,0:T(8,128)(2,1)S(1)} %copy-done.2, bf16[1,4,256,256]{3,2,1,0:T(8,128)(2,1)S(1)} %collective-permute-done.1.refs_0_, bf16[1,4,256,256]{3,2,1,0:T(8,128)(2,1)S(1)} %collective-permute-done.4.refs_1_, ...), custom_call_target="tpu_custom_call" | custom-call | flops 1006632960 | bytes 4194304 | tf_op jit(solution)/shard_map/second/pallas_call | solution.py:307
  60.7 0.0 collective-permute-done.13.refs_4_
  60.7 0.0 collective-permute-done.14.refs_5_
  60.7 0.0 collective-permute-done.12.refs_3_
  60.7 0.0 copy-done.3
  60.7 6.6 %last.1 = f32[1,13,256,128]{3,2,1,0:T(8,128)} custom-call(s32[1,13]{1,0:T(1,128)S(1)} %copy-done.3, bf16[1,13,256,256]{3,2,1,0:T(8,128)(2,1)S(1)} %copy-done.2, bf16[1,13,256,256]{3,2,1,0:T(8,128)(2,1)S(1)} %collective-permute-done.beside, bf16[24,256,256]{2,1,0:T(8,128)(2,1)S(1)} %get-tuple-element.33.far, ...), custom_call_target="tpu_custom_call" | custom-call | flops 4026531840 | bytes 4194304 | tf_op jit(solution)/shard_map/last/pallas_call | solution.py:322
Async XLA Ops:
  0.0 8.1 %collective-permute-start = (bf16[1,13,256,256]{3,2,1,0:T(8,128)(2,1)}, bf16[1,13,256,256]{3,2,1,0:T(8,128)(2,1)S(1)}, u32[]{:S(2)}, u32[]{:S(2)}) collective-permute-start(bf16[1,13,256,256]{3,2,1,0:T(8,128)(2,1)} %own.5), channel_id=1, source_target_pairs={{0,2},{2,0},{4,6},{6,4},{1,3},{3,1},{5,7},{7,5},{8,10},{10,8},{12,... | collective-permute-start | bytes 5111816 | tf_op jit(solution)/shard_map/ppermute | solution.py:368
  0.7 1.5 %copy-start = (bf16[1,13,256,256]{3,2,1,0:T(8,128)(2,1)S(1)}, bf16[1,13,256,256]{3,2,1,0:T(8,128)(2,1)}, u32[]{:S(2)}) copy-start(bf16[1,13,256,256]{3,2,1,0:T(8,128)(2,1)} %own.5) | copy-start | bytes 5111812
  2.3 19.5 %collective-permute-start.1 = (bf16[1,4,256,256]{3,2,1,0:T(8,128)(2,1)S(1)}, bf16[1,4,256,256]{3,2,1,0:T(8,128)(2,1)S(1)}, u32[]{:S(2)}, u32[]{:S(2)}) collective-permute-start(bf16[1,4,256,256]{3,2,1,0:T(8,128)(2,1)S(1)} %get-tuple-element.21), channel_id=1, source_target_pairs={{0,24},{1,9},{2,10},{3,27},{4,28},{5,13},{6,14},{7,31},{8,0},{9,17... | collective-permute-start | bytes 1572872 | tf_op jit(solution)/shard_map/ppermute | solution.py:357
  2.5 40.1 %collective-permute-start.6 = (bf16[1,8,256,256]{3,2,1,0:T(8,128)(2,1)S(1)}, bf16[1,8,256,256]{3,2,1,0:T(8,128)(2,1)S(1)}, u32[]{:S(2)}, u32[]{:S(2)}) collective-permute-start(bf16[1,8,256,256]{3,2,1,0:T(8,128)(2,1)S(1)} %get-tuple-element.28), channel_id=1, source_target_pairs={{0,4},{2,6},{4,0},{6,2},{1,5},{3,7},{5,1},{7,3},{8,12},{10,14},{12... | collective-permute-start | bytes 3145736 | tf_op jit(solution)/shard_map/ppermute | solution.py:368
  3.8 23.8 %collective-permute-start.2 = (bf16[1,2,256,256]{3,2,1,0:T(8,128)(2,1)S(1)}, bf16[1,2,256,256]{3,2,1,0:T(8,128)(2,1)S(1)}, u32[]{:S(2)}, u32[]{:S(2)}) collective-permute-start(bf16[1,2,256,256]{3,2,1,0:T(8,128)(2,1)S(1)} %get-tuple-element.23), channel_id=1, source_target_pairs={{0,20},{1,13},{2,14},{3,23},{4,24},{5,17},{6,18},{7,27},{8,28},{9,... | collective-permute-start | bytes 786440 | tf_op jit(solution)/shard_map/ppermute | solution.py:357
  6.9 27.0 %collective-permute-start.3 = (bf16[1,4,256,256]{3,2,1,0:T(8,128)(2,1)S(1)}, bf16[1,4,256,256]{3,2,1,0:T(8,128)(2,1)S(1)}, u32[]{:S(2)}, u32[]{:S(2)}) collective-permute-start(bf16[1,4,256,256]{3,2,1,0:T(8,128)(2,1)S(1)} %get-tuple-element.26), channel_id=1, source_target_pairs={{0,28},{2,30},{4,8},{6,10},{8,4},{10,6},{12,16},{14,18},{16,12},{1... | collective-permute-start | bytes 1572872 | tf_op jit(solution)/shard_map/ppermute | solution.py:364
  8.1 1.5 %copy-start.1 = (bf16[1,13,256,256]{3,2,1,0:T(8,128)(2,1)S(1)}, bf16[1,13,256,256]{3,2,1,0:T(8,128)(2,1)}, u32[]{:S(2)}) copy-start(bf16[1,13,256,256]{3,2,1,0:T(8,128)(2,1)} %own.5) | copy-start | bytes 5111812
  9.6 49.5 %copy-start.2 = (bf16[1,13,256,256]{3,2,1,0:T(8,128)(2,1)S(1)}, bf16[1,13,256,256]{3,2,1,0:T(8,128)(2,1)}, u32[]{:S(2)}) copy-start(bf16[1,13,256,256]{3,2,1,0:T(8,128)(2,1)} %own.5) | copy-start | bytes 5111812
  11.4 49.4 %copy-start.3 = (s32[1,13]{1,0:T(1,128)S(1)}, s32[1,13]{1,0:T(1,128)}, u32[]{:S(2)}) copy-start(s32[1,13]{1,0:T(1,128)} %keep.1) | copy-start | bytes 160
  21.8 20.8 %collective-permute-start.4 = (bf16[1,4,256,256]{3,2,1,0:T(8,128)(2,1)S(1)}, bf16[1,4,256,256]{3,2,1,0:T(8,128)(2,1)S(1)}, u32[]{:S(2)}, u32[]{:S(2)}) collective-permute-start(bf16[1,4,256,256]{3,2,1,0:T(8,128)(2,1)S(1)} %collective-permute-done.1.refs_0_), channel_id=1, source_target_pairs={{0,1},{1,0},{2,3},{3,2},{4,5},{5,4},{6,7},{7,6},{8,9},{9,8},{10,11... | collective-permute-start | bytes 1572872 | tf_op jit(solution)/shard_map/ppermute | solution.py:368
  27.6 15.0 %collective-permute-start.5 = (bf16[1,2,256,256]{3,2,1,0:T(8,128)(2,1)S(1)}, bf16[1,2,256,256]{3,2,1,0:T(8,128)(2,1)S(1)}, u32[]{:S(2)}, u32[]{:S(2)}) collective-permute-start(bf16[1,2,256,256]{3,2,1,0:T(8,128)(2,1)S(1)} %collective-permute-done.2.refs_2_), channel_id=1, source_target_pairs={{0,1},{1,0},{2,3},{3,2},{4,5},{5,4},{6,7},{7,6},{8,9},{9,8},{10,11... | collective-permute-start | bytes 786440 | tf_op jit(solution)/shard_map/ppermute | solution.py:368
  33.9 21.5 %collective-permute-start.11 = (bf16[1,4,256,256]{3,2,1,0:T(8,128)(2,1)S(1)}, bf16[1,4,256,256]{3,2,1,0:T(8,128)(2,1)S(1)}, u32[]{:S(2)}, u32[]{:S(2)}) collective-permute-start(bf16[1,4,256,256]{3,2,1,0:T(8,128)(2,1)S(1)} %collective-permute-done.3.refs_1_), channel_id=1, source_target_pairs={{0,1},{1,0},{2,3},{3,2},{4,5},{5,4},{6,7},{7,6},{8,9},{9,8},{10,11... | collective-permute-start | bytes 1572872 | tf_op jit(solution)/shard_map/ppermute | solution.py:368
  42.6 18.1 %collective-permute-start.12 = (bf16[1,8,256,256]{3,2,1,0:T(8,128)(2,1)S(1)}, bf16[1,8,256,256]{3,2,1,0:T(8,128)(2,1)S(1)}, u32[]{:S(2)}, u32[]{:S(2)}) collective-permute-start(bf16[1,8,256,256]{3,2,1,0:T(8,128)(2,1)S(1)} %collective-permute-done.6.refs_0_), channel_id=1, source_target_pairs={{0,2},{2,0},{4,6},{6,4},{1,3},{3,1},{5,7},{7,5},{8,10},{10,8},{12,... | collective-permute-start | bytes 3145736 | tf_op jit(solution)/shard_map/ppermute | solution.py:368
  51.6 5.6 %collective-permute-start.7 = (bf16[1,4,256,256]{3,2,1,0:T(8,128)(2,1)S(1)}, bf16[1,4,256,256]{3,2,1,0:T(8,128)(2,1)S(1)}, u32[]{:S(2)}, u32[]{:S(2)}) collective-permute-start(bf16[1,4,256,256]{3,2,1,0:T(8,128)(2,1)S(1)} %collective-permute-done.1.refs_0_), channel_id=1, source_target_pairs={{0,2},{2,0},{4,6},{6,4},{1,3},{3,1},{5,7},{7,5},{8,10},{10,8},{12,... | collective-permute-start | bytes 1572872 | tf_op jit(solution)/shard_map/ppermute | solution.py:368
  51.6 3.4 %collective-permute-start.9 = (bf16[1,2,256,256]{3,2,1,0:T(8,128)(2,1)S(1)}, bf16[1,2,256,256]{3,2,1,0:T(8,128)(2,1)S(1)}, u32[]{:S(2)}, u32[]{:S(2)}) collective-permute-start(bf16[1,2,256,256]{3,2,1,0:T(8,128)(2,1)S(1)} %collective-permute-done.2.refs_2_), channel_id=1, source_target_pairs={{0,2},{2,0},{4,6},{6,4},{1,3},{3,1},{5,7},{7,5},{8,10},{10,8},{12,... | collective-permute-start | bytes 786440 | tf_op jit(solution)/shard_map/ppermute | solution.py:368
  52.1 7.0 %collective-permute-start.8 = (bf16[1,4,256,256]{3,2,1,0:T(8,128)(2,1)S(1)}, bf16[1,4,256,256]{3,2,1,0:T(8,128)(2,1)S(1)}, u32[]{:S(2)}, u32[]{:S(2)}) collective-permute-start(bf16[1,4,256,256]{3,2,1,0:T(8,128)(2,1)S(1)} %collective-permute-done.4.refs_1_), channel_id=1, source_target_pairs={{0,2},{2,0},{4,6},{6,4},{1,3},{3,1},{5,7},{7,5},{8,10},{10,8},{12,... | collective-permute-start | bytes 1572872 | tf_op jit(solution)/shard_map/ppermute | solution.py:368
  55.0 5.7 %collective-permute-start.13 = (bf16[1,4,256,256]{3,2,1,0:T(8,128)(2,1)S(1)}, bf16[1,4,256,256]{3,2,1,0:T(8,128)(2,1)S(1)}, u32[]{:S(2)}, u32[]{:S(2)}) collective-permute-start(bf16[1,4,256,256]{3,2,1,0:T(8,128)(2,1)S(1)} %collective-permute-done.3.refs_1_), channel_id=1, source_target_pairs={{0,2},{2,0},{4,6},{6,4},{1,3},{3,1},{5,7},{7,5},{8,10},{10,8},{12,... | collective-permute-start | bytes 1572872 | tf_op jit(solution)/shard_map/ppermute | solution.py:368
  55.4 5.3 %collective-permute-start.14 = (bf16[1,4,256,256]{3,2,1,0:T(8,128)(2,1)S(1)}, bf16[1,4,256,256]{3,2,1,0:T(8,128)(2,1)S(1)}, u32[]{:S(2)}, u32[]{:S(2)}) collective-permute-start(bf16[1,4,256,256]{3,2,1,0:T(8,128)(2,1)S(1)} %collective-permute-done.11.refs_2_), channel_id=1, source_target_pairs={{0,2},{2,0},{4,6},{6,4},{1,3},{3,1},{5,7},{7,5},{8,10},{10,8},{12,... | collective-permute-start | bytes 1572872 | tf_op jit(solution)/shard_map/ppermute | solution.py:368
  57.2 1.9 %collective-permute-start.10 = (bf16[1,2,256,256]{3,2,1,0:T(8,128)(2,1)S(1)}, bf16[1,2,256,256]{3,2,1,0:T(8,128)(2,1)S(1)}, u32[]{:S(2)}, u32[]{:S(2)}) collective-permute-start(bf16[1,2,256,256]{3,2,1,0:T(8,128)(2,1)S(1)} %collective-permute-done.5.refs_3_), channel_id=1, source_target_pairs={{0,2},{2,0},{4,6},{6,4},{1,3},{3,1},{5,7},{7,5},{8,10},{10,8},{12,... | collective-permute-start | bytes 786440 | tf_op jit(solution)/shard_map/ppermute | solution.py:368

commit v4 on v3

--- a/solution.py
+++ b/solution.py
@@ -43,7 +43,7 @@
 def stage(slot):
     if slot < 2 * BAND:
         return 0
-    return 1 if (slot - 2 * BAND) % FETCHED >= WHOLE else 2
+    return 1 if WHOLE <= (slot - 2 * BAND) % FETCHED < WHOLE + MIDDLE else 2
 
 
 def terms(column, stages=(0, 1, 2)):
@@ -163,60 +163,70 @@
         sums[column + HALF] = column_product(left, block, column, (0,))
 
 
-def second_kernel(own, *refs):
-    sources, (before, sums, far, sems) = refs[:8], refs[8:]
+def middle_place(slot):
+    group, item = divmod(slot - 2 * BAND, FETCHED)
+    return group * MIDDLE + item - WHOLE
+
+
+def bundle_kernel(*refs):
+    arrays, out = refs[:-1], refs[-1]
+    place = 0
+    for array in arrays:
+        for item in range(array.shape[1]):
+            out[0, place] = array[0, item]
+            place += 1
+
+
+def second_kernel(own, near, far, other_near, other_far, before, sums, held, sems):
     way, layer_kind, row_kind = position()
     copies = []
-    for group in range(2):
-        for step, start in ((1, 0), (2, MIDDLE)):
-            for place in range(2):
-                source = sources[group * 4 + (step - 1) * 2 + place]
-                kind = layer_kind if place == 0 else 1 - layer_kind
-                base = (group * 2 + kind) * (MIDDLE + OUTER) + start
-                copies.append(
-                    pltpu.make_async_copy(
-                        source.at[0], far.at[pl.ds(base, SIZES[step])], sems.at[len(copies)]
-                    )
+    for other, sources in enumerate(((near, far), (other_near, other_far))):
+        for source, kind in zip(sources, (layer_kind, 1 - layer_kind)):
+            copies.append(
+                pltpu.make_async_copy(
+                    source.at[0, pl.ds(0, MIDDLE)],
+                    held.at[pl.ds((other * 2 + kind) * MIDDLE, MIDDLE)],
+                    sems.at[len(copies)],
                 )
+            )
     for copy in copies:
         copy.start()
     for copy in copies:
         copy.wait()
     left = frame_row(way, own)
     for column in FRAME:
-        block = lambda slot: far[far_place(slot)]
+        block = lambda slot: held[middle_place(slot)]
         total = column_product(left, block, column, (1,))
         sums[column + HALF] = before[column + HALF] + (0.0 if total is None else total)
 
 
-def far_place(slot):
-    group, item = divmod(slot - 2 * BAND, FETCHED)
-    return group * (MIDDLE + OUTER) + item - WHOLE
-
-
-def last_kernel(keep, own, beside, far, *refs):
+def last_kernel(keep, own, beside, middle, *refs):
     sources, refs = refs[:6], refs[6:]
     before, out, following, rounded, square, result, sems, out_sems = refs
     way, layer_kind, row_kind = position()
     part = lax.axis_index("layer") * (own.shape[2] // lax.axis_size("layer")) // LANES
     copies = []
 
-    def bring(source, first, size):
+    def bring(source, first, size, target):
         copies.append(
             pltpu.make_async_copy(
-                source.at[0], following.at[pl.ds(first, size)], sems.at[len(copies)]
+                source.at[0, pl.ds(first, size)],
+                following.at[pl.ds(target, size)],
+                sems.at[len(copies)],
             )
         )
-
-    for group in range(2):
-        pure, near, remote = sources[group * 3 : group * 3 + 3]
-        kind = row_kind if group == 0 else 1 - row_kind
-        bring(pure, (group * 2 + kind) * WHOLE, WHOLE)
-        base = (group * 2 + 1 - kind) * WHOLE
-        bring(near, base + layer_kind * PART, PART)
-        bring(remote, base + (1 - layer_kind) * PART, PART)
-    for copy in copies:
-        copy.start()
+        copies[-1].start()
+
+    for other in range(2):
+        pure, near, far = sources[other * 3 : other * 3 + 3]
+        kind = row_kind if other == 0 else 1 - row_kind
+        bring(pure, 0, WHOLE, (other * 2 + kind) * WHOLE)
+        base = (other * 2 + 1 - kind) * WHOLE
+        bring(near, MIDDLE, PART, base + layer_kind * PART)
+        bring(far, 0, PART, base + (1 - layer_kind) * PART)
+        base = 4 * WHOLE + other * 2 * OUTER
+        bring(near, MIDDLE + PART, OUTER, base + layer_kind * OUTER)
+        bring(far, PART, OUTER, base + (1 - layer_kind) * OUTER)
     for copy in copies:
         copy.wait()
 
@@ -224,7 +234,9 @@
 
     def next_place(slot):
         group, item = divmod(slot - 2 * BAND, FETCHED)
-        return group * WHOLE + item
+        if item < WHOLE:
+            return group * WHOLE + item
+        return 4 * WHOLE + group * OUTER + item - WHOLE - MIDDLE
 
     for column in FRAME:
         total = column_product(left, lambda slot: following[next_place(slot)], column, (2,))
@@ -244,7 +256,7 @@
         elif slot < 2 * BAND:
             array, index = beside, (0, HALF + way * (slot - BAND - HALF))
         elif stage(slot) == 1:
-            array, index = far, (far_place(slot),)
+            array, index = middle, (middle_place(slot),)
         else:
             array, index = following, (next_place(slot),)
         return array[(*index, lanes, slice(None)) if turned else (*index, slice(None), lanes)]
@@ -298,25 +310,29 @@
     return call(first_kernel, "first", shape, [VECTOR] * 2, VECTOR, [], 46, 16)(own, beside)
 
 
-def second(own, far, before):
+def bundle(*arrays):
+    shape = list(arrays[0].shape)
+    shape[1] = sum(array.shape[1] for array in arrays)
+    shape = jax.ShapeDtypeStruct(tuple(shape), arrays[0].dtype)
+    return call(bundle_kernel, "bundle", shape, [VECTOR] * len(arrays), VECTOR, [], 1, 4)(*arrays)
+
+
+def second(own, sources, before):
     block = own.shape[2]
-    shapes = [
-        jax.ShapeDtypeStruct((BAND, block, block), jnp.float32),
-        jax.ShapeDtypeStruct((4 * (MIDDLE + OUTER), block, block), own.dtype),
-    ]
+    shapes = [before, jax.ShapeDtypeStruct((4 * MIDDLE, block, block), own.dtype)]
     return call(
         second_kernel,
         "second",
         shapes,
-        [VECTOR] + [ANYWHERE] * 8 + [VECTOR],
+        [VECTOR] + [ANYWHERE] * 4 + [VECTOR],
         [VECTOR] * 2,
-        [pltpu.SemaphoreType.DMA((8,))],
+        [pltpu.SemaphoreType.DMA((4,))],
         30,
-        24,
-    )(own, *far, before)
-
-
-def last(keep, own, beside, far, following, before):
+        8,
+    )(own, *sources, before)
+
+
+def last(keep, own, beside, middle, sources, before):
     block = own.shape[2]
     shape = jax.ShapeDtypeStruct((1, BAND, block, LANES), jnp.float32)
     return call(
@@ -326,16 +342,16 @@
         [SCALARS] + [VECTOR] * 3 + [ANYWHERE] * 6 + [VECTOR],
         ANYWHERE,
         [
-            pltpu.VMEM((4 * WHOLE, block, block), own.dtype),
+            pltpu.VMEM((4 * (WHOLE + OUTER), block, block), own.dtype),
             pltpu.VMEM((BAND, block, block), own.dtype),
             pltpu.VMEM((BAND, block, LANES), jnp.float32),
             pltpu.VMEM((BAND, block, LANES), jnp.float32),
-            pltpu.SemaphoreType.DMA((6,)),
+            pltpu.SemaphoreType.DMA((10,)),
             pltpu.SemaphoreType.DMA((BAND,)),
         ],
         120,
-        32,
-    )(keep, own, beside, far, *following, before)
+        24,
+    )(keep, own, beside, middle, *sources, before)
 
 
 def after(*arrays):
@@ -368,7 +384,14 @@
         return lax.ppermute(array, axis, [(peer, peer ^ distance) for peer in range(peers)])
 
     swap_cores = lambda array: swap(array, "col", 1)
-    swap_layers = lambda array: swap(array, "layer", 1)
+
+    def swap_layers(array):
+        peers = lax.axis_size("col")
+        pairs = []
+        for peer in range(peers):
+            for plane in range(layers):
+                pairs.append((peer * layers + plane, (peer ^ 1) * layers + (plane ^ 1)))
+        return lax.ppermute(array, ("col", "layer"), pairs)
 
     beside = swap_cores(density)
     diag, middle, outer, pure = pack(density)
@@ -379,23 +402,19 @@
     sums = first(density, beside)
     sums, middle = after(sums, middle)
     far_middle = swap_layers(middle)
-    other_middle = swap_cores(middle)
-    middle, outer = after(middle, outer)
+    far_diag = swap_layers(diag)
+    far_middle, outer = after(far_middle, outer)
     far_outer = swap_layers(outer)
-    other_outer = swap_cores(outer)
-    outer, diag = after(outer, diag)
-    far_diag = swap_layers(diag)
-    other_diag = swap_cores(diag)
-    diag, far_middle, far_outer, pure = after(diag, far_middle, far_outer, pure)
-    other_far_middle = swap_cores(far_middle)
-    other_far_outer = swap_cores(far_outer)
+    near = bundle(middle, diag, outer)
+    other_near = swap_cores(near)
+    far_diag, pure = after(far_diag, pure)
+    own_far_middle = swap_cores(far_middle)
+    sums, middle = second(density, [near, own_far_middle, other_near, far_middle], sums)
     other_pure = swap_cores(pure)
-    far = [middle, far_middle, outer, far_outer]
-    far = far + [other_middle, other_far_middle, other_outer, other_far_outer]
-    sums, far = second(density, far, sums)
-    other_far_diag = swap_cores(far_diag)
-    following = [pure, diag, far_diag, other_pure, other_diag, other_far_diag]
-    out = last(pattern, density, beside, far, following, sums)
+    far = bundle(far_diag, far_outer)
+    own_far = swap_cores(far)
+    sources = [pure, near, own_far, other_pure, other_near, far]
+    out = last(pattern, density, beside, middle, sources, sums)
     if width < LANES:
         layer = lax.axis_index("layer")
         out = lax.dynamic_slice_in_dim(out, layer * width % LANES, width, 3)

time: 67.5 us -> 63.3 us (0.938)
  the two profiles are of different devices: /device:TPU:19 before, /device:TPU:0 now
where the time goes in v4:
time: 63.3 us; the launch traced here: 63.2 us
  waiting for transfers between devices  36.1 us (57%)
  starting transfers between devices  15.5 us (24%)
  Pallas kernels  10 us (16%)
  local copies, waits for them, and re-layouts  1.46 us (2%)
    ppermute x2, waiting for transfers between devices, fetch(): return lax.ppermute(array, axes, pairs)  13.4 us
    ppermute x1, waiting for transfers between devices, fetch_diag(): return lax.ppermute(array, ('row', 'col'), pairs)  10.2 us
    pallas_call x1, Pallas kernels, last(): call(last_kernel, 'last', shape, [SCALARS] + [VECTOR] * 3 + [ANYWHERE] *...  6.74 us
    ppermute x3, waiting for transfers between devices, swap_layers(): return lax.ppermute(array, ('col', 'layer'), pairs)  6.45 us
    ppermute x6, waiting for transfers between devices, swap(): lax.ppermute(array, axis, [(peer, peer ^ distance) for peer in range(peer...  6.08 us
    ppermute x6, starting transfers between devices, swap(): lax.ppermute(array, axis, [(peer, peer ^ distance) for peer in range(peer...  5.86 us
    ppermute x2, starting transfers between devices, fetch(): return lax.ppermute(array, axes, pairs)  5.04 us
    ppermute x3, starting transfers between devices, swap_layers(): return lax.ppermute(array, ('col', 'layer'), pairs)  3.23 us
  transfers between devices with their start and end apart: 12, of which 7 were waited for; matrix products, arithmetic and copies ran while one was open for 0% of the time, Pallas kernels for 5%

profile of v4, /device:TPU:0, one launch (start us, length us, event | category | flops | bytes accessed | tf_op | source)
XLA Modules:
  0.0 63.2 jit_solution(12893774497070641706)
XLA Ops:
  0.0 0.5 collective-permute-start
  0.5 0.0 copy-start
  0.5 1.5 %copy-done = bf16[1,13,256,256]{3,2,1,0:T(8,128)(2,1)S(1)} copy-done((bf16[1,13,256,256]{3,2,1,0:T(8,128)(2,1)S(1)}, bf16[1,13,256,256]{3,2,1,0:T(8,128)(2,1)}, u32[]{:S(2)}) %copy-start) | copy-done | bytes 1703960
  1.9 0.0 copy-start.1
  1.9 0.2 pack.1
  2.1 4.7 %collective-permute-start.1 = (bf16[1,4,256,256]{3,2,1,0:T(8,128)(2,1)S(1)}, bf16[1,4,256,256]{3,2,1,0:T(8,128)(2,1)S(1)}, u32[]{:S(2)}, u32[]{:S(2)}) collective-permute-start(bf16[1,4,256,256]{3,2,1,0:T(8,128)(2,1)S(1)} %get-tuple-element.17), channel_id=1, source_target_pairs={{0,24},{1,9},{2,10},{3,27},{4,28},{5,13},{6,14},{7,31},{8,0},{9,17... | collective-permute-start | bytes 1572872 | tf_op jit(solution)/shard_map/ppermute | solution.py:373
  6.7 1.4 %collective-permute-start.2 = (bf16[1,4,256,256]{3,2,1,0:T(8,128)(2,1)S(1)}, bf16[1,4,256,256]{3,2,1,0:T(8,128)(2,1)S(1)}, u32[]{:S(2)}, u32[]{:S(2)}) collective-permute-start(bf16[1,4,256,256]{3,2,1,0:T(8,128)(2,1)S(1)} %get-tuple-element.19), channel_id=1, source_target_pairs={{0,28},{2,30},{4,8},{6,10},{8,4},{10,6},{12,16},{14,18},{16,12},{1... | collective-permute-start | bytes 1572872 | tf_op jit(solution)/shard_map/ppermute | solution.py:380
  8.1 0.1 collective-permute-start.8
  8.2 0.0 collective-permute-done.beside
  8.2 0.0 copy-done.1
  8.3 1.7 %first.1.before = f32[13,256,256]{2,1,0:T(8,128)S(1)} custom-call(bf16[1,13,256,256]{3,2,1,0:T(8,128)(2,1)S(1)} %copy-done.1, bf16[1,13,256,256]{3,2,1,0:T(8,128)(2,1)S(1)} %collective-permute-done.beside), custom_call_target="tpu_custom_call" | custom-call | flops 1543503872 | bytes 4194304 | tf_op jit(solution)/shard_map/first/pallas_call | solution.py:310
  10.0 11.0 %collective-permute-done.1.refs_0_ = bf16[1,4,256,256]{3,2,1,0:T(8,128)(2,1)S(1)} collective-permute-done((bf16[1,4,256,256]{3,2,1,0:T(8,128)(2,1)S(1)}, bf16[1,4,256,256]{3,2,1,0:T(8,128)(2,1)S(1)}, u32[]{:S(2)}, u32[]{:S(2)}) %collective-permute-start.1) | collective-permute-done | bytes 524320 | tf_op jit(solution)/shard_map/ppermute | solution.py:373
  21.1 0.5 collective-permute-start.3
  21.6 0.4 collective-permute-start.4
  22.0 10.2 %collective-permute-done.2.refs_1_ = bf16[1,4,256,256]{3,2,1,0:T(8,128)(2,1)S(1)} collective-permute-done((bf16[1,4,256,256]{3,2,1,0:T(8,128)(2,1)S(1)}, bf16[1,4,256,256]{3,2,1,0:T(8,128)(2,1)S(1)}, u32[]{:S(2)}, u32[]{:S(2)}) %collective-permute-start.2) | collective-permute-done | bytes 524320 | tf_op jit(solution)/shard_map/ppermute | solution.py:380
  32.1 0.6 %collective-permute-start.7 = (bf16[1,4,256,256]{3,2,1,0:T(8,128)(2,1)S(1)}, bf16[1,4,256,256]{3,2,1,0:T(8,128)(2,1)S(1)}, u32[]{:S(2)}, u32[]{:S(2)}) collective-permute-start(bf16[1,4,256,256]{3,2,1,0:T(8,128)(2,1)S(1)} %collective-permute-done.2.refs_1_), channel_id=1, source_target_pairs={{0,3},{1,2},{2,1},{3,0},{4,7},{5,6},{6,5},{7,4},{8,11},{9,10},{10,... | collective-permute-start | bytes 1572872 | tf_op jit(solution)/shard_map/ppermute | solution.py:394
  32.8 2.3 %collective-permute-done.4.refs_2_ = bf16[1,2,256,256]{3,2,1,0:T(8,128)(2,1)S(1)} collective-permute-done((bf16[1,2,256,256]{3,2,1,0:T(8,128)(2,1)S(1)}, bf16[1,2,256,256]{3,2,1,0:T(8,128)(2,1)S(1)}, u32[]{:S(2)}, u32[]{:S(2)}) %collective-permute-start.4) | collective-permute-done | bytes 262176 | tf_op jit(solution)/shard_map/ppermute | solution.py:373
  35.1 0.0 collective-permute-done.3.other_far
  35.1 0.1 bundle.2.near.refs_1_
  35.2 4.7 %collective-permute-start.6 = (bf16[1,10,256,256]{3,2,1,0:T(8,128)(2,1)S(1)}, bf16[1,10,256,256]{3,2,1,0:T(8,128)(2,1)S(1)}, u32[]{:S(2)}, u32[]{:S(2)}) collective-permute-start(bf16[1,10,256,256]{3,2,1,0:T(8,128)(2,1)S(1)} %bundle.2.near.refs_1_), channel_id=1, source_target_pairs={{0,2},{2,0},{4,6},{6,4},{1,3},{3,1},{5,7},{7,5},{8,10},{10,8},{12,... | collective-permute-start | bytes 3932168 | tf_op jit(solution)/shard_map/ppermute | solution.py:384
  39.9 2.0 %collective-permute-start.9 = (bf16[1,2,256,256]{3,2,1,0:T(8,128)(2,1)S(1)}, bf16[1,2,256,256]{3,2,1,0:T(8,128)(2,1)S(1)}, u32[]{:S(2)}, u32[]{:S(2)}) collective-permute-start(bf16[1,2,256,256]{3,2,1,0:T(8,128)(2,1)S(1)} %collective-permute-done.4.refs_2_), channel_id=1, source_target_pairs={{0,3},{1,2},{2,1},{3,0},{4,7},{5,6},{6,5},{7,4},{8,11},{9,10},{10,... | collective-permute-start | bytes 786440 | tf_op jit(solution)/shard_map/ppermute | solution.py:394
  42.0 4.4 %collective-permute-done.7.refs_0_ = bf16[1,4,256,256]{3,2,1,0:T(8,128)(2,1)S(1)} collective-permute-done((bf16[1,4,256,256]{3,2,1,0:T(8,128)(2,1)S(1)}, bf16[1,4,256,256]{3,2,1,0:T(8,128)(2,1)S(1)}, u32[]{:S(2)}, u32[]{:S(2)}) %collective-permute-start.7) | collective-permute-done | bytes 524320 | tf_op jit(solution)/shard_map/ppermute | solution.py:394
  46.4 3.5 %collective-permute-done.8.refs_0_ = bf16[1,8,256,256]{3,2,1,0:T(8,128)(2,1)S(1)} collective-permute-done((bf16[1,8,256,256]{3,2,1,0:T(8,128)(2,1)S(1)}, bf16[1,8,256,256]{3,2,1,0:T(8,128)(2,1)S(1)}, u32[]{:S(2)}, u32[]{:S(2)}) %collective-permute-start.8) | collective-permute-done | bytes 1048608 | tf_op jit(solution)/shard_map/ppermute | solution.py:384
  49.9 0.0 collective-permute-start.11
  49.9 2.1 %collective-permute-done.9.refs_1_ = bf16[1,2,256,256]{3,2,1,0:T(8,128)(2,1)S(1)} collective-permute-done((bf16[1,2,256,256]{3,2,1,0:T(8,128)(2,1)S(1)}, bf16[1,2,256,256]{3,2,1,0:T(8,128)(2,1)S(1)}, u32[]{:S(2)}, u32[]{:S(2)}) %collective-permute-start.9) | collective-permute-done | bytes 262176 | tf_op jit(solution)/shard_map/ppermute | solution.py:394
  52.0 0.1 bundle.3.refs_5_
  52.0 0.0 copy-start.2
  52.0 0.2 collective-permute-start.10
  52.2 0.4 collective-permute-start.5
  52.6 2.5 %collective-permute-done.5.far = bf16[1,4,256,256]{3,2,1,0:T(8,128)(2,1)S(1)} collective-permute-done((bf16[1,4,256,256]{3,2,1,0:T(8,128)(2,1)S(1)}, bf16[1,4,256,256]{3,2,1,0:T(8,128)(2,1)S(1)}, u32[]{:S(2)}, u32[]{:S(2)}) %collective-permute-start.5) | collective-permute-done | bytes 524320 | tf_op jit(solution)/shard_map/ppermute | solution.py:384
  55.1 0.0 collective-permute-done.6.other_near.refs_4_
  55.1 1.3 %second.1 = (f32[13,256,256]{2,1,0:T(8,128)S(1)}, bf16[16,256,256]{2,1,0:T(8,128)(2,1)S(1)}) custom-call(bf16[1,13,256,256]{3,2,1,0:T(8,128)(2,1)S(1)} %copy-done.1, bf16[1,10,256,256]{3,2,1,0:T(8,128)(2,1)S(1)} %bundle.2.near.refs_1_, bf16[1,4,256,256]{3,2,1,0:T(8,128)(2,1)S(1)} %collective-permute-done.5.far, ...), custom_call_target="tpu_custom_call" | custom-call | flops 1006632960 | bytes 4194304 | tf_op jit(solution)/shard_map/second/pallas_call | solution.py:323
  56.4 0.0 collective-permute-done.11.refs_3_
  56.4 0.0 collective-permute-done.10.refs_2_
  56.4 0.0 copy-done.2
  56.4 6.7 %last.1 = f32[1,13,256,128]{3,2,1,0:T(8,128)} custom-call(s32[1,13]{1,0:T(1,128)S(1)} %copy-done.2, bf16[1,13,256,256]{3,2,1,0:T(8,128)(2,1)S(1)} %copy-done.1, bf16[1,13,256,256]{3,2,1,0:T(8,128)(2,1)S(1)} %collective-permute-done.beside, bf16[16,256,256]{2,1,0:T(8,128)(2,1)S(1)} %get-tuple-element.24.middle, ...), custom_call_target="tpu_custom_call" | custom-call | flops 4026531840 | bytes 4194304 | tf_op jit(solution)/shard_map/last/pallas_call | solution.py:338
Async XLA Ops:
  0.0 8.2 %collective-permute-start = (bf16[1,13,256,256]{3,2,1,0:T(8,128)(2,1)}, bf16[1,13,256,256]{3,2,1,0:T(8,128)(2,1)S(1)}, u32[]{:S(2)}, u32[]{:S(2)}) collective-permute-start(bf16[1,13,256,256]{3,2,1,0:T(8,128)(2,1)} %own.5), channel_id=1, source_target_pairs={{0,2},{2,0},{4,6},{6,4},{1,3},{3,1},{5,7},{7,5},{8,10},{10,8},{12,... | collective-permute-start | bytes 5111816 | tf_op jit(solution)/shard_map/ppermute | solution.py:384
  0.5 1.5 %copy-start = (bf16[1,13,256,256]{3,2,1,0:T(8,128)(2,1)S(1)}, bf16[1,13,256,256]{3,2,1,0:T(8,128)(2,1)}, u32[]{:S(2)}) copy-start(bf16[1,13,256,256]{3,2,1,0:T(8,128)(2,1)} %own.5) | copy-start | bytes 5111812
  1.9 6.3 %copy-start.1 = (bf16[1,13,256,256]{3,2,1,0:T(8,128)(2,1)S(1)}, bf16[1,13,256,256]{3,2,1,0:T(8,128)(2,1)}, u32[]{:S(2)}) copy-start(bf16[1,13,256,256]{3,2,1,0:T(8,128)(2,1)} %own.5) | copy-start | bytes 5111812
  2.1 19.0 %collective-permute-start.1 = (bf16[1,4,256,256]{3,2,1,0:T(8,128)(2,1)S(1)}, bf16[1,4,256,256]{3,2,1,0:T(8,128)(2,1)S(1)}, u32[]{:S(2)}, u32[]{:S(2)}) collective-permute-start(bf16[1,4,256,256]{3,2,1,0:T(8,128)(2,1)S(1)} %get-tuple-element.17), channel_id=1, source_target_pairs={{0,24},{1,9},{2,10},{3,27},{4,28},{5,13},{6,14},{7,31},{8,0},{9,17... | collective-permute-start | bytes 1572872 | tf_op jit(solution)/shard_map/ppermute | solution.py:373
  6.7 25.4 %collective-permute-start.2 = (bf16[1,4,256,256]{3,2,1,0:T(8,128)(2,1)S(1)}, bf16[1,4,256,256]{3,2,1,0:T(8,128)(2,1)S(1)}, u32[]{:S(2)}, u32[]{:S(2)}) collective-permute-start(bf16[1,4,256,256]{3,2,1,0:T(8,128)(2,1)S(1)} %get-tuple-element.19), channel_id=1, source_target_pairs={{0,28},{2,30},{4,8},{6,10},{8,4},{10,6},{12,16},{14,18},{16,12},{1... | collective-permute-start | bytes 1572872 | tf_op jit(solution)/shard_map/ppermute | solution.py:380
  8.1 41.8 %collective-permute-start.8 = (bf16[1,8,256,256]{3,2,1,0:T(8,128)(2,1)S(1)}, bf16[1,8,256,256]{3,2,1,0:T(8,128)(2,1)S(1)}, u32[]{:S(2)}, u32[]{:S(2)}) collective-permute-start(bf16[1,8,256,256]{3,2,1,0:T(8,128)(2,1)S(1)} %get-tuple-element.25), channel_id=1, source_target_pairs={{0,4},{2,6},{4,0},{6,2},{1,5},{3,7},{5,1},{7,3},{8,12},{10,14},{12... | collective-permute-start | bytes 3145736 | tf_op jit(solution)/shard_map/ppermute | solution.py:384
  21.1 14.1 %collective-permute-start.3 = (bf16[1,4,256,256]{3,2,1,0:T(8,128)(2,1)S(1)}, bf16[1,4,256,256]{3,2,1,0:T(8,128)(2,1)S(1)}, u32[]{:S(2)}, u32[]{:S(2)}) collective-permute-start(bf16[1,4,256,256]{3,2,1,0:T(8,128)(2,1)S(1)} %collective-permute-done.1.refs_0_), channel_id=1, source_target_pairs={{0,3},{1,2},{2,1},{3,0},{4,7},{5,6},{6,5},{7,4},{8,11},{9,10},{10,... | collective-permute-start | bytes 1572872 | tf_op jit(solution)/shard_map/ppermute | solution.py:394
  21.6 13.5 %collective-permute-start.4 = (bf16[1,2,256,256]{3,2,1,0:T(8,128)(2,1)S(1)}, bf16[1,2,256,256]{3,2,1,0:T(8,128)(2,1)S(1)}, u32[]{:S(2)}, u32[]{:S(2)}) collective-permute-start(bf16[1,2,256,256]{3,2,1,0:T(8,128)(2,1)S(1)} %get-tuple-element.20), channel_id=1, source_target_pairs={{0,20},{1,13},{2,14},{3,23},{4,24},{5,17},{6,18},{7,27},{8,28},{9,... | collective-permute-start | bytes 786440 | tf_op jit(solution)/shard_map/ppermute | solution.py:373
  32.1 14.2 %collective-permute-start.7 = (bf16[1,4,256,256]{3,2,1,0:T(8,128)(2,1)S(1)}, bf16[1,4,256,256]{3,2,1,0:T(8,128)(2,1)S(1)}, u32[]{:S(2)}, u32[]{:S(2)}) collective-permute-start(bf16[1,4,256,256]{3,2,1,0:T(8,128)(2,1)S(1)} %collective-permute-done.2.refs_1_), channel_id=1, source_target_pairs={{0,3},{1,2},{2,1},{3,0},{4,7},{5,6},{6,5},{7,4},{8,11},{9,10},{10,... | collective-permute-start | bytes 1572872 | tf_op jit(solution)/shard_map/ppermute | solution.py:394
  35.2 19.9 %collective-permute-start.6 = (bf16[1,10,256,256]{3,2,1,0:T(8,128)(2,1)S(1)}, bf16[1,10,256,256]{3,2,1,0:T(8,128)(2,1)S(1)}, u32[]{:S(2)}, u32[]{:S(2)}) collective-permute-start(bf16[1,10,256,256]{3,2,1,0:T(8,128)(2,1)S(1)} %bundle.2.near.refs_1_), channel_id=1, source_target_pairs={{0,2},{2,0},{4,6},{6,4},{1,3},{3,1},{5,7},{7,5},{8,10},{10,8},{12,... | collective-permute-start | bytes 3932168 | tf_op jit(solution)/shard_map/ppermute | solution.py:384
  39.9 12.1 %collective-permute-start.9 = (bf16[1,2,256,256]{3,2,1,0:T(8,128)(2,1)S(1)}, bf16[1,2,256,256]{3,2,1,0:T(8,128)(2,1)S(1)}, u32[]{:S(2)}, u32[]{:S(2)}) collective-permute-start(bf16[1,2,256,256]{3,2,1,0:T(8,128)(2,1)S(1)} %collective-permute-done.4.refs_2_), channel_id=1, source_target_pairs={{0,3},{1,2},{2,1},{3,0},{4,7},{5,6},{6,5},{7,4},{8,11},{9,10},{10,... | collective-permute-start | bytes 786440 | tf_op jit(solution)/shard_map/ppermute | solution.py:394
  49.9 6.5 %collective-permute-start.11 = (bf16[1,8,256,256]{3,2,1,0:T(8,128)(2,1)S(1)}, bf16[1,8,256,256]{3,2,1,0:T(8,128)(2,1)S(1)}, u32[]{:S(2)}, u32[]{:S(2)}) collective-permute-start(bf16[1,8,256,256]{3,2,1,0:T(8,128)(2,1)S(1)} %collective-permute-done.8.refs_0_), channel_id=1, source_target_pairs={{0,2},{2,0},{4,6},{6,4},{1,3},{3,1},{5,7},{7,5},{8,10},{10,8},{12,... | collective-permute-start | bytes 3145736 | tf_op jit(solution)/shard_map/ppermute | solution.py:384
  52.0 4.4 %copy-start.2 = (s32[1,13]{1,0:T(1,128)S(1)}, s32[1,13]{1,0:T(1,128)}, u32[]{:S(2)}) copy-start(s32[1,13]{1,0:T(1,128)} %keep.1) | copy-start | bytes 160
  52.0 4.4 %collective-permute-start.10 = (bf16[1,6,256,256]{3,2,1,0:T(8,128)(2,1)S(1)}, bf16[1,6,256,256]{3,2,1,0:T(8,128)(2,1)S(1)}, u32[]{:S(2)}, u32[]{:S(2)}) collective-permute-start(bf16[1,6,256,256]{3,2,1,0:T(8,128)(2,1)S(1)} %bundle.3.refs_5_), channel_id=1, source_target_pairs={{0,2},{2,0},{4,6},{6,4},{1,3},{3,1},{5,7},{7,5},{8,10},{10,8},{12,... | collective-permute-start | bytes 2359304 | tf_op jit(solution)/shard_map/ppermute | solution.py:384
  52.2 2.9 %collective-permute-start.5 = (bf16[1,4,256,256]{3,2,1,0:T(8,128)(2,1)S(1)}, bf16[1,4,256,256]{3,2,1,0:T(8,128)(2,1)S(1)}, u32[]{:S(2)}, u32[]{:S(2)}) collective-permute-start(bf16[1,4,256,256]{3,2,1,0:T(8,128)(2,1)S(1)} %collective-permute-done.3.other_far), channel_id=1, source_target_pairs={{0,2},{2,0},{4,6},{6,4},{1,3},{3,1},{5,7},{7,5},{8,10},{10,8},{12,... | collective-permute-start | bytes 1572872 | tf_op jit(solution)/shard_map/ppermute | solution.py:384

commit v5 on v4

--- a/solution.py
+++ b/solution.py
@@ -43,10 +43,13 @@
 def stage(slot):
     if slot < 2 * BAND:
         return 0
-    return 1 if WHOLE <= (slot - 2 * BAND) % FETCHED < WHOLE + MIDDLE else 2
-
-
-def terms(column, stages=(0, 1, 2)):
+    group, item = divmod(slot - 2 * BAND, FETCHED)
+    if item < WHOLE:
+        return 2 if group in (0, 3) else 3
+    return 1 if item < WHOLE + MIDDLE else 4
+
+
+def terms(column, stages=(0, 1, 2, 3, 4)):
     plain = {}
     turned = {}
     for row in FRAME:
@@ -200,9 +203,25 @@
         sums[column + HALF] = before[column + HALF] + (0.0 if total is None else total)
 
 
+def third_kernel(own, pure, other_pure, before, sums):
+    way, layer_kind, row_kind = position()
+    left = frame_row(way, own)
+    for kind in (0, 1):
+
+        def block(slot):
+            place, item = divmod(slot - 2 * BAND, FETCHED)
+            return other_pure[0, item] if place >= 2 else pure[0, item]
+
+        @pl.when(row_kind == kind)
+        def _():
+            for column in FRAME:
+                total = column_product(left, block, column, (2 + kind,))
+                sums[column + HALF] = before[column + HALF] + (0.0 if total is None else total)
+
+
 def last_kernel(keep, own, beside, middle, *refs):
     sources, refs = refs[:6], refs[6:]
-    before, out, following, rounded, square, result, sems, out_sems = refs
+    before, out, following, sums, rounded, square, result, sems, out_sems = refs
     way, layer_kind, row_kind = position()
     part = lax.axis_index("layer") * (own.shape[2] // lax.axis_size("layer")) // LANES
     copies = []
@@ -238,9 +257,17 @@
             return group * WHOLE + item
         return 4 * WHOLE + group * OUTER + item - WHOLE - MIDDLE
 
+    for kind in (0, 1):
+
+        @pl.when(row_kind == kind)
+        def _():
+            block = lambda slot: following[next_place(slot)]
+            for column in FRAME:
+                total = column_product(left, block, column, (3 - kind, 4))
+                sums[column + HALF] = before[column + HALF] + (0.0 if total is None else total)
+
     for column in FRAME:
-        total = column_product(left, lambda slot: following[next_place(slot)], column, (2,))
-        total = before[column + HALF] + (0.0 if total is None else total)
+        total = sums[column + HALF]
         total = total * keep[0, HALF + way * column].astype(jnp.float32)
         rounded[column + HALF] = total.astype(jnp.bfloat16)
         mine = total[:, :LANES]
@@ -332,6 +359,12 @@
     )(own, *sources, before)
 
 
+def third(own, pure, other_pure, before):
+    return call(third_kernel, "third", before, [VECTOR] * 4, VECTOR, [], 30, 8)(
+        own, pure, other_pure, before
+    )
+
+
 def last(keep, own, beside, middle, sources, before):
     block = own.shape[2]
     shape = jax.ShapeDtypeStruct((1, BAND, block, LANES), jnp.float32)
@@ -343,6 +376,7 @@
         ANYWHERE,
         [
             pltpu.VMEM((4 * (WHOLE + OUTER), block, block), own.dtype),
+            pltpu.VMEM((BAND, block, block), jnp.float32),
             pltpu.VMEM((BAND, block, block), own.dtype),
             pltpu.VMEM((BAND, block, LANES), jnp.float32),
             pltpu.VMEM((BAND, block, LANES), jnp.float32),
@@ -407,10 +441,11 @@
     far_outer = swap_layers(outer)
     near = bundle(middle, diag, outer)
     other_near = swap_cores(near)
-    far_diag, pure = after(far_diag, pure)
-    own_far_middle = swap_cores(far_middle)
+    own_far_middle = swap_cores(bundle(far_middle, far_middle))
     sums, middle = second(density, [near, own_far_middle, other_near, far_middle], sums)
+    far_outer, far_diag, pure = after(far_outer, far_diag, pure)
     other_pure = swap_cores(pure)
+    sums = third(density, pure, other_pure, sums)
     far = bundle(far_diag, far_outer)
     own_far = swap_cores(far)
     sources = [pure, near, own_far, other_pure, other_near, far]

time: 63.3 us -> 62 us (0.979)
  waiting for transfers between devices: 36.1 us -> 34.1 us
    ppermute x6, waiting for transfers between devices: 6.08 us -> 4.34 us  [swap(): lax.ppermute(array, axis, [(peer, peer ^ distance) for peer in range(peer...]
    pallas_call x0 -> x1, Pallas kernels: none -> 1.09 us  [third(): call(third_kernel, 'third', before, [VECTOR] * 4, VECTOR, [], 30, 8)]
  transfers between devices with their start and end apart: 12 -> 12, of which waited for: 7 -> 7; matrix products, arithmetic and copies ran while one was open for 0% -> 0% of each run, Pallas kernels for 5% -> 7%
where the time goes in v5:
time: 62 us; the launch traced here: 61.9 us
  waiting for transfers between devices  34.1 us (55%)
  starting transfers between devices  15.7 us (25%)
  Pallas kernels  10.6 us (17%)
  local copies, waits for them, and re-layouts  1.46 us (2%)
    ppermute x2, waiting for transfers between devices, fetch(): return lax.ppermute(array, axes, pairs)  13.4 us
    ppermute x1, waiting for transfers between devices, fetch_diag(): return lax.ppermute(array, ('row', 'col'), pairs)  10.2 us
    ppermute x3, waiting for transfers between devices, swap_layers(): return lax.ppermute(array, ('col', 'layer'), pairs)  6.25 us
    pallas_call x1, Pallas kernels, last(): call(last_kernel, 'last', shape, [SCALARS] + [VECTOR] * 3 + [ANYWHERE] *...  6.14 us
    ppermute x6, starting transfers between devices, swap(): lax.ppermute(array, axis, [(peer, peer ^ distance) for peer in range(peer...  5.99 us
    ppermute x2, starting transfers between devices, fetch(): return lax.ppermute(array, axes, pairs)  5.04 us
    ppermute x6, waiting for transfers between devices, swap(): lax.ppermute(array, axis, [(peer, peer ^ distance) for peer in range(peer...  4.34 us
    ppermute x3, starting transfers between devices, swap_layers(): return lax.ppermute(array, ('col', 'layer'), pairs)  3.23 us
  transfers between devices with their start and end apart: 12, of which 7 were waited for; matrix products, arithmetic and copies ran while one was open for 0% of the time, Pallas kernels for 7%

profile of v5, /device:TPU:0, one launch (start us, length us, event | category | flops | bytes accessed | tf_op | source)
XLA Modules:
  0.0 61.9 jit_solution(17388225631297166776)
XLA Ops:
  0.0 0.5 collective-permute-start
  0.5 0.0 copy-start
  0.5 1.5 %copy-done = bf16[1,13,256,256]{3,2,1,0:T(8,128)(2,1)S(1)} copy-done((bf16[1,13,256,256]{3,2,1,0:T(8,128)(2,1)S(1)}, bf16[1,13,256,256]{3,2,1,0:T(8,128)(2,1)}, u32[]{:S(2)}) %copy-start) | copy-done | bytes 1703960
  1.9 0.0 copy-start.1
  1.9 0.2 pack.1
  2.1 4.7 %collective-permute-start.1 = (bf16[1,4,256,256]{3,2,1,0:T(8,128)(2,1)S(1)}, bf16[1,4,256,256]{3,2,1,0:T(8,128)(2,1)S(1)}, u32[]{:S(2)}, u32[]{:S(2)}) collective-permute-start(bf16[1,4,256,256]{3,2,1,0:T(8,128)(2,1)S(1)} %get-tuple-element.18), channel_id=1, source_target_pairs={{0,24},{1,9},{2,10},{3,27},{4,28},{5,13},{6,14},{7,31},{8,0},{9,17... | collective-permute-start | bytes 1572872 | tf_op jit(solution)/shard_map/ppermute | solution.py:407
  6.7 1.4 %collective-permute-start.2 = (bf16[1,4,256,256]{3,2,1,0:T(8,128)(2,1)S(1)}, bf16[1,4,256,256]{3,2,1,0:T(8,128)(2,1)S(1)}, u32[]{:S(2)}, u32[]{:S(2)}) collective-permute-start(bf16[1,4,256,256]{3,2,1,0:T(8,128)(2,1)S(1)} %get-tuple-element.20), channel_id=1, source_target_pairs={{0,28},{2,30},{4,8},{6,10},{8,4},{10,6},{12,16},{14,18},{16,12},{1... | collective-permute-start | bytes 1572872 | tf_op jit(solution)/shard_map/ppermute | solution.py:414
  8.1 0.1 collective-permute-start.9
  8.2 0.0 collective-permute-done.beside
  8.2 0.0 copy-done.1
  8.3 1.7 %first.1.before = f32[13,256,256]{2,1,0:T(8,128)S(1)} custom-call(bf16[1,13,256,256]{3,2,1,0:T(8,128)(2,1)S(1)} %copy-done.1, bf16[1,13,256,256]{3,2,1,0:T(8,128)(2,1)S(1)} %collective-permute-done.beside), custom_call_target="tpu_custom_call" | custom-call | flops 1543503872 | bytes 4194304 | tf_op jit(solution)/shard_map/first/pallas_call | solution.py:337
  10.0 11.1 %collective-permute-done.1.refs_0_ = bf16[1,4,256,256]{3,2,1,0:T(8,128)(2,1)S(1)} collective-permute-done((bf16[1,4,256,256]{3,2,1,0:T(8,128)(2,1)S(1)}, bf16[1,4,256,256]{3,2,1,0:T(8,128)(2,1)S(1)}, u32[]{:S(2)}, u32[]{:S(2)}) %collective-permute-start.1) | collective-permute-done | bytes 524320 | tf_op jit(solution)/shard_map/ppermute | solution.py:407
  21.1 0.5 collective-permute-start.3
  21.6 0.4 collective-permute-start.4
  22.0 10.2 %collective-permute-done.2.refs_1_ = bf16[1,4,256,256]{3,2,1,0:T(8,128)(2,1)S(1)} collective-permute-done((bf16[1,4,256,256]{3,2,1,0:T(8,128)(2,1)S(1)}, bf16[1,4,256,256]{3,2,1,0:T(8,128)(2,1)S(1)}, u32[]{:S(2)}, u32[]{:S(2)}) %collective-permute-start.2) | collective-permute-done | bytes 524320 | tf_op jit(solution)/shard_map/ppermute | solution.py:414
  32.1 0.6 %collective-permute-start.8 = (bf16[1,4,256,256]{3,2,1,0:T(8,128)(2,1)S(1)}, bf16[1,4,256,256]{3,2,1,0:T(8,128)(2,1)S(1)}, u32[]{:S(2)}, u32[]{:S(2)}) collective-permute-start(bf16[1,4,256,256]{3,2,1,0:T(8,128)(2,1)S(1)} %collective-permute-done.2.refs_1_), channel_id=1, source_target_pairs={{0,3},{1,2},{2,1},{3,0},{4,7},{5,6},{6,5},{7,4},{8,11},{9,10},{10,... | collective-permute-start | bytes 1572872 | tf_op jit(solution)/shard_map/ppermute | solution.py:428
  32.8 2.3 %collective-permute-done.4.refs_2_ = bf16[1,2,256,256]{3,2,1,0:T(8,128)(2,1)S(1)} collective-permute-done((bf16[1,2,256,256]{3,2,1,0:T(8,128)(2,1)S(1)}, bf16[1,2,256,256]{3,2,1,0:T(8,128)(2,1)S(1)}, u32[]{:S(2)}, u32[]{:S(2)}) %collective-permute-start.4) | collective-permute-done | bytes 262176 | tf_op jit(solution)/shard_map/ppermute | solution.py:407
  35.1 0.0 collective-permute-done.3.refs_0_.refs_1_.other_far
  35.1 0.1 bundle.3.near.refs_1_
  35.2 4.7 %collective-permute-start.6 = (bf16[1,10,256,256]{3,2,1,0:T(8,128)(2,1)S(1)}, bf16[1,10,256,256]{3,2,1,0:T(8,128)(2,1)S(1)}, u32[]{:S(2)}, u32[]{:S(2)}) collective-permute-start(bf16[1,10,256,256]{3,2,1,0:T(8,128)(2,1)S(1)} %bundle.3.near.refs_1_), channel_id=1, source_target_pairs={{0,2},{2,0},{4,6},{6,4},{1,3},{3,1},{5,7},{7,5},{8,10},{10,8},{12,... | collective-permute-start | bytes 3932168 | tf_op jit(solution)/shard_map/ppermute | solution.py:418
  39.9 2.0 %collective-permute-start.7 = (bf16[1,2,256,256]{3,2,1,0:T(8,128)(2,1)S(1)}, bf16[1,2,256,256]{3,2,1,0:T(8,128)(2,1)S(1)}, u32[]{:S(2)}, u32[]{:S(2)}) collective-permute-start(bf16[1,2,256,256]{3,2,1,0:T(8,128)(2,1)S(1)} %collective-permute-done.4.refs_2_), channel_id=1, source_target_pairs={{0,3},{1,2},{2,1},{3,0},{4,7},{5,6},{6,5},{7,4},{8,11},{9,10},{10,... | collective-permute-start | bytes 786440 | tf_op jit(solution)/shard_map/ppermute | solution.py:428
  42.0 0.1 bundle.4
  42.0 0.1 collective-permute-start.5
  42.2 4.2 %collective-permute-done.8.refs_0_ = bf16[1,4,256,256]{3,2,1,0:T(8,128)(2,1)S(1)} collective-permute-done((bf16[1,4,256,256]{3,2,1,0:T(8,128)(2,1)S(1)}, bf16[1,4,256,256]{3,2,1,0:T(8,128)(2,1)S(1)}, u32[]{:S(2)}, u32[]{:S(2)}) %collective-permute-start.8) | collective-permute-done | bytes 524320 | tf_op jit(solution)/shard_map/ppermute | solution.py:428
  46.4 3.5 %collective-permute-done.9.pure.refs_0_ = bf16[1,8,256,256]{3,2,1,0:T(8,128)(2,1)S(1)} collective-permute-done((bf16[1,8,256,256]{3,2,1,0:T(8,128)(2,1)S(1)}, bf16[1,8,256,256]{3,2,1,0:T(8,128)(2,1)S(1)}, u32[]{:S(2)}, u32[]{:S(2)}) %collective-permute-start.9) | collective-permute-done | bytes 1048608 | tf_op jit(solution)/shard_map/ppermute | solution.py:418
  49.9 2.1 %collective-permute-done.7.refs_1_ = bf16[1,2,256,256]{3,2,1,0:T(8,128)(2,1)S(1)} collective-permute-done((bf16[1,2,256,256]{3,2,1,0:T(8,128)(2,1)S(1)}, bf16[1,2,256,256]{3,2,1,0:T(8,128)(2,1)S(1)}, u32[]{:S(2)}, u32[]{:S(2)}) %collective-permute-start.7) | collective-permute-done | bytes 262176 | tf_op jit(solution)/shard_map/ppermute | solution.py:428
  52.0 0.1 collective-permute-start.11
  52.1 0.1 bundle.5.refs_5_
  52.1 0.5 collective-permute-start.10
  52.6 0.0 collective-permute-done.5.far
  52.6 0.0 collective-permute-done.6.other_near.refs_4_
  52.6 1.3 %second.1 = (f32[13,256,256]{2,1,0:T(8,128)S(1)}, bf16[16,256,256]{2,1,0:T(8,128)(2,1)S(1)}) custom-call(bf16[1,13,256,256]{3,2,1,0:T(8,128)(2,1)S(1)} %copy-done.1, bf16[1,10,256,256]{3,2,1,0:T(8,128)(2,1)S(1)} %bundle.3.near.refs_1_, bf16[1,8,256,256]{3,2,1,0:T(8,128)(2,1)S(1)} %collective-permute-done.5.far, ...), custom_call_target="tpu_custom_call" | custom-call | flops 1006632960 | bytes 4194304 | tf_op jit(solution)/shard_map/second/pallas_call | solution.py:350
  53.9 0.8 %collective-permute-done.11.other_pure.refs_3_ = bf16[1,8,256,256]{3,2,1,0:T(8,128)(2,1)S(1)} collective-permute-done((bf16[1,8,256,256]{3,2,1,0:T(8,128)(2,1)S(1)}, bf16[1,8,256,256]{3,2,1,0:T(8,128)(2,1)S(1)}, u32[]{:S(2)}, u32[]{:S(2)}) %collective-permute-start.11) | collective-permute-done | bytes 1048608 | tf_op jit(solution)/shard_map/ppermute | solution.py:418
  54.6 0.0 copy-start.2
  54.6 1.1 %third.1.refs_6_ = f32[13,256,256]{2,1,0:T(8,128)S(1)} custom-call(bf16[1,13,256,256]{3,2,1,0:T(8,128)(2,1)S(1)} %copy-done.1, bf16[1,8,256,256]{3,2,1,0:T(8,128)(2,1)S(1)} %collective-permute-done.9.pure.refs_0_, bf16[1,8,256,256]{3,2,1,0:T(8,128)(2,1)S(1)} %collective-permute-done.11.other_pure.refs_3_, f32[13,256,256]{2,1,0:T(8,128)S(1)} %get-tuple-element.30.before), custom_call_target="tpu_custom_call" | custom-call | flops 1006632960 | bytes 4194304 | tf_op jit(solution)/shard_map/third/pallas_call | solution.py:363
  55.7 0.0 collective-permute-done.10.refs_2_
  55.8 0.0 copy-done.2
  55.8 6.1 %last.1 = f32[1,13,256,128]{3,2,1,0:T(8,128)} custom-call(s32[1,13]{1,0:T(1,128)S(1)} %copy-done.2, bf16[1,13,256,256]{3,2,1,0:T(8,128)(2,1)S(1)} %copy-done.1, bf16[1,13,256,256]{3,2,1,0:T(8,128)(2,1)S(1)} %collective-permute-done.beside, bf16[16,256,256]{2,1,0:T(8,128)(2,1)S(1)} %get-tuple-element.25.middle, ...), custom_call_target="tpu_custom_call" | custom-call | flops 4026531840 | bytes 4194304 | tf_op jit(solution)/shard_map/last/pallas_call | solution.py:371
Async XLA Ops:
  0.0 8.2 %collective-permute-start = (bf16[1,13,256,256]{3,2,1,0:T(8,128)(2,1)}, bf16[1,13,256,256]{3,2,1,0:T(8,128)(2,1)S(1)}, u32[]{:S(2)}, u32[]{:S(2)}) collective-permute-start(bf16[1,13,256,256]{3,2,1,0:T(8,128)(2,1)} %own.7), channel_id=1, source_target_pairs={{0,2},{2,0},{4,6},{6,4},{1,3},{3,1},{5,7},{7,5},{8,10},{10,8},{12,... | collective-permute-start | bytes 5111816 | tf_op jit(solution)/shard_map/ppermute | solution.py:418
  0.5 1.5 %copy-start = (bf16[1,13,256,256]{3,2,1,0:T(8,128)(2,1)S(1)}, bf16[1,13,256,256]{3,2,1,0:T(8,128)(2,1)}, u32[]{:S(2)}) copy-start(bf16[1,13,256,256]{3,2,1,0:T(8,128)(2,1)} %own.7) | copy-start | bytes 5111812
  1.9 6.3 %copy-start.1 = (bf16[1,13,256,256]{3,2,1,0:T(8,128)(2,1)S(1)}, bf16[1,13,256,256]{3,2,1,0:T(8,128)(2,1)}, u32[]{:S(2)}) copy-start(bf16[1,13,256,256]{3,2,1,0:T(8,128)(2,1)} %own.7) | copy-start | bytes 5111812
  2.1 19.0 %collective-permute-start.1 = (bf16[1,4,256,256]{3,2,1,0:T(8,128)(2,1)S(1)}, bf16[1,4,256,256]{3,2,1,0:T(8,128)(2,1)S(1)}, u32[]{:S(2)}, u32[]{:S(2)}) collective-permute-start(bf16[1,4,256,256]{3,2,1,0:T(8,128)(2,1)S(1)} %get-tuple-element.18), channel_id=1, source_target_pairs={{0,24},{1,9},{2,10},{3,27},{4,28},{5,13},{6,14},{7,31},{8,0},{9,17... | collective-permute-start | bytes 1572872 | tf_op jit(solution)/shard_map/ppermute | solution.py:407
  6.7 25.4 %collective-permute-start.2 = (bf16[1,4,256,256]{3,2,1,0:T(8,128)(2,1)S(1)}, bf16[1,4,256,256]{3,2,1,0:T(8,128)(2,1)S(1)}, u32[]{:S(2)}, u32[]{:S(2)}) collective-permute-start(bf16[1,4,256,256]{3,2,1,0:T(8,128)(2,1)S(1)} %get-tuple-element.20), channel_id=1, source_target_pairs={{0,28},{2,30},{4,8},{6,10},{8,4},{10,6},{12,16},{14,18},{16,12},{1... | collective-permute-start | bytes 1572872 | tf_op jit(solution)/shard_map/ppermute | solution.py:414
  8.1 41.8 %collective-permute-start.9 = (bf16[1,8,256,256]{3,2,1,0:T(8,128)(2,1)S(1)}, bf16[1,8,256,256]{3,2,1,0:T(8,128)(2,1)S(1)}, u32[]{:S(2)}, u32[]{:S(2)}) collective-permute-start(bf16[1,8,256,256]{3,2,1,0:T(8,128)(2,1)S(1)} %get-tuple-element.26), channel_id=1, source_target_pairs={{0,4},{2,6},{4,0},{6,2},{1,5},{3,7},{5,1},{7,3},{8,12},{10,14},{12... | collective-permute-start | bytes 3145736 | tf_op jit(solution)/shard_map/ppermute | solution.py:418
  21.1 14.1 %collective-permute-start.3 = (bf16[1,4,256,256]{3,2,1,0:T(8,128)(2,1)S(1)}, bf16[1,4,256,256]{3,2,1,0:T(8,128)(2,1)S(1)}, u32[]{:S(2)}, u32[]{:S(2)}) collective-permute-start(bf16[1,4,256,256]{3,2,1,0:T(8,128)(2,1)S(1)} %collective-permute-done.1.refs_0_), channel_id=1, source_target_pairs={{0,3},{1,2},{2,1},{3,0},{4,7},{5,6},{6,5},{7,4},{8,11},{9,10},{10,... | collective-permute-start | bytes 1572872 | tf_op jit(solution)/shard_map/ppermute | solution.py:428
  21.6 13.5 %collective-permute-start.4 = (bf16[1,2,256,256]{3,2,1,0:T(8,128)(2,1)S(1)}, bf16[1,2,256,256]{3,2,1,0:T(8,128)(2,1)S(1)}, u32[]{:S(2)}, u32[]{:S(2)}) collective-permute-start(bf16[1,2,256,256]{3,2,1,0:T(8,128)(2,1)S(1)} %get-tuple-element.21), channel_id=1, source_target_pairs={{0,20},{1,13},{2,14},{3,23},{4,24},{5,17},{6,18},{7,27},{8,28},{9,... | collective-permute-start | bytes 786440 | tf_op jit(solution)/shard_map/ppermute | solution.py:407
  32.1 14.2 %collective-permute-start.8 = (bf16[1,4,256,256]{3,2,1,0:T(8,128)(2,1)S(1)}, bf16[1,4,256,256]{3,2,1,0:T(8,128)(2,1)S(1)}, u32[]{:S(2)}, u32[]{:S(2)}) collective-permute-start(bf16[1,4,256,256]{3,2,1,0:T(8,128)(2,1)S(1)} %collective-permute-done.2.refs_1_), channel_id=1, source_target_pairs={{0,3},{1,2},{2,1},{3,0},{4,7},{5,6},{6,5},{7,4},{8,11},{9,10},{10,... | collective-permute-start | bytes 1572872 | tf_op jit(solution)/shard_map/ppermute | solution.py:428
  35.2 17.4 %collective-permute-start.6 = (bf16[1,10,256,256]{3,2,1,0:T(8,128)(2,1)S(1)}, bf16[1,10,256,256]{3,2,1,0:T(8,128)(2,1)S(1)}, u32[]{:S(2)}, u32[]{:S(2)}) collective-permute-start(bf16[1,10,256,256]{3,2,1,0:T(8,128)(2,1)S(1)} %bundle.3.near.refs_1_), channel_id=1, source_target_pairs={{0,2},{2,0},{4,6},{6,4},{1,3},{3,1},{5,7},{7,5},{8,10},{10,8},{12,... | collective-permute-start | bytes 3932168 | tf_op jit(solution)/shard_map/ppermute | solution.py:418
  39.9 12.1 %collective-permute-start.7 = (bf16[1,2,256,256]{3,2,1,0:T(8,128)(2,1)S(1)}, bf16[1,2,256,256]{3,2,1,0:T(8,128)(2,1)S(1)}, u32[]{:S(2)}, u32[]{:S(2)}) collective-permute-start(bf16[1,2,256,256]{3,2,1,0:T(8,128)(2,1)S(1)} %collective-permute-done.4.refs_2_), channel_id=1, source_target_pairs={{0,3},{1,2},{2,1},{3,0},{4,7},{5,6},{6,5},{7,4},{8,11},{9,10},{10,... | collective-permute-start | bytes 786440 | tf_op jit(solution)/shard_map/ppermute | solution.py:428
  42.0 10.6 %collective-permute-start.5 = (bf16[1,8,256,256]{3,2,1,0:T(8,128)(2,1)S(1)}, bf16[1,8,256,256]{3,2,1,0:T(8,128)(2,1)S(1)}, u32[]{:S(2)}, u32[]{:S(2)}) collective-permute-start(bf16[1,8,256,256]{3,2,1,0:T(8,128)(2,1)S(1)} %bundle.4), channel_id=1, source_target_pairs={{0,2},{2,0},{4,6},{6,4},{1,3},{3,1},{5,7},{7,5},{8,10},{10,8},{12,... | collective-permute-start | bytes 3145736 | tf_op jit(solution)/shard_map/ppermute | solution.py:418
  52.0 2.7 %collective-permute-start.11 = (bf16[1,8,256,256]{3,2,1,0:T(8,128)(2,1)S(1)}, bf16[1,8,256,256]{3,2,1,0:T(8,128)(2,1)S(1)}, u32[]{:S(2)}, u32[]{:S(2)}) collective-permute-start(bf16[1,8,256,256]{3,2,1,0:T(8,128)(2,1)S(1)} %collective-permute-done.9.pure.refs_0_), channel_id=1, source_target_pairs={{0,2},{2,0},{4,6},{6,4},{1,3},{3,1},{5,7},{7,5},{8,10},{10,8},{12,... | collective-permute-start | bytes 3145736 | tf_op jit(solution)/shard_map/ppermute | solution.py:418
  52.1 3.6 %collective-permute-start.10 = (bf16[1,6,256,256]{3,2,1,0:T(8,128)(2,1)S(1)}, bf16[1,6,256,256]{3,2,1,0:T(8,128)(2,1)S(1)}, u32[]{:S(2)}, u32[]{:S(2)}) collective-permute-start(bf16[1,6,256,256]{3,2,1,0:T(8,128)(2,1)S(1)} %bundle.5.refs_5_), channel_id=1, source_target_pairs={{0,2},{2,0},{4,6},{6,4},{1,3},{3,1},{5,7},{7,5},{8,10},{10,8},{12,... | collective-permute-start | bytes 2359304 | tf_op jit(solution)/shard_map/ppermute | solution.py:418
  54.6 1.1 %copy-start.2 = (s32[1,13]{1,0:T(1,128)S(1)}, s32[1,13]{1,0:T(1,128)}, u32[]{:S(2)}) copy-start(s32[1,13]{1,0:T(1,128)} %keep.1) | copy-start | bytes 160

commit v6 on v5

--- a/solution.py
+++ b/solution.py
@@ -11,7 +11,10 @@
 BACKWARD = ((0, 1, 2, 3, 4, -4, -5, -6), (0, 1, 2, -6), (0, 0))
 SIZES = tuple(len(part) for part in FORWARD)
 WHOLE, MIDDLE, OUTER = SIZES
-PART = WHOLE // 2
+LEFT_OUT = 6
+PARTS = ((0, 1, 2), (3, 4, 5, 7))
+PART = len(PARTS[1])
+SENT = len(PARTS[0])
 STARTS = (0, WHOLE, WHOLE + MIDDLE)
 FETCHED = sum(SIZES)
 LANES = 128
@@ -143,8 +146,9 @@
         out[0, item] = density[0, index]
 
     for item in range(PART):
-        forward = jnp.where(layer_kind == 0, FORWARD[0][item], FORWARD[0][PART + item])
-        backward = jnp.where(layer_kind == 0, BACKWARD[0][item], BACKWARD[0][PART + item])
+        one, other = PARTS[0][min(item, SENT - 1)], PARTS[1][item]
+        forward = jnp.where(layer_kind == 0, FORWARD[0][one], FORWARD[0][other])
+        backward = jnp.where(layer_kind == 0, BACKWARD[0][one], BACKWARD[0][other])
         bring(diag, item, forward, backward, row_kind)
     for out, step in ((middle, 1), (outer, 2)):
         for item in range(SIZES[step]):
@@ -178,6 +182,25 @@
         for item in range(array.shape[1]):
             out[0, place] = array[0, item]
             place += 1
+
+
+def swap_kernel(diag, out):
+    for item in range(SENT):
+        out[0, item] = diag[0, item]
+
+
+def rest_kernel(diag, outer, out):
+    way, layer_kind, row_kind = position()
+
+    @pl.when(layer_kind == 0)
+    def _():
+        for item in range(OUTER):
+            out[0, item] = outer[0, item]
+
+    @pl.when(layer_kind == 1)
+    def _():
+        out[0, 0] = diag[0, SENT]
+        out[0, 1] = outer[0, 0]
 
 
 def second_kernel(own, near, far, other_near, other_far, before, sums, held, sems):
@@ -203,8 +226,9 @@
         sums[column + HALF] = before[column + HALF] + (0.0 if total is None else total)
 
 
-def third_kernel(own, pure, other_pure, before, sums):
-    way, layer_kind, row_kind = position()
+def third_kernel(own, pure, other_pure, before, sums, turned):
+    way, layer_kind, row_kind = position()
+    turned[0] = other_pure[0, LEFT_OUT].T
     left = frame_row(way, own)
     for kind in (0, 1):
 
@@ -221,33 +245,31 @@
 
 def last_kernel(keep, own, beside, middle, *refs):
     sources, refs = refs[:6], refs[6:]
-    before, out, following, sums, rounded, square, result, sems, out_sems = refs
+    turned, before, out, following, rounded, square, result, out_sems = refs
     way, layer_kind, row_kind = position()
     part = lax.axis_index("layer") * (own.shape[2] // lax.axis_size("layer")) // LANES
-    copies = []
 
     def bring(source, first, size, target):
-        copies.append(
-            pltpu.make_async_copy(
-                source.at[0, pl.ds(first, size)],
-                following.at[pl.ds(target, size)],
-                sems.at[len(copies)],
-            )
-        )
-        copies[-1].start()
+        for item in range(size):
+            following[target + item] = source[0, first + item]
 
     for other in range(2):
         pure, near, far = sources[other * 3 : other * 3 + 3]
         kind = row_kind if other == 0 else 1 - row_kind
         bring(pure, 0, WHOLE, (other * 2 + kind) * WHOLE)
         base = (other * 2 + 1 - kind) * WHOLE
-        bring(near, MIDDLE, PART, base + layer_kind * PART)
-        bring(far, 0, PART, base + (1 - layer_kind) * PART)
-        base = 4 * WHOLE + other * 2 * OUTER
-        bring(near, MIDDLE + PART, OUTER, base + layer_kind * OUTER)
-        bring(far, PART, OUTER, base + (1 - layer_kind) * OUTER)
-    for copy in copies:
-        copy.wait()
+        last_item = base + PARTS[1][-1]
+        ends = (4 * WHOLE + other * 2 * OUTER, 4 * WHOLE + (other * 2 + 1) * OUTER)
+        even = layer_kind == 0
+        spare = 4 * (WHOLE + OUTER) + other
+        bring(near, MIDDLE, SENT, base + layer_kind * SENT)
+        bring(far, 0, SENT, base + (1 - layer_kind) * SENT)
+        following[jnp.where(even, spare, last_item)] = near[0, MIDDLE + SENT]
+        for item in range(OUTER):
+            following[jnp.where(even, *ends) + item] = near[0, MIDDLE + PART + item]
+        following[jnp.where(even, last_item, ends[0])] = far[0, SENT]
+        following[jnp.where(even, ends[1], ends[0] + 1)] = far[0, SENT + 1]
+    following[(1 - row_kind) * WHOLE + LEFT_OUT] = turned[0]
 
     left = frame_row(way, own)
 
@@ -264,16 +286,14 @@
             block = lambda slot: following[next_place(slot)]
             for column in FRAME:
                 total = column_product(left, block, column, (3 - kind, 4))
-                sums[column + HALF] = before[column + HALF] + (0.0 if total is None else total)
-
-    for column in FRAME:
-        total = sums[column + HALF]
-        total = total * keep[0, HALF + way * column].astype(jnp.float32)
-        rounded[column + HALF] = total.astype(jnp.bfloat16)
-        mine = total[:, :LANES]
-        for piece in range(1, total.shape[1] // LANES):
-            mine = jnp.where(part == piece, total[:, piece * LANES : (piece + 1) * LANES], mine)
-        square[column + HALF] = mine
+                total = before[column + HALF] + (0.0 if total is None else total)
+                total = total * keep[0, HALF + way * column].astype(jnp.float32)
+                rounded[column + HALF] = total.astype(jnp.bfloat16)
+                mine = total[:, :LANES]
+                for piece in range(1, total.shape[1] // LANES):
+                    lanes = slice(piece * LANES, (piece + 1) * LANES)
+                    mine = jnp.where(part == piece, total[:, lanes], mine)
+                square[column + HALF] = mine
 
     lanes = pl.ds(pl.multiple_of(part * LANES, LANES), LANES)
 
@@ -344,6 +364,13 @@
     return call(bundle_kernel, "bundle", shape, [VECTOR] * len(arrays), VECTOR, [], 1, 4)(*arrays)
 
 
+def cut(kernel, size, *arrays):
+    shape = list(arrays[0].shape)
+    shape[1] = size
+    shape = jax.ShapeDtypeStruct(tuple(shape), arrays[0].dtype)
+    return call(kernel, "cut", shape, [VECTOR] * len(arrays), VECTOR, [], 1, 4)(*arrays)
+
+
 def second(own, sources, before):
     block = own.shape[2]
     shapes = [before, jax.ShapeDtypeStruct((4 * MIDDLE, block, block), own.dtype)]
@@ -360,32 +387,32 @@
 
 
 def third(own, pure, other_pure, before):
-    return call(third_kernel, "third", before, [VECTOR] * 4, VECTOR, [], 30, 8)(
+    block = own.shape[2]
+    shapes = [before, jax.ShapeDtypeStruct((1, block, block), own.dtype)]
+    return call(third_kernel, "third", shapes, [VECTOR] * 4, [VECTOR] * 2, [], 30, 8)(
         own, pure, other_pure, before
     )
 
 
-def last(keep, own, beside, middle, sources, before):
+def last(keep, own, beside, middle, sources, turned, before):
     block = own.shape[2]
     shape = jax.ShapeDtypeStruct((1, BAND, block, LANES), jnp.float32)
     return call(
         last_kernel,
         "last",
         shape,
-        [SCALARS] + [VECTOR] * 3 + [ANYWHERE] * 6 + [VECTOR],
+        [SCALARS] + [VECTOR] * 11,
         ANYWHERE,
         [
-            pltpu.VMEM((4 * (WHOLE + OUTER), block, block), own.dtype),
-            pltpu.VMEM((BAND, block, block), jnp.float32),
+            pltpu.VMEM((4 * (WHOLE + OUTER) + 2, block, block), own.dtype),
             pltpu.VMEM((BAND, block, block), own.dtype),
             pltpu.VMEM((BAND, block, LANES), jnp.float32),
             pltpu.VMEM((BAND, block, LANES), jnp.float32),
-            pltpu.SemaphoreType.DMA((10,)),
             pltpu.SemaphoreType.DMA((BAND,)),
         ],
         120,
         24,
-    )(keep, own, beside, middle, *sources, before)
+    )(keep, own, beside, middle, *sources, turned, before)
 
 
 def after(*arrays):
@@ -436,20 +463,20 @@
     sums = first(density, beside)
     sums, middle = after(sums, middle)
     far_middle = swap_layers(middle)
-    far_diag = swap_layers(diag)
+    far_diag = swap_layers(cut(swap_kernel, SENT, diag))
     far_middle, outer = after(far_middle, outer)
-    far_outer = swap_layers(outer)
+    far_outer = swap_layers(cut(rest_kernel, OUTER, diag, outer))
     near = bundle(middle, diag, outer)
     other_near = swap_cores(near)
     own_far_middle = swap_cores(bundle(far_middle, far_middle))
     sums, middle = second(density, [near, own_far_middle, other_near, far_middle], sums)
     far_outer, far_diag, pure = after(far_outer, far_diag, pure)
     other_pure = swap_cores(pure)
-    sums = third(density, pure, other_pure, sums)
+    sums, turned = third(density, pure, other_pure, sums)
     far = bundle(far_diag, far_outer)
     own_far = swap_cores(far)
     sources = [pure, near, own_far, other_pure, other_near, far]
-    out = last(pattern, density, beside, middle, sources, sums)
+    out = last(pattern, density, beside, middle, sources, turned, sums)
     if width < LANES:
         layer = lax.axis_index("layer")
         out = lax.dynamic_slice_in_dim(out, layer * width % LANES, width, 3)

time: 62 us -> 60.3 us (0.973)
  the two profiles are of different devices: /device:TPU:0 before, /device:TPU:13 now
where the time goes in v6:
time: 60.3 us; the launch traced here: 60.2 us
  starting transfers between devices  25.2 us (42%)
  waiting for transfers between devices  22.8 us (38%)
  Pallas kernels  10.6 us (18%)
  local copies, waits for them, and re-layouts  1.46 us (2%)
    ppermute x2, waiting for transfers between devices, fetch(): return lax.ppermute(array, axes, pairs)  11.1 us
    ppermute x2, starting transfers between devices, fetch(): return lax.ppermute(array, axes, pairs)  9.6 us
    ppermute x3, starting transfers between devices, swap_layers(): return lax.ppermute(array, ('col', 'layer'), pairs)  7.64 us
    pallas_call x1, Pallas kernels, last(): call(last_kernel, 'last', shape, [SCALARS] + [VECTOR] * 11, ANYWHERE, [pl...  5.99 us
    ppermute x6, starting transfers between devices, swap(): lax.ppermute(array, axis, [(peer, peer ^ distance) for peer in range(peer...  5.71 us
    ppermute x3, waiting for transfers between devices, swap_layers(): return lax.ppermute(array, ('col', 'layer'), pairs)  5.18 us
    ppermute x6, waiting for transfers between devices, swap(): lax.ppermute(array, axis, [(peer, peer ^ distance) for peer in range(peer...  4.37 us
    ppermute x1, starting transfers between devices, fetch_diag(): return lax.ppermute(array, ('row', 'col'), pairs)  2.25 us
  transfers between devices with their start and end apart: 12, of which 7 were waited for; matrix products, arithmetic and copies ran while one was open for 0% of the time, Pallas kernels for 8%

profile of v6, /device:TPU:13, one launch (start us, length us, event | category | flops | bytes accessed | tf_op | source)
XLA Modules:
  0.0 60.2 jit_solution(3881601037825446843)
XLA Ops:
  0.0 0.7 %collective-permute-start = (bf16[1,13,256,256]{3,2,1,0:T(8,128)(2,1)}, bf16[1,13,256,256]{3,2,1,0:T(8,128)(2,1)S(1)}, u32[]{:S(2)}, u32[]{:S(2)}) collective-permute-start(bf16[1,13,256,256]{3,2,1,0:T(8,128)(2,1)} %own.7), channel_id=1, source_target_pairs={{0,2},{2,0},{4,6},{6,4},{1,3},{3,1},{5,7},{7,5},{8,10},{10,8},{12,... | collective-permute-start | bytes 5111816 | tf_op jit(solution)/shard_map/ppermute | solution.py:445
  0.7 0.0 copy-start
  0.7 1.5 %copy-done = bf16[1,13,256,256]{3,2,1,0:T(8,128)(2,1)S(1)} copy-done((bf16[1,13,256,256]{3,2,1,0:T(8,128)(2,1)S(1)}, bf16[1,13,256,256]{3,2,1,0:T(8,128)(2,1)}, u32[]{:S(2)}) %copy-start) | copy-done | bytes 1703960
  2.1 0.0 copy-start.1
  2.1 0.2 pack.1
  2.3 1.3 %collective-permute-start.1 = (bf16[1,4,256,256]{3,2,1,0:T(8,128)(2,1)S(1)}, bf16[1,4,256,256]{3,2,1,0:T(8,128)(2,1)S(1)}, u32[]{:S(2)}, u32[]{:S(2)}) collective-permute-start(bf16[1,4,256,256]{3,2,1,0:T(8,128)(2,1)S(1)} %get-tuple-element.20), channel_id=1, source_target_pairs={{0,24},{1,9},{2,10},{3,27},{4,28},{5,13},{6,14},{7,31},{8,0},{9,17... | collective-permute-start | bytes 1572872 | tf_op jit(solution)/shard_map/ppermute | solution.py:434
  3.6 0.2 collective-permute-start.9
  3.9 2.3 %collective-permute-start.2 = (bf16[1,4,256,256]{3,2,1,0:T(8,128)(2,1)S(1)}, bf16[1,4,256,256]{3,2,1,0:T(8,128)(2,1)S(1)}, u32[]{:S(2)}, u32[]{:S(2)}) collective-permute-start(bf16[1,4,256,256]{3,2,1,0:T(8,128)(2,1)S(1)} %get-tuple-element.22), channel_id=1, source_target_pairs={{0,28},{2,30},{4,8},{6,10},{8,4},{10,6},{12,16},{14,18},{16,12},{1... | collective-permute-start | bytes 1572872 | tf_op jit(solution)/shard_map/ppermute | solution.py:441
  6.1 0.0 collective-permute-done.beside
  6.1 0.0 copy-done.1
  6.1 1.7 %first.1.before = f32[13,256,256]{2,1,0:T(8,128)S(1)} custom-call(bf16[1,13,256,256]{3,2,1,0:T(8,128)(2,1)S(1)} %copy-done.1, bf16[1,13,256,256]{3,2,1,0:T(8,128)(2,1)S(1)} %collective-permute-done.beside), custom_call_target="tpu_custom_call" | custom-call | flops 1543503872 | bytes 4194304 | tf_op jit(solution)/shard_map/first/pallas_call | solution.py:357
  7.9 10.5 %collective-permute-done.1.refs_0_ = bf16[1,4,256,256]{3,2,1,0:T(8,128)(2,1)S(1)} collective-permute-done((bf16[1,4,256,256]{3,2,1,0:T(8,128)(2,1)S(1)}, bf16[1,4,256,256]{3,2,1,0:T(8,128)(2,1)S(1)}, u32[]{:S(2)}, u32[]{:S(2)}) %collective-permute-start.1) | collective-permute-done | bytes 524320 | tf_op jit(solution)/shard_map/ppermute | solution.py:434
  18.4 3.7 %collective-permute-start.3 = (bf16[1,4,256,256]{3,2,1,0:T(8,128)(2,1)S(1)}, bf16[1,4,256,256]{3,2,1,0:T(8,128)(2,1)S(1)}, u32[]{:S(2)}, u32[]{:S(2)}) collective-permute-start(bf16[1,4,256,256]{3,2,1,0:T(8,128)(2,1)S(1)} %collective-permute-done.1.refs_0_), channel_id=1, source_target_pairs={{0,3},{1,2},{2,1},{3,0},{4,7},{5,6},{6,5},{7,4},{8,11},{9,10},{10,... | collective-permute-start | bytes 1572872 | tf_op jit(solution)/shard_map/ppermute | solution.py:455
  22.1 8.3 %collective-permute-start.4 = (bf16[1,2,256,256]{3,2,1,0:T(8,128)(2,1)S(1)}, bf16[1,2,256,256]{3,2,1,0:T(8,128)(2,1)S(1)}, u32[]{:S(2)}, u32[]{:S(2)}) collective-permute-start(bf16[1,2,256,256]{3,2,1,0:T(8,128)(2,1)S(1)} %get-tuple-element.23), channel_id=1, source_target_pairs={{0,20},{1,13},{2,14},{3,23},{4,24},{5,17},{6,18},{7,27},{8,28},{9,... | collective-permute-start | bytes 786440 | tf_op jit(solution)/shard_map/ppermute | solution.py:434
  30.3 2.2 %collective-permute-done.2.refs_1_.diag = bf16[1,4,256,256]{3,2,1,0:T(8,128)(2,1)S(1)} collective-permute-done((bf16[1,4,256,256]{3,2,1,0:T(8,128)(2,1)S(1)}, bf16[1,4,256,256]{3,2,1,0:T(8,128)(2,1)S(1)}, u32[]{:S(2)}, u32[]{:S(2)}) %collective-permute-start.2) | collective-permute-done | bytes 524320 | tf_op jit(solution)/shard_map/ppermute | solution.py:441
  32.5 2.2 %collective-permute-start.8 = (bf16[1,3,256,256]{3,2,1,0:T(8,128)(2,1)S(1)}, bf16[1,3,256,256]{3,2,1,0:T(8,128)(2,1)S(1)}, u32[]{:S(2)}, u32[]{:S(2)}) collective-permute-start(bf16[1,3,256,256]{3,2,1,0:T(8,128)(2,1)S(1)} %cut.3), channel_id=1, source_target_pairs={{0,3},{1,2},{2,1},{3,0},{4,7},{5,6},{6,5},{7,4},{8,11},{9,10},{10,... | collective-permute-start | bytes 1179656 | tf_op jit(solution)/shard_map/ppermute | solution.py:455
  34.7 0.6 collective-permute-done.4.refs_2_.outer
  35.3 0.0 collective-permute-done.3.refs_0_.refs_1_.other_far
  35.3 0.1 bundle.3.near.refs_1_
  35.4 1.3 %collective-permute-start.6 = (bf16[1,10,256,256]{3,2,1,0:T(8,128)(2,1)S(1)}, bf16[1,10,256,256]{3,2,1,0:T(8,128)(2,1)S(1)}, u32[]{:S(2)}, u32[]{:S(2)}) collective-permute-start(bf16[1,10,256,256]{3,2,1,0:T(8,128)(2,1)S(1)} %bundle.3.near.refs_1_), channel_id=1, source_target_pairs={{0,2},{2,0},{4,6},{6,4},{1,3},{3,1},{5,7},{7,5},{8,10},{10,8},{12,... | collective-permute-start | bytes 3932168 | tf_op jit(solution)/shard_map/ppermute | solution.py:445
  36.7 1.8 %collective-permute-start.7 = (bf16[1,2,256,256]{3,2,1,0:T(8,128)(2,1)S(1)}, bf16[1,2,256,256]{3,2,1,0:T(8,128)(2,1)S(1)}, u32[]{:S(2)}, u32[]{:S(2)}) collective-permute-start(bf16[1,2,256,256]{3,2,1,0:T(8,128)(2,1)S(1)} %cut.2), channel_id=1, source_target_pairs={{0,3},{1,2},{2,1},{3,0},{4,7},{5,6},{6,5},{7,4},{8,11},{9,10},{10,... | collective-permute-start | bytes 786440 | tf_op jit(solution)/shard_map/ppermute | solution.py:455
  38.5 0.1 bundle.4
  38.6 0.1 collective-permute-start.5
  38.7 3.1 %collective-permute-done.8.refs_0_ = bf16[1,3,256,256]{3,2,1,0:T(8,128)(2,1)S(1)} collective-permute-done((bf16[1,3,256,256]{3,2,1,0:T(8,128)(2,1)S(1)}, bf16[1,3,256,256]{3,2,1,0:T(8,128)(2,1)S(1)}, u32[]{:S(2)}, u32[]{:S(2)}) %collective-permute-start.8) | collective-permute-done | bytes 393248 | tf_op jit(solution)/shard_map/ppermute | solution.py:455
  41.8 3.5 %collective-permute-done.9.pure.refs_0_ = bf16[1,8,256,256]{3,2,1,0:T(8,128)(2,1)S(1)} collective-permute-done((bf16[1,8,256,256]{3,2,1,0:T(8,128)(2,1)S(1)}, bf16[1,8,256,256]{3,2,1,0:T(8,128)(2,1)S(1)}, u32[]{:S(2)}, u32[]{:S(2)}) %collective-permute-start.9) | collective-permute-done | bytes 1048608 | tf_op jit(solution)/shard_map/ppermute | solution.py:445
  45.3 2.1 %collective-permute-done.7.refs_1_ = bf16[1,2,256,256]{3,2,1,0:T(8,128)(2,1)S(1)} collective-permute-done((bf16[1,2,256,256]{3,2,1,0:T(8,128)(2,1)S(1)}, bf16[1,2,256,256]{3,2,1,0:T(8,128)(2,1)S(1)}, u32[]{:S(2)}, u32[]{:S(2)}) %collective-permute-start.7) | collective-permute-done | bytes 262176 | tf_op jit(solution)/shard_map/ppermute | solution.py:455
  47.4 3.3 %collective-permute-start.11 = (bf16[1,8,256,256]{3,2,1,0:T(8,128)(2,1)S(1)}, bf16[1,8,256,256]{3,2,1,0:T(8,128)(2,1)S(1)}, u32[]{:S(2)}, u32[]{:S(2)}) collective-permute-start(bf16[1,8,256,256]{3,2,1,0:T(8,128)(2,1)S(1)} %collective-permute-done.9.pure.refs_0_), channel_id=1, source_target_pairs={{0,2},{2,0},{4,6},{6,4},{1,3},{3,1},{5,7},{7,5},{8,10},{10,8},{12,... | collective-permute-start | bytes 3145736 | tf_op jit(solution)/shard_map/ppermute | solution.py:445
  50.8 0.1 collective-permute-start.10
  50.8 0.0 collective-permute-done.5.far
  50.8 0.0 collective-permute-done.6.other_near.refs_4_
  50.9 1.3 %second.1 = (f32[13,256,256]{2,1,0:T(8,128)S(1)}, bf16[16,256,256]{2,1,0:T(8,128)(2,1)S(1)}) custom-call(bf16[1,13,256,256]{3,2,1,0:T(8,128)(2,1)S(1)} %copy-done.1, bf16[1,10,256,256]{3,2,1,0:T(8,128)(2,1)S(1)} %bundle.3.near.refs_1_, bf16[1,8,256,256]{3,2,1,0:T(8,128)(2,1)S(1)} %collective-permute-done.5.far, ...), custom_call_target="tpu_custom_call" | custom-call | flops 1006632960 | bytes 4194304 | tf_op jit(solution)/shard_map/second/pallas_call | solution.py:377
  52.2 0.8 %collective-permute-done.11.other_pure.refs_3_ = bf16[1,8,256,256]{3,2,1,0:T(8,128)(2,1)S(1)} collective-permute-done((bf16[1,8,256,256]{3,2,1,0:T(8,128)(2,1)S(1)}, bf16[1,8,256,256]{3,2,1,0:T(8,128)(2,1)S(1)}, u32[]{:S(2)}, u32[]{:S(2)}) %collective-permute-start.11) | collective-permute-done | bytes 1048608 | tf_op jit(solution)/shard_map/ppermute | solution.py:445
  53.0 0.0 copy-start.2
  53.0 1.2 %third.1 = (f32[13,256,256]{2,1,0:T(8,128)S(1)}, bf16[1,256,256]{2,1,0:T(8,128)(2,1)S(1)}) custom-call(bf16[1,13,256,256]{3,2,1,0:T(8,128)(2,1)S(1)} %copy-done.1, bf16[1,8,256,256]{3,2,1,0:T(8,128)(2,1)S(1)} %collective-permute-done.9.pure.refs_0_, bf16[1,8,256,256]{3,2,1,0:T(8,128)(2,1)S(1)} %collective-permute-done.11.other_pure.refs_3_, ...), custom_call_target="tpu_custom_call" | custom-call | flops 1006632960 | bytes 4194304 | tf_op jit(solution)/shard_map/third/pallas_call | solution.py:392
  54.2 0.0 collective-permute-done.10.refs_2_
  54.2 0.0 copy-done.2
  54.2 6.0 %last.1 = f32[1,13,256,128]{3,2,1,0:T(8,128)} custom-call(s32[1,13]{1,0:T(1,128)S(1)} %copy-done.2, bf16[1,13,256,256]{3,2,1,0:T(8,128)(2,1)S(1)} %copy-done.1, bf16[1,13,256,256]{3,2,1,0:T(8,128)(2,1)S(1)} %collective-permute-done.beside, bf16[16,256,256]{2,1,0:T(8,128)(2,1)S(1)} %get-tuple-element.27.middle, ...), custom_call_target="tpu_custom_call" | custom-call | flops 4026531840 | bytes 4194304 | tf_op jit(solution)/shard_map/last/pallas_call | solution.py:400
  (3 shorter events, 0.1 us)
Async XLA Ops:
  0.0 6.1 %collective-permute-start = (bf16[1,13,256,256]{3,2,1,0:T(8,128)(2,1)}, bf16[1,13,256,256]{3,2,1,0:T(8,128)(2,1)S(1)}, u32[]{:S(2)}, u32[]{:S(2)}) collective-permute-start(bf16[1,13,256,256]{3,2,1,0:T(8,128)(2,1)} %own.7), channel_id=1, source_target_pairs={{0,2},{2,0},{4,6},{6,4},{1,3},{3,1},{5,7},{7,5},{8,10},{10,8},{12,... | collective-permute-start | bytes 5111816 | tf_op jit(solution)/shard_map/ppermute | solution.py:445
  0.7 1.5 %copy-start = (bf16[1,13,256,256]{3,2,1,0:T(8,128)(2,1)S(1)}, bf16[1,13,256,256]{3,2,1,0:T(8,128)(2,1)}, u32[]{:S(2)}) copy-start(bf16[1,13,256,256]{3,2,1,0:T(8,128)(2,1)} %own.7) | copy-start | bytes 5111812
  2.1 4.0 %copy-start.1 = (bf16[1,13,256,256]{3,2,1,0:T(8,128)(2,1)S(1)}, bf16[1,13,256,256]{3,2,1,0:T(8,128)(2,1)}, u32[]{:S(2)}) copy-start(bf16[1,13,256,256]{3,2,1,0:T(8,128)(2,1)} %own.7) | copy-start | bytes 5111812
  2.3 16.1 %collective-permute-start.1 = (bf16[1,4,256,256]{3,2,1,0:T(8,128)(2,1)S(1)}, bf16[1,4,256,256]{3,2,1,0:T(8,128)(2,1)S(1)}, u32[]{:S(2)}, u32[]{:S(2)}) collective-permute-start(bf16[1,4,256,256]{3,2,1,0:T(8,128)(2,1)S(1)} %get-tuple-element.20), channel_id=1, source_target_pairs={{0,24},{1,9},{2,10},{3,27},{4,28},{5,13},{6,14},{7,31},{8,0},{9,17... | collective-permute-start | bytes 1572872 | tf_op jit(solution)/shard_map/ppermute | solution.py:434
  3.6 41.6 %collective-permute-start.9 = (bf16[1,8,256,256]{3,2,1,0:T(8,128)(2,1)S(1)}, bf16[1,8,256,256]{3,2,1,0:T(8,128)(2,1)S(1)}, u32[]{:S(2)}, u32[]{:S(2)}) collective-permute-start(bf16[1,8,256,256]{3,2,1,0:T(8,128)(2,1)S(1)} %get-tuple-element.28), channel_id=1, source_target_pairs={{0,4},{2,6},{4,0},{6,2},{1,5},{3,7},{5,1},{7,3},{8,12},{10,14},{12... | collective-permute-start | bytes 3145736 | tf_op jit(solution)/shard_map/ppermute | solution.py:445
  3.9 28.6 %collective-permute-start.2 = (bf16[1,4,256,256]{3,2,1,0:T(8,128)(2,1)S(1)}, bf16[1,4,256,256]{3,2,1,0:T(8,128)(2,1)S(1)}, u32[]{:S(2)}, u32[]{:S(2)}) collective-permute-start(bf16[1,4,256,256]{3,2,1,0:T(8,128)(2,1)S(1)} %get-tuple-element.22), channel_id=1, source_target_pairs={{0,28},{2,30},{4,8},{6,10},{8,4},{10,6},{12,16},{14,18},{16,12},{1... | collective-permute-start | bytes 1572872 | tf_op jit(solution)/shard_map/ppermute | solution.py:441
  18.4 16.9 %collective-permute-start.3 = (bf16[1,4,256,256]{3,2,1,0:T(8,128)(2,1)S(1)}, bf16[1,4,256,256]{3,2,1,0:T(8,128)(2,1)S(1)}, u32[]{:S(2)}, u32[]{:S(2)}) collective-permute-start(bf16[1,4,256,256]{3,2,1,0:T(8,128)(2,1)S(1)} %collective-permute-done.1.refs_0_), channel_id=1, source_target_pairs={{0,3},{1,2},{2,1},{3,0},{4,7},{5,6},{6,5},{7,4},{8,11},{9,10},{10,... | collective-permute-start | bytes 1572872 | tf_op jit(solution)/shard_map/ppermute | solution.py:455
  22.1 13.2 %collective-permute-start.4 = (bf16[1,2,256,256]{3,2,1,0:T(8,128)(2,1)S(1)}, bf16[1,2,256,256]{3,2,1,0:T(8,128)(2,1)S(1)}, u32[]{:S(2)}, u32[]{:S(2)}) collective-permute-start(bf16[1,2,256,256]{3,2,1,0:T(8,128)(2,1)S(1)} %get-tuple-element.23), channel_id=1, source_target_pairs={{0,20},{1,13},{2,14},{3,23},{4,24},{5,17},{6,18},{7,27},{8,28},{9,... | collective-permute-start | bytes 786440 | tf_op jit(solution)/shard_map/ppermute | solution.py:434
  32.5 9.3 %collective-permute-start.8 = (bf16[1,3,256,256]{3,2,1,0:T(8,128)(2,1)S(1)}, bf16[1,3,256,256]{3,2,1,0:T(8,128)(2,1)S(1)}, u32[]{:S(2)}, u32[]{:S(2)}) collective-permute-start(bf16[1,3,256,256]{3,2,1,0:T(8,128)(2,1)S(1)} %cut.3), channel_id=1, source_target_pairs={{0,3},{1,2},{2,1},{3,0},{4,7},{5,6},{6,5},{7,4},{8,11},{9,10},{10,... | collective-permute-start | bytes 1179656 | tf_op jit(solution)/shard_map/ppermute | solution.py:455
  35.4 15.4 %collective-permute-start.6 = (bf16[1,10,256,256]{3,2,1,0:T(8,128)(2,1)S(1)}, bf16[1,10,256,256]{3,2,1,0:T(8,128)(2,1)S(1)}, u32[]{:S(2)}, u32[]{:S(2)}) collective-permute-start(bf16[1,10,256,256]{3,2,1,0:T(8,128)(2,1)S(1)} %bundle.3.near.refs_1_), channel_id=1, source_target_pairs={{0,2},{2,0},{4,6},{6,4},{1,3},{3,1},{5,7},{7,5},{8,10},{10,8},{12,... | collective-permute-start | bytes 3932168 | tf_op jit(solution)/shard_map/ppermute | solution.py:445
  36.7 10.6 %collective-permute-start.7 = (bf16[1,2,256,256]{3,2,1,0:T(8,128)(2,1)S(1)}, bf16[1,2,256,256]{3,2,1,0:T(8,128)(2,1)S(1)}, u32[]{:S(2)}, u32[]{:S(2)}) collective-permute-start(bf16[1,2,256,256]{3,2,1,0:T(8,128)(2,1)S(1)} %cut.2), channel_id=1, source_target_pairs={{0,3},{1,2},{2,1},{3,0},{4,7},{5,6},{6,5},{7,4},{8,11},{9,10},{10,... | collective-permute-start | bytes 786440 | tf_op jit(solution)/shard_map/ppermute | solution.py:455
  38.6 12.2 %collective-permute-start.5 = (bf16[1,8,256,256]{3,2,1,0:T(8,128)(2,1)S(1)}, bf16[1,8,256,256]{3,2,1,0:T(8,128)(2,1)S(1)}, u32[]{:S(2)}, u32[]{:S(2)}) collective-permute-start(bf16[1,8,256,256]{3,2,1,0:T(8,128)(2,1)S(1)} %bundle.4), channel_id=1, source_target_pairs={{0,2},{2,0},{4,6},{6,4},{1,3},{3,1},{5,7},{7,5},{8,10},{10,8},{12,... | collective-permute-start | bytes 3145736 | tf_op jit(solution)/shard_map/ppermute | solution.py:445
  47.4 5.6 %collective-permute-start.11 = (bf16[1,8,256,256]{3,2,1,0:T(8,128)(2,1)S(1)}, bf16[1,8,256,256]{3,2,1,0:T(8,128)(2,1)S(1)}, u32[]{:S(2)}, u32[]{:S(2)}) collective-permute-start(bf16[1,8,256,256]{3,2,1,0:T(8,128)(2,1)S(1)} %collective-permute-done.9.pure.refs_0_), channel_id=1, source_target_pairs={{0,2},{2,0},{4,6},{6,4},{1,3},{3,1},{5,7},{7,5},{8,10},{10,8},{12,... | collective-permute-start | bytes 3145736 | tf_op jit(solution)/shard_map/ppermute | solution.py:445
  50.8 3.4 %collective-permute-start.10 = (bf16[1,5,256,256]{3,2,1,0:T(8,128)(2,1)S(1)}, bf16[1,5,256,256]{3,2,1,0:T(8,128)(2,1)S(1)}, u32[]{:S(2)}, u32[]{:S(2)}) collective-permute-start(bf16[1,5,256,256]{3,2,1,0:T(8,128)(2,1)S(1)} %bundle.5.refs_5_), channel_id=1, source_target_pairs={{0,2},{2,0},{4,6},{6,4},{1,3},{3,1},{5,7},{7,5},{8,10},{10,8},{12,... | collective-permute-start | bytes 1966088 | tf_op jit(solution)/shard_map/ppermute | solution.py:445
  53.0 1.2 %copy-start.2 = (s32[1,13]{1,0:T(1,128)S(1)}, s32[1,13]{1,0:T(1,128)}, u32[]{:S(2)}) copy-start(s32[1,13]{1,0:T(1,128)} %keep.1) | copy-start | bytes 160

commit v7 on v6

--- a/solution.py
+++ b/solution.py
@@ -244,7 +244,7 @@
 
 
 def last_kernel(keep, own, beside, middle, *refs):
-    sources, refs = refs[:6], refs[6:]
+    sources, outers, refs = refs[:6], refs[6:8], refs[8:]
     turned, before, out, following, rounded, square, result, out_sems = refs
     way, layer_kind, row_kind = position()
     part = lax.axis_index("layer") * (own.shape[2] // lax.axis_size("layer")) // LANES
@@ -266,7 +266,7 @@
         bring(far, 0, SENT, base + (1 - layer_kind) * SENT)
         following[jnp.where(even, spare, last_item)] = near[0, MIDDLE + SENT]
         for item in range(OUTER):
-            following[jnp.where(even, *ends) + item] = near[0, MIDDLE + PART + item]
+            following[jnp.where(even, *ends) + item] = outers[other][0, MIDDLE + item]
         following[jnp.where(even, last_item, ends[0])] = far[0, SENT]
         following[jnp.where(even, ends[1], ends[0] + 1)] = far[0, SENT + 1]
     following[(1 - row_kind) * WHOLE + LEFT_OUT] = turned[0]
@@ -394,14 +394,14 @@
     )
 
 
-def last(keep, own, beside, middle, sources, turned, before):
+def last(keep, own, beside, middle, sources, outers, turned, before):
     block = own.shape[2]
     shape = jax.ShapeDtypeStruct((1, BAND, block, LANES), jnp.float32)
     return call(
         last_kernel,
         "last",
         shape,
-        [SCALARS] + [VECTOR] * 11,
+        [SCALARS] + [VECTOR] * 13,
         ANYWHERE,
         [
             pltpu.VMEM((4 * (WHOLE + OUTER) + 2, block, block), own.dtype),
@@ -412,7 +412,7 @@
         ],
         120,
         24,
-    )(keep, own, beside, middle, *sources, turned, before)
+    )(keep, own, beside, middle, *sources, *outers, turned, before)
 
 
 def after(*arrays):
@@ -464,19 +464,20 @@
     sums, middle = after(sums, middle)
     far_middle = swap_layers(middle)
     far_diag = swap_layers(cut(swap_kernel, SENT, diag))
-    far_middle, outer = after(far_middle, outer)
-    far_outer = swap_layers(cut(rest_kernel, OUTER, diag, outer))
-    near = bundle(middle, diag, outer)
+    late_outer = after(outer, far_middle)[0]
+    far_outer = swap_layers(cut(rest_kernel, OUTER, diag, late_outer))
+    near = bundle(middle, diag)
     other_near = swap_cores(near)
-    own_far_middle = swap_cores(bundle(far_middle, far_middle))
-    sums, middle = second(density, [near, own_far_middle, other_near, far_middle], sums)
+    ends = bundle(far_middle, outer, outer)
+    other_ends = swap_cores(ends)
+    sums, middle = second(density, [near, other_ends, other_near, far_middle], sums)
     far_outer, far_diag, pure = after(far_outer, far_diag, pure)
     other_pure = swap_cores(pure)
     sums, turned = third(density, pure, other_pure, sums)
     far = bundle(far_diag, far_outer)
     own_far = swap_cores(far)
     sources = [pure, near, own_far, other_pure, other_near, far]
-    out = last(pattern, density, beside, middle, sources, turned, sums)
+    out = last(pattern, density, beside, middle, sources, (ends, other_ends), turned, sums)
     if width < LANES:
         layer = lax.axis_index("layer")
         out = lax.dynamic_slice_in_dim(out, layer * width % LANES, width, 3)

time: 60.3 us -> 60.3 us (level)
  no operation moved by 1% of the time
where the time goes in v7:
time: 60.3 us; the launch traced here: 60.1 us
  starting transfers between devices  25.2 us (42%)
  waiting for transfers between devices  22.9 us (38%)
  Pallas kernels  10.5 us (17%)
  local copies, waits for them, and re-layouts  1.46 us (2%)
    ppermute x2, waiting for transfers between devices, fetch(): return lax.ppermute(array, axes, pairs)  11.1 us
    ppermute x2, starting transfers between devices, fetch(): return lax.ppermute(array, axes, pairs)  9.6 us
    ppermute x3, starting transfers between devices, swap_layers(): return lax.ppermute(array, ('col', 'layer'), pairs)  8.03 us
    pallas_call x1, Pallas kernels, last(): call(last_kernel, 'last', shape, [SCALARS] + [VECTOR] * 13, ANYWHERE, [pl...  5.96 us
    ppermute x6, starting transfers between devices, swap(): lax.ppermute(array, axis, [(peer, peer ^ distance) for peer in range(peer...  5.31 us
    ppermute x3, waiting for transfers between devices, swap_layers(): return lax.ppermute(array, ('col', 'layer'), pairs)  5.22 us
    ppermute x6, waiting for transfers between devices, swap(): lax.ppermute(array, axis, [(peer, peer ^ distance) for peer in range(peer...  4.38 us
    ppermute x1, starting transfers between devices, fetch_diag(): return lax.ppermute(array, ('row', 'col'), pairs)  2.25 us
  transfers between devices with their start and end apart: 12, of which 7 were waited for; matrix products, arithmetic and copies ran while one was open for 0% of the time, Pallas kernels for 8%

profile of v7, /device:TPU:13, one launch (start us, length us, event | category | flops | bytes accessed | tf_op | source)
XLA Modules:
  0.0 60.1 jit_solution(14612341946998320717)
XLA Ops:
  0.0 0.7 %collective-permute-start = (bf16[1,13,256,256]{3,2,1,0:T(8,128)(2,1)}, bf16[1,13,256,256]{3,2,1,0:T(8,128)(2,1)S(1)}, u32[]{:S(2)}, u32[]{:S(2)}) collective-permute-start(bf16[1,13,256,256]{3,2,1,0:T(8,128)(2,1)} %own.7), channel_id=1, source_target_pairs={{0,2},{2,0},{4,6},{6,4},{1,3},{3,1},{5,7},{7,5},{8,10},{10,8},{12,... | collective-permute-start | bytes 5111816 | tf_op jit(solution)/shard_map/ppermute | solution.py:445
  0.7 0.0 copy-start
  0.7 1.5 %copy-done = bf16[1,13,256,256]{3,2,1,0:T(8,128)(2,1)S(1)} copy-done((bf16[1,13,256,256]{3,2,1,0:T(8,128)(2,1)S(1)}, bf16[1,13,256,256]{3,2,1,0:T(8,128)(2,1)}, u32[]{:S(2)}) %copy-start) | copy-done | bytes 1703960
  2.1 0.0 copy-start.1
  2.1 0.2 pack.1
  2.3 1.3 %collective-permute-start.1 = (bf16[1,4,256,256]{3,2,1,0:T(8,128)(2,1)S(1)}, bf16[1,4,256,256]{3,2,1,0:T(8,128)(2,1)S(1)}, u32[]{:S(2)}, u32[]{:S(2)}) collective-permute-start(bf16[1,4,256,256]{3,2,1,0:T(8,128)(2,1)S(1)} %get-tuple-element.19), channel_id=1, source_target_pairs={{0,24},{1,9},{2,10},{3,27},{4,28},{5,13},{6,14},{7,31},{8,0},{9,17... | collective-permute-start | bytes 1572872 | tf_op jit(solution)/shard_map/ppermute | solution.py:434
  3.6 0.2 collective-permute-start.9
  3.9 2.3 %collective-permute-start.2 = (bf16[1,4,256,256]{3,2,1,0:T(8,128)(2,1)S(1)}, bf16[1,4,256,256]{3,2,1,0:T(8,128)(2,1)S(1)}, u32[]{:S(2)}, u32[]{:S(2)}) collective-permute-start(bf16[1,4,256,256]{3,2,1,0:T(8,128)(2,1)S(1)} %get-tuple-element.21), channel_id=1, source_target_pairs={{0,28},{2,30},{4,8},{6,10},{8,4},{10,6},{12,16},{14,18},{16,12},{1... | collective-permute-start | bytes 1572872 | tf_op jit(solution)/shard_map/ppermute | solution.py:441
  6.1 0.0 collective-permute-done.beside
  6.1 0.0 copy-done.1
  6.1 1.7 %first.1.before = f32[13,256,256]{2,1,0:T(8,128)S(1)} custom-call(bf16[1,13,256,256]{3,2,1,0:T(8,128)(2,1)S(1)} %copy-done.1, bf16[1,13,256,256]{3,2,1,0:T(8,128)(2,1)S(1)} %collective-permute-done.beside), custom_call_target="tpu_custom_call" | custom-call | flops 1543503872 | bytes 4194304 | tf_op jit(solution)/shard_map/first/pallas_call | solution.py:357
  7.9 10.5 %collective-permute-done.1.refs_0_ = bf16[1,4,256,256]{3,2,1,0:T(8,128)(2,1)S(1)} collective-permute-done((bf16[1,4,256,256]{3,2,1,0:T(8,128)(2,1)S(1)}, bf16[1,4,256,256]{3,2,1,0:T(8,128)(2,1)S(1)}, u32[]{:S(2)}, u32[]{:S(2)}) %collective-permute-start.1) | collective-permute-done | bytes 524320 | tf_op jit(solution)/shard_map/ppermute | solution.py:434
  18.4 3.7 %collective-permute-start.3 = (bf16[1,4,256,256]{3,2,1,0:T(8,128)(2,1)S(1)}, bf16[1,4,256,256]{3,2,1,0:T(8,128)(2,1)S(1)}, u32[]{:S(2)}, u32[]{:S(2)}) collective-permute-start(bf16[1,4,256,256]{3,2,1,0:T(8,128)(2,1)S(1)} %collective-permute-done.1.refs_0_), channel_id=1, source_target_pairs={{0,3},{1,2},{2,1},{3,0},{4,7},{5,6},{6,5},{7,4},{8,11},{9,10},{10,... | collective-permute-start | bytes 1572872 | tf_op jit(solution)/shard_map/ppermute | solution.py:455
  22.1 8.3 %collective-permute-start.4 = (bf16[1,2,256,256]{3,2,1,0:T(8,128)(2,1)S(1)}, bf16[1,2,256,256]{3,2,1,0:T(8,128)(2,1)S(1)}, u32[]{:S(2)}, u32[]{:S(2)}) collective-permute-start(bf16[1,2,256,256]{3,2,1,0:T(8,128)(2,1)S(1)} %get-tuple-element.22), channel_id=1, source_target_pairs={{0,20},{1,13},{2,14},{3,23},{4,24},{5,17},{6,18},{7,27},{8,28},{9,... | collective-permute-start | bytes 786440 | tf_op jit(solution)/shard_map/ppermute | solution.py:434
  30.3 2.2 %collective-permute-done.2.refs_1_.diag = bf16[1,4,256,256]{3,2,1,0:T(8,128)(2,1)S(1)} collective-permute-done((bf16[1,4,256,256]{3,2,1,0:T(8,128)(2,1)S(1)}, bf16[1,4,256,256]{3,2,1,0:T(8,128)(2,1)S(1)}, u32[]{:S(2)}, u32[]{:S(2)}) %collective-permute-start.2) | collective-permute-done | bytes 524320 | tf_op jit(solution)/shard_map/ppermute | solution.py:441
  32.5 2.2 %collective-permute-start.8 = (bf16[1,3,256,256]{3,2,1,0:T(8,128)(2,1)S(1)}, bf16[1,3,256,256]{3,2,1,0:T(8,128)(2,1)S(1)}, u32[]{:S(2)}, u32[]{:S(2)}) collective-permute-start(bf16[1,3,256,256]{3,2,1,0:T(8,128)(2,1)S(1)} %cut.3), channel_id=1, source_target_pairs={{0,3},{1,2},{2,1},{3,0},{4,7},{5,6},{6,5},{7,4},{8,11},{9,10},{10,... | collective-permute-start | bytes 1179656 | tf_op jit(solution)/shard_map/ppermute | solution.py:455
  34.7 0.6 collective-permute-done.4.refs_1_.refs_2_.outer
  35.3 0.0 collective-permute-done.3.refs_0_.other_far
  35.3 2.2 %collective-permute-start.7 = (bf16[1,2,256,256]{3,2,1,0:T(8,128)(2,1)S(1)}, bf16[1,2,256,256]{3,2,1,0:T(8,128)(2,1)S(1)}, u32[]{:S(2)}, u32[]{:S(2)}) collective-permute-start(bf16[1,2,256,256]{3,2,1,0:T(8,128)(2,1)S(1)} %cut.2), channel_id=1, source_target_pairs={{0,3},{1,2},{2,1},{3,0},{4,7},{5,6},{6,5},{7,4},{8,11},{9,10},{10,... | collective-permute-start | bytes 786440 | tf_op jit(solution)/shard_map/ppermute | solution.py:455
  37.5 0.1 bundle.3.near.refs_1_
  37.6 0.9 %collective-permute-start.6 = (bf16[1,8,256,256]{3,2,1,0:T(8,128)(2,1)S(1)}, bf16[1,8,256,256]{3,2,1,0:T(8,128)(2,1)S(1)}, u32[]{:S(2)}, u32[]{:S(2)}) collective-permute-start(bf16[1,8,256,256]{3,2,1,0:T(8,128)(2,1)S(1)} %bundle.3.near.refs_1_), channel_id=1, source_target_pairs={{0,2},{2,0},{4,6},{6,4},{1,3},{3,1},{5,7},{7,5},{8,10},{10,8},{12,... | collective-permute-start | bytes 3145736 | tf_op jit(solution)/shard_map/ppermute | solution.py:445
  38.5 0.1 bundle.4.refs_6_
  38.6 0.1 collective-permute-start.5
  38.7 3.1 %collective-permute-done.8.refs_0_ = bf16[1,3,256,256]{3,2,1,0:T(8,128)(2,1)S(1)} collective-permute-done((bf16[1,3,256,256]{3,2,1,0:T(8,128)(2,1)S(1)}, bf16[1,3,256,256]{3,2,1,0:T(8,128)(2,1)S(1)}, u32[]{:S(2)}, u32[]{:S(2)}) %collective-permute-start.8) | collective-permute-done | bytes 393248 | tf_op jit(solution)/shard_map/ppermute | solution.py:455
  41.8 3.5 %collective-permute-done.9.pure.refs_0_ = bf16[1,8,256,256]{3,2,1,0:T(8,128)(2,1)S(1)} collective-permute-done((bf16[1,8,256,256]{3,2,1,0:T(8,128)(2,1)S(1)}, bf16[1,8,256,256]{3,2,1,0:T(8,128)(2,1)S(1)}, u32[]{:S(2)}, u32[]{:S(2)}) %collective-permute-start.9) | collective-permute-done | bytes 1048608 | tf_op jit(solution)/shard_map/ppermute | solution.py:445
  45.3 2.1 %collective-permute-done.7.refs_1_ = bf16[1,2,256,256]{3,2,1,0:T(8,128)(2,1)S(1)} collective-permute-done((bf16[1,2,256,256]{3,2,1,0:T(8,128)(2,1)S(1)}, bf16[1,2,256,256]{3,2,1,0:T(8,128)(2,1)S(1)}, u32[]{:S(2)}, u32[]{:S(2)}) %collective-permute-start.7) | collective-permute-done | bytes 262176 | tf_op jit(solution)/shard_map/ppermute | solution.py:455
  47.4 3.3 %collective-permute-start.11 = (bf16[1,8,256,256]{3,2,1,0:T(8,128)(2,1)S(1)}, bf16[1,8,256,256]{3,2,1,0:T(8,128)(2,1)S(1)}, u32[]{:S(2)}, u32[]{:S(2)}) collective-permute-start(bf16[1,8,256,256]{3,2,1,0:T(8,128)(2,1)S(1)} %collective-permute-done.9.pure.refs_0_), channel_id=1, source_target_pairs={{0,2},{2,0},{4,6},{6,4},{1,3},{3,1},{5,7},{7,5},{8,10},{10,8},{12,... | collective-permute-start | bytes 3145736 | tf_op jit(solution)/shard_map/ppermute | solution.py:445
  50.8 0.1 collective-permute-start.10
  50.8 0.0 collective-permute-done.6.other_near.refs_4_
  50.8 0.0 collective-permute-done.5.far.refs_7_
  50.9 1.3 %second.1 = (f32[13,256,256]{2,1,0:T(8,128)S(1)}, bf16[16,256,256]{2,1,0:T(8,128)(2,1)S(1)}) custom-call(bf16[1,13,256,256]{3,2,1,0:T(8,128)(2,1)S(1)} %copy-done.1, bf16[1,8,256,256]{3,2,1,0:T(8,128)(2,1)S(1)} %bundle.3.near.refs_1_, bf16[1,8,256,256]{3,2,1,0:T(8,128)(2,1)S(1)} %collective-permute-done.5.far.refs_7_, ...), custom_call_target="tpu_custom_call" | custom-call | flops 1006632960 | bytes 4194304 | tf_op jit(solution)/shard_map/second/pallas_call | solution.py:377
  52.1 0.8 %collective-permute-done.11.other_pure.refs_3_ = bf16[1,8,256,256]{3,2,1,0:T(8,128)(2,1)S(1)} collective-permute-done((bf16[1,8,256,256]{3,2,1,0:T(8,128)(2,1)S(1)}, bf16[1,8,256,256]{3,2,1,0:T(8,128)(2,1)S(1)}, u32[]{:S(2)}, u32[]{:S(2)}) %collective-permute-start.11) | collective-permute-done | bytes 1048608 | tf_op jit(solution)/shard_map/ppermute | solution.py:445
  53.0 0.0 copy-start.2
  53.0 1.2 %third.1 = (f32[13,256,256]{2,1,0:T(8,128)S(1)}, bf16[1,256,256]{2,1,0:T(8,128)(2,1)S(1)}) custom-call(bf16[1,13,256,256]{3,2,1,0:T(8,128)(2,1)S(1)} %copy-done.1, bf16[1,8,256,256]{3,2,1,0:T(8,128)(2,1)S(1)} %collective-permute-done.9.pure.refs_0_, bf16[1,8,256,256]{3,2,1,0:T(8,128)(2,1)S(1)} %collective-permute-done.11.other_pure.refs_3_, ...), custom_call_target="tpu_custom_call" | custom-call | flops 1006632960 | bytes 4194304 | tf_op jit(solution)/shard_map/third/pallas_call | solution.py:392
  54.2 0.0 collective-permute-done.10.refs_2_
  54.2 0.0 copy-done.2
  54.2 6.0 %last.1 = f32[1,13,256,128]{3,2,1,0:T(8,128)} custom-call(s32[1,13]{1,0:T(1,128)S(1)} %copy-done.2, bf16[1,13,256,256]{3,2,1,0:T(8,128)(2,1)S(1)} %copy-done.1, bf16[1,13,256,256]{3,2,1,0:T(8,128)(2,1)S(1)} %collective-permute-done.beside, bf16[16,256,256]{2,1,0:T(8,128)(2,1)S(1)} %get-tuple-element.24.middle, ...), custom_call_target="tpu_custom_call" | custom-call | flops 4026531840 | bytes 4194304 | tf_op jit(solution)/shard_map/last/pallas_call | solution.py:400
  (3 shorter events, 0.1 us)
Async XLA Ops:
  0.0 6.1 %collective-permute-start = (bf16[1,13,256,256]{3,2,1,0:T(8,128)(2,1)}, bf16[1,13,256,256]{3,2,1,0:T(8,128)(2,1)S(1)}, u32[]{:S(2)}, u32[]{:S(2)}) collective-permute-start(bf16[1,13,256,256]{3,2,1,0:T(8,128)(2,1)} %own.7), channel_id=1, source_target_pairs={{0,2},{2,0},{4,6},{6,4},{1,3},{3,1},{5,7},{7,5},{8,10},{10,8},{12,... | collective-permute-start | bytes 5111816 | tf_op jit(solution)/shard_map/ppermute | solution.py:445
  0.7 1.5 %copy-start = (bf16[1,13,256,256]{3,2,1,0:T(8,128)(2,1)S(1)}, bf16[1,13,256,256]{3,2,1,0:T(8,128)(2,1)}, u32[]{:S(2)}) copy-start(bf16[1,13,256,256]{3,2,1,0:T(8,128)(2,1)} %own.7) | copy-start | bytes 5111812
  2.1 4.0 %copy-start.1 = (bf16[1,13,256,256]{3,2,1,0:T(8,128)(2,1)S(1)}, bf16[1,13,256,256]{3,2,1,0:T(8,128)(2,1)}, u32[]{:S(2)}) copy-start(bf16[1,13,256,256]{3,2,1,0:T(8,128)(2,1)} %own.7) | copy-start | bytes 5111812
  2.3 16.1 %collective-permute-start.1 = (bf16[1,4,256,256]{3,2,1,0:T(8,128)(2,1)S(1)}, bf16[1,4,256,256]{3,2,1,0:T(8,128)(2,1)S(1)}, u32[]{:S(2)}, u32[]{:S(2)}) collective-permute-start(bf16[1,4,256,256]{3,2,1,0:T(8,128)(2,1)S(1)} %get-tuple-element.19), channel_id=1, source_target_pairs={{0,24},{1,9},{2,10},{3,27},{4,28},{5,13},{6,14},{7,31},{8,0},{9,17... | collective-permute-start | bytes 1572872 | tf_op jit(solution)/shard_map/ppermute | solution.py:434
  3.6 41.6 %collective-permute-start.9 = (bf16[1,8,256,256]{3,2,1,0:T(8,128)(2,1)S(1)}, bf16[1,8,256,256]{3,2,1,0:T(8,128)(2,1)S(1)}, u32[]{:S(2)}, u32[]{:S(2)}) collective-permute-start(bf16[1,8,256,256]{3,2,1,0:T(8,128)(2,1)S(1)} %get-tuple-element.26), channel_id=1, source_target_pairs={{0,4},{2,6},{4,0},{6,2},{1,5},{3,7},{5,1},{7,3},{8,12},{10,14},{12... | collective-permute-start | bytes 3145736 | tf_op jit(solution)/shard_map/ppermute | solution.py:445
  3.9 28.6 %collective-permute-start.2 = (bf16[1,4,256,256]{3,2,1,0:T(8,128)(2,1)S(1)}, bf16[1,4,256,256]{3,2,1,0:T(8,128)(2,1)S(1)}, u32[]{:S(2)}, u32[]{:S(2)}) collective-permute-start(bf16[1,4,256,256]{3,2,1,0:T(8,128)(2,1)S(1)} %get-tuple-element.21), channel_id=1, source_target_pairs={{0,28},{2,30},{4,8},{6,10},{8,4},{10,6},{12,16},{14,18},{16,12},{1... | collective-permute-start | bytes 1572872 | tf_op jit(solution)/shard_map/ppermute | solution.py:441
  18.4 16.9 %collective-permute-start.3 = (bf16[1,4,256,256]{3,2,1,0:T(8,128)(2,1)S(1)}, bf16[1,4,256,256]{3,2,1,0:T(8,128)(2,1)S(1)}, u32[]{:S(2)}, u32[]{:S(2)}) collective-permute-start(bf16[1,4,256,256]{3,2,1,0:T(8,128)(2,1)S(1)} %collective-permute-done.1.refs_0_), channel_id=1, source_target_pairs={{0,3},{1,2},{2,1},{3,0},{4,7},{5,6},{6,5},{7,4},{8,11},{9,10},{10,... | collective-permute-start | bytes 1572872 | tf_op jit(solution)/shard_map/ppermute | solution.py:455
  22.1 13.2 %collective-permute-start.4 = (bf16[1,2,256,256]{3,2,1,0:T(8,128)(2,1)S(1)}, bf16[1,2,256,256]{3,2,1,0:T(8,128)(2,1)S(1)}, u32[]{:S(2)}, u32[]{:S(2)}) collective-permute-start(bf16[1,2,256,256]{3,2,1,0:T(8,128)(2,1)S(1)} %get-tuple-element.22), channel_id=1, source_target_pairs={{0,20},{1,13},{2,14},{3,23},{4,24},{5,17},{6,18},{7,27},{8,28},{9,... | collective-permute-start | bytes 786440 | tf_op jit(solution)/shard_map/ppermute | solution.py:434
  32.5 9.3 %collective-permute-start.8 = (bf16[1,3,256,256]{3,2,1,0:T(8,128)(2,1)S(1)}, bf16[1,3,256,256]{3,2,1,0:T(8,128)(2,1)S(1)}, u32[]{:S(2)}, u32[]{:S(2)}) collective-permute-start(bf16[1,3,256,256]{3,2,1,0:T(8,128)(2,1)S(1)} %cut.3), channel_id=1, source_target_pairs={{0,3},{1,2},{2,1},{3,0},{4,7},{5,6},{6,5},{7,4},{8,11},{9,10},{10,... | collective-permute-start | bytes 1179656 | tf_op jit(solution)/shard_map/ppermute | solution.py:455
  35.3 12.1 %collective-permute-start.7 = (bf16[1,2,256,256]{3,2,1,0:T(8,128)(2,1)S(1)}, bf16[1,2,256,256]{3,2,1,0:T(8,128)(2,1)S(1)}, u32[]{:S(2)}, u32[]{:S(2)}) collective-permute-start(bf16[1,2,256,256]{3,2,1,0:T(8,128)(2,1)S(1)} %cut.2), channel_id=1, source_target_pairs={{0,3},{1,2},{2,1},{3,0},{4,7},{5,6},{6,5},{7,4},{8,11},{9,10},{10,... | collective-permute-start | bytes 786440 | tf_op jit(solution)/shard_map/ppermute | solution.py:455
  37.6 13.3 %collective-permute-start.6 = (bf16[1,8,256,256]{3,2,1,0:T(8,128)(2,1)S(1)}, bf16[1,8,256,256]{3,2,1,0:T(8,128)(2,1)S(1)}, u32[]{:S(2)}, u32[]{:S(2)}) collective-permute-start(bf16[1,8,256,256]{3,2,1,0:T(8,128)(2,1)S(1)} %bundle.3.near.refs_1_), channel_id=1, source_target_pairs={{0,2},{2,0},{4,6},{6,4},{1,3},{3,1},{5,7},{7,5},{8,10},{10,8},{12,... | collective-permute-start | bytes 3145736 | tf_op jit(solution)/shard_map/ppermute | solution.py:445
  38.6 12.3 %collective-permute-start.5 = (bf16[1,8,256,256]{3,2,1,0:T(8,128)(2,1)S(1)}, bf16[1,8,256,256]{3,2,1,0:T(8,128)(2,1)S(1)}, u32[]{:S(2)}, u32[]{:S(2)}) collective-permute-start(bf16[1,8,256,256]{3,2,1,0:T(8,128)(2,1)S(1)} %bundle.4.refs_6_), channel_id=1, source_target_pairs={{0,2},{2,0},{4,6},{6,4},{1,3},{3,1},{5,7},{7,5},{8,10},{10,8},{12,... | collective-permute-start | bytes 3145736 | tf_op jit(solution)/shard_map/ppermute | solution.py:445
  47.4 5.6 %collective-permute-start.11 = (bf16[1,8,256,256]{3,2,1,0:T(8,128)(2,1)S(1)}, bf16[1,8,256,256]{3,2,1,0:T(8,128)(2,1)S(1)}, u32[]{:S(2)}, u32[]{:S(2)}) collective-permute-start(bf16[1,8,256,256]{3,2,1,0:T(8,128)(2,1)S(1)} %collective-permute-done.9.pure.refs_0_), channel_id=1, source_target_pairs={{0,2},{2,0},{4,6},{6,4},{1,3},{3,1},{5,7},{7,5},{8,10},{10,8},{12,... | collective-permute-start | bytes 3145736 | tf_op jit(solution)/shard_map/ppermute | solution.py:445
  50.8 3.4 %collective-permute-start.10 = (bf16[1,5,256,256]{3,2,1,0:T(8,128)(2,1)S(1)}, bf16[1,5,256,256]{3,2,1,0:T(8,128)(2,1)S(1)}, u32[]{:S(2)}, u32[]{:S(2)}) collective-permute-start(bf16[1,5,256,256]{3,2,1,0:T(8,128)(2,1)S(1)} %bundle.5.refs_5_), channel_id=1, source_target_pairs={{0,2},{2,0},{4,6},{6,4},{1,3},{3,1},{5,7},{7,5},{8,10},{10,8},{12,... | collective-permute-start | bytes 1966088 | tf_op jit(solution)/shard_map/ppermute | solution.py:445
  53.0 1.2 %copy-start.2 = (s32[1,13]{1,0:T(1,128)S(1)}, s32[1,13]{1,0:T(1,128)}, u32[]{:S(2)}) copy-start(s32[1,13]{1,0:T(1,128)} %keep.1) | copy-start | bytes 160

commit v8 on v7

--- a/solution.py
+++ b/solution.py
@@ -461,7 +461,6 @@
     outer = fetch(outer, 3)
     pure = swap(pure, "col", 2)
     sums = first(density, beside)
-    sums, middle = after(sums, middle)
     far_middle = swap_layers(middle)
     far_diag = swap_layers(cut(swap_kernel, SENT, diag))
     late_outer = after(outer, far_middle)[0]

time: 60.3 us -> 59.5 us (0.987)
  the two profiles are of different devices: /device:TPU:13 before, /device:TPU:0 now
where the time goes in v8:
time: 59.5 us; the launch traced here: 58.7 us
  waiting for transfers between devices  31 us (52%)
  starting transfers between devices  15.6 us (26%)
  Pallas kernels  10.5 us (18%)
  local copies, waits for them, and re-layouts  1.47 us (2%)
    ppermute x2, waiting for transfers between devices, fetch(): return lax.ppermute(array, axes, pairs)  16.2 us
    ppermute x1, waiting for transfers between devices, fetch_diag(): return lax.ppermute(array, ('row', 'col'), pairs)  9.57 us
    ppermute x6, starting transfers between devices, swap(): lax.ppermute(array, axis, [(peer, peer ^ distance) for peer in range(peer...  8.23 us
    pallas_call x1, Pallas kernels, last(): call(last_kernel, 'last', shape, [SCALARS] + [VECTOR] * 13, ANYWHERE, [pl...  5.96 us
    ppermute x2, starting transfers between devices, fetch(): return lax.ppermute(array, axes, pairs)  5.1 us
    ppermute x6, waiting for transfers between devices, swap(): lax.ppermute(array, axis, [(peer, peer ^ distance) for peer in range(peer...  2.61 us
    ppermute x3, waiting for transfers between devices, swap_layers(): return lax.ppermute(array, ('col', 'layer'), pairs)  2.54 us
    ppermute x3, starting transfers between devices, swap_layers(): return lax.ppermute(array, ('col', 'layer'), pairs)  1.9 us
  transfers between devices with their start and end apart: 12, of which 6 were waited for; matrix products, arithmetic and copies ran while one was open for 0% of the time, Pallas kernels for 8%

profile of v8, /device:TPU:0, one launch (start us, length us, event | category | flops | bytes accessed | tf_op | source)
XLA Modules:
  0.0 58.7 jit_solution(15928910003644506147)
XLA Ops:
  0.0 0.0 copy-start
  0.0 1.5 %copy-done = bf16[1,13,256,256]{3,2,1,0:T(8,128)(2,1)S(1)} copy-done((bf16[1,13,256,256]{3,2,1,0:T(8,128)(2,1)S(1)}, bf16[1,13,256,256]{3,2,1,0:T(8,128)(2,1)}, u32[]{:S(2)}) %copy-start) | copy-done | bytes 1703960
  1.5 0.2 pack.1
  1.6 5.1 %collective-permute-start.1 = (bf16[1,4,256,256]{3,2,1,0:T(8,128)(2,1)S(1)}, bf16[1,4,256,256]{3,2,1,0:T(8,128)(2,1)S(1)}, u32[]{:S(2)}, u32[]{:S(2)}) collective-permute-start(bf16[1,4,256,256]{3,2,1,0:T(8,128)(2,1)S(1)} %get-tuple-element.17), channel_id=1, source_target_pairs={{0,24},{1,9},{2,10},{3,27},{4,28},{5,13},{6,14},{7,31},{8,0},{9,17... | collective-permute-start | bytes 1572872 | tf_op jit(solution)/shard_map/ppermute | solution.py:434
  6.7 1.5 %collective-permute-start.9 = (bf16[1,8,256,256]{3,2,1,0:T(8,128)(2,1)S(1)}, bf16[1,8,256,256]{3,2,1,0:T(8,128)(2,1)S(1)}, u32[]{:S(2)}, u32[]{:S(2)}) collective-permute-start(bf16[1,8,256,256]{3,2,1,0:T(8,128)(2,1)S(1)} %get-tuple-element.22), channel_id=1, source_target_pairs={{0,4},{2,6},{4,0},{6,2},{1,5},{3,7},{5,1},{7,3},{8,12},{10,14},{12... | collective-permute-start | bytes 3145736 | tf_op jit(solution)/shard_map/ppermute | solution.py:445
  8.2 0.4 collective-permute-start.2
  8.6 0.0 collective-permute-start
  8.6 13.1 %collective-permute-done.1.refs_0_ = bf16[1,4,256,256]{3,2,1,0:T(8,128)(2,1)S(1)} collective-permute-done((bf16[1,4,256,256]{3,2,1,0:T(8,128)(2,1)S(1)}, bf16[1,4,256,256]{3,2,1,0:T(8,128)(2,1)S(1)}, u32[]{:S(2)}, u32[]{:S(2)}) %collective-permute-start.1) | collective-permute-done | bytes 524320 | tf_op jit(solution)/shard_map/ppermute | solution.py:434
  21.7 0.0 collective-permute-start.3
  21.8 0.0 collective-permute-start.4
  21.8 9.6 %collective-permute-done.2.refs_1_.diag = bf16[1,4,256,256]{3,2,1,0:T(8,128)(2,1)S(1)} collective-permute-done((bf16[1,4,256,256]{3,2,1,0:T(8,128)(2,1)S(1)}, bf16[1,4,256,256]{3,2,1,0:T(8,128)(2,1)S(1)}, u32[]{:S(2)}, u32[]{:S(2)}) %collective-permute-start.2) | collective-permute-done | bytes 524320 | tf_op jit(solution)/shard_map/ppermute | solution.py:441
  31.4 0.1 collective-permute-start.8
  31.4 3.1 %collective-permute-done.4.refs_1_.refs_2_.outer = bf16[1,2,256,256]{3,2,1,0:T(8,128)(2,1)S(1)} collective-permute-done((bf16[1,2,256,256]{3,2,1,0:T(8,128)(2,1)S(1)}, bf16[1,2,256,256]{3,2,1,0:T(8,128)(2,1)S(1)}, u32[]{:S(2)}, u32[]{:S(2)}) %collective-permute-start.4) | collective-permute-done | bytes 262176 | tf_op jit(solution)/shard_map/ppermute | solution.py:434
  34.5 0.0 collective-permute-done.3.refs_0_.other_far
  34.6 1.8 %collective-permute-start.7 = (bf16[1,2,256,256]{3,2,1,0:T(8,128)(2,1)S(1)}, bf16[1,2,256,256]{3,2,1,0:T(8,128)(2,1)S(1)}, u32[]{:S(2)}, u32[]{:S(2)}) collective-permute-start(bf16[1,2,256,256]{3,2,1,0:T(8,128)(2,1)S(1)} %cut.2), channel_id=1, source_target_pairs={{0,3},{1,2},{2,1},{3,0},{4,7},{5,6},{6,5},{7,4},{8,11},{9,10},{10,... | collective-permute-start | bytes 786440 | tf_op jit(solution)/shard_map/ppermute | solution.py:455
  36.4 0.1 bundle.3.near.refs_1_
  36.5 0.0 copy-start.1
  36.5 4.8 %collective-permute-start.6 = (bf16[1,8,256,256]{3,2,1,0:T(8,128)(2,1)S(1)}, bf16[1,8,256,256]{3,2,1,0:T(8,128)(2,1)S(1)}, u32[]{:S(2)}, u32[]{:S(2)}) collective-permute-start(bf16[1,8,256,256]{3,2,1,0:T(8,128)(2,1)S(1)} %bundle.3.near.refs_1_), channel_id=1, source_target_pairs={{0,2},{2,0},{4,6},{6,4},{1,3},{3,1},{5,7},{7,5},{8,10},{10,8},{12,... | collective-permute-start | bytes 3145736 | tf_op jit(solution)/shard_map/ppermute | solution.py:445
  41.3 0.1 bundle.4.refs_6_
  41.3 0.9 %collective-permute-done.8.refs_0_ = bf16[1,3,256,256]{3,2,1,0:T(8,128)(2,1)S(1)} collective-permute-done((bf16[1,3,256,256]{3,2,1,0:T(8,128)(2,1)S(1)}, bf16[1,3,256,256]{3,2,1,0:T(8,128)(2,1)S(1)}, u32[]{:S(2)}, u32[]{:S(2)}) %collective-permute-start.8) | collective-permute-done | bytes 393248 | tf_op jit(solution)/shard_map/ppermute | solution.py:455
  42.2 1.3 %collective-permute-start.5 = (bf16[1,8,256,256]{3,2,1,0:T(8,128)(2,1)S(1)}, bf16[1,8,256,256]{3,2,1,0:T(8,128)(2,1)S(1)}, u32[]{:S(2)}, u32[]{:S(2)}) collective-permute-start(bf16[1,8,256,256]{3,2,1,0:T(8,128)(2,1)S(1)} %bundle.4.refs_6_), channel_id=1, source_target_pairs={{0,2},{2,0},{4,6},{6,4},{1,3},{3,1},{5,7},{7,5},{8,10},{10,8},{12,... | collective-permute-start | bytes 3145736 | tf_op jit(solution)/shard_map/ppermute | solution.py:445
  43.6 2.6 %collective-permute-done.9.pure.refs_0_ = bf16[1,8,256,256]{3,2,1,0:T(8,128)(2,1)S(1)} collective-permute-done((bf16[1,8,256,256]{3,2,1,0:T(8,128)(2,1)S(1)}, bf16[1,8,256,256]{3,2,1,0:T(8,128)(2,1)S(1)}, u32[]{:S(2)}, u32[]{:S(2)}) %collective-permute-start.9) | collective-permute-done | bytes 1048608 | tf_op jit(solution)/shard_map/ppermute | solution.py:445
  46.2 1.7 %collective-permute-done.7.refs_1_ = bf16[1,2,256,256]{3,2,1,0:T(8,128)(2,1)S(1)} collective-permute-done((bf16[1,2,256,256]{3,2,1,0:T(8,128)(2,1)S(1)}, bf16[1,2,256,256]{3,2,1,0:T(8,128)(2,1)S(1)}, u32[]{:S(2)}, u32[]{:S(2)}) %collective-permute-start.7) | collective-permute-done | bytes 262176 | tf_op jit(solution)/shard_map/ppermute | solution.py:455
  47.8 0.4 collective-permute-start.11
  48.3 0.1 collective-permute-start.10
  48.5 0.0 collective-permute-done.beside
  48.5 0.0 copy-done.1
  48.5 1.7 %first.1.before = f32[13,256,256]{2,1,0:T(8,128)S(1)} custom-call(bf16[1,13,256,256]{3,2,1,0:T(8,128)(2,1)S(1)} %copy-done.1, bf16[1,13,256,256]{3,2,1,0:T(8,128)(2,1)S(1)} %collective-permute-done.beside), custom_call_target="tpu_custom_call" | custom-call | flops 1543503872 | bytes 4194304 | tf_op jit(solution)/shard_map/first/pallas_call | solution.py:357
  50.2 0.0 collective-permute-done.6.other_near.refs_4_
  50.2 0.0 collective-permute-done.5.far.refs_7_
  50.2 1.3 %second.1 = (f32[13,256,256]{2,1,0:T(8,128)S(1)}, bf16[16,256,256]{2,1,0:T(8,128)(2,1)S(1)}) custom-call(bf16[1,13,256,256]{3,2,1,0:T(8,128)(2,1)S(1)} %copy-done.1, bf16[1,8,256,256]{3,2,1,0:T(8,128)(2,1)S(1)} %bundle.3.near.refs_1_, bf16[1,8,256,256]{3,2,1,0:T(8,128)(2,1)S(1)} %collective-permute-done.5.far.refs_7_, ...), custom_call_target="tpu_custom_call" | custom-call | flops 1006632960 | bytes 4194304 | tf_op jit(solution)/shard_map/second/pallas_call | solution.py:377
  51.5 0.0 collective-permute-done.11.other_pure.refs_3_
  51.5 0.0 copy-start.2
  51.5 1.2 %third.1 = (f32[13,256,256]{2,1,0:T(8,128)S(1)}, bf16[1,256,256]{2,1,0:T(8,128)(2,1)S(1)}) custom-call(bf16[1,13,256,256]{3,2,1,0:T(8,128)(2,1)S(1)} %copy-done.1, bf16[1,8,256,256]{3,2,1,0:T(8,128)(2,1)S(1)} %collective-permute-done.9.pure.refs_0_, bf16[1,8,256,256]{3,2,1,0:T(8,128)(2,1)S(1)} %collective-permute-done.11.other_pure.refs_3_, ...), custom_call_target="tpu_custom_call" | custom-call | flops 1006632960 | bytes 4194304 | tf_op jit(solution)/shard_map/third/pallas_call | solution.py:392
  52.7 0.0 collective-permute-done.10.refs_2_
  52.7 0.0 copy-done.2
  52.7 6.0 %last.1 = f32[1,13,256,128]{3,2,1,0:T(8,128)} custom-call(s32[1,13]{1,0:T(1,128)S(1)} %copy-done.2, bf16[1,13,256,256]{3,2,1,0:T(8,128)(2,1)S(1)} %copy-done.1, bf16[1,13,256,256]{3,2,1,0:T(8,128)(2,1)S(1)} %collective-permute-done.beside, bf16[16,256,256]{2,1,0:T(8,128)(2,1)S(1)} %get-tuple-element.20.middle, ...), custom_call_target="tpu_custom_call" | custom-call | flops 4026531840 | bytes 4194304 | tf_op jit(solution)/shard_map/last/pallas_call | solution.py:400
  (3 shorter events, 0.1 us)
Async XLA Ops:
  0.0 1.5 %copy-start = (bf16[1,13,256,256]{3,2,1,0:T(8,128)(2,1)S(1)}, bf16[1,13,256,256]{3,2,1,0:T(8,128)(2,1)}, u32[]{:S(2)}) copy-start(bf16[1,13,256,256]{3,2,1,0:T(8,128)(2,1)} %own.7) | copy-start | bytes 5111812
  1.6 20.1 %collective-permute-start.1 = (bf16[1,4,256,256]{3,2,1,0:T(8,128)(2,1)S(1)}, bf16[1,4,256,256]{3,2,1,0:T(8,128)(2,1)S(1)}, u32[]{:S(2)}, u32[]{:S(2)}) collective-permute-start(bf16[1,4,256,256]{3,2,1,0:T(8,128)(2,1)S(1)} %get-tuple-element.17), channel_id=1, source_target_pairs={{0,24},{1,9},{2,10},{3,27},{4,28},{5,13},{6,14},{7,31},{8,0},{9,17... | collective-permute-start | bytes 1572872 | tf_op jit(solution)/shard_map/ppermute | solution.py:434
  6.7 39.4 %collective-permute-start.9 = (bf16[1,8,256,256]{3,2,1,0:T(8,128)(2,1)S(1)}, bf16[1,8,256,256]{3,2,1,0:T(8,128)(2,1)S(1)}, u32[]{:S(2)}, u32[]{:S(2)}) collective-permute-start(bf16[1,8,256,256]{3,2,1,0:T(8,128)(2,1)S(1)} %get-tuple-element.22), channel_id=1, source_target_pairs={{0,4},{2,6},{4,0},{6,2},{1,5},{3,7},{5,1},{7,3},{8,12},{10,14},{12... | collective-permute-start | bytes 3145736 | tf_op jit(solution)/shard_map/ppermute | solution.py:445
  8.2 23.1 %collective-permute-start.2 = (bf16[1,4,256,256]{3,2,1,0:T(8,128)(2,1)S(1)}, bf16[1,4,256,256]{3,2,1,0:T(8,128)(2,1)S(1)}, u32[]{:S(2)}, u32[]{:S(2)}) collective-permute-start(bf16[1,4,256,256]{3,2,1,0:T(8,128)(2,1)S(1)} %get-tuple-element.18), channel_id=1, source_target_pairs={{0,28},{2,30},{4,8},{6,10},{8,4},{10,6},{12,16},{14,18},{16,12},{1... | collective-permute-start | bytes 1572872 | tf_op jit(solution)/shard_map/ppermute | solution.py:441
  8.6 39.8 %collective-permute-start = (bf16[1,13,256,256]{3,2,1,0:T(8,128)(2,1)S(1)}, bf16[1,13,256,256]{3,2,1,0:T(8,128)(2,1)S(1)}, u32[]{:S(2)}, u32[]{:S(2)}) collective-permute-start(bf16[1,13,256,256]{3,2,1,0:T(8,128)(2,1)S(1)} %copy-done), channel_id=1, source_target_pairs={{0,2},{2,0},{4,6},{6,4},{1,3},{3,1},{5,7},{7,5},{8,10},{10,8},{12,... | collective-permute-start | bytes 5111816 | tf_op jit(solution)/shard_map/ppermute | solution.py:445
  21.7 12.8 %collective-permute-start.3 = (bf16[1,4,256,256]{3,2,1,0:T(8,128)(2,1)S(1)}, bf16[1,4,256,256]{3,2,1,0:T(8,128)(2,1)S(1)}, u32[]{:S(2)}, u32[]{:S(2)}) collective-permute-start(bf16[1,4,256,256]{3,2,1,0:T(8,128)(2,1)S(1)} %collective-permute-done.1.refs_0_), channel_id=1, source_target_pairs={{0,3},{1,2},{2,1},{3,0},{4,7},{5,6},{6,5},{7,4},{8,11},{9,10},{10,... | collective-permute-start | bytes 1572872 | tf_op jit(solution)/shard_map/ppermute | solution.py:455
  21.8 12.8 %collective-permute-start.4 = (bf16[1,2,256,256]{3,2,1,0:T(8,128)(2,1)S(1)}, bf16[1,2,256,256]{3,2,1,0:T(8,128)(2,1)S(1)}, u32[]{:S(2)}, u32[]{:S(2)}) collective-permute-start(bf16[1,2,256,256]{3,2,1,0:T(8,128)(2,1)S(1)} %get-tuple-element.19), channel_id=1, source_target_pairs={{0,20},{1,13},{2,14},{3,23},{4,24},{5,17},{6,18},{7,27},{8,28},{9,... | collective-permute-start | bytes 786440 | tf_op jit(solution)/shard_map/ppermute | solution.py:434
  31.4 10.9 %collective-permute-start.8 = (bf16[1,3,256,256]{3,2,1,0:T(8,128)(2,1)S(1)}, bf16[1,3,256,256]{3,2,1,0:T(8,128)(2,1)S(1)}, u32[]{:S(2)}, u32[]{:S(2)}) collective-permute-start(bf16[1,3,256,256]{3,2,1,0:T(8,128)(2,1)S(1)} %cut.3), channel_id=1, source_target_pairs={{0,3},{1,2},{2,1},{3,0},{4,7},{5,6},{6,5},{7,4},{8,11},{9,10},{10,... | collective-permute-start | bytes 1179656 | tf_op jit(solution)/shard_map/ppermute | solution.py:455
  34.6 13.3 %collective-permute-start.7 = (bf16[1,2,256,256]{3,2,1,0:T(8,128)(2,1)S(1)}, bf16[1,2,256,256]{3,2,1,0:T(8,128)(2,1)S(1)}, u32[]{:S(2)}, u32[]{:S(2)}) collective-permute-start(bf16[1,2,256,256]{3,2,1,0:T(8,128)(2,1)S(1)} %cut.2), channel_id=1, source_target_pairs={{0,3},{1,2},{2,1},{3,0},{4,7},{5,6},{6,5},{7,4},{8,11},{9,10},{10,... | collective-permute-start | bytes 786440 | tf_op jit(solution)/shard_map/ppermute | solution.py:455
  36.5 12.0 %copy-start.1 = (bf16[1,13,256,256]{3,2,1,0:T(8,128)(2,1)S(1)}, bf16[1,13,256,256]{3,2,1,0:T(8,128)(2,1)}, u32[]{:S(2)}) copy-start(bf16[1,13,256,256]{3,2,1,0:T(8,128)(2,1)} %own.7) | copy-start | bytes 5111812
  36.5 13.7 %collective-permute-start.6 = (bf16[1,8,256,256]{3,2,1,0:T(8,128)(2,1)S(1)}, bf16[1,8,256,256]{3,2,1,0:T(8,128)(2,1)S(1)}, u32[]{:S(2)}, u32[]{:S(2)}) collective-permute-start(bf16[1,8,256,256]{3,2,1,0:T(8,128)(2,1)S(1)} %bundle.3.near.refs_1_), channel_id=1, source_target_pairs={{0,2},{2,0},{4,6},{6,4},{1,3},{3,1},{5,7},{7,5},{8,10},{10,8},{12,... | collective-permute-start | bytes 3145736 | tf_op jit(solution)/shard_map/ppermute | solution.py:445
  42.2 8.0 %collective-permute-start.5 = (bf16[1,8,256,256]{3,2,1,0:T(8,128)(2,1)S(1)}, bf16[1,8,256,256]{3,2,1,0:T(8,128)(2,1)S(1)}, u32[]{:S(2)}, u32[]{:S(2)}) collective-permute-start(bf16[1,8,256,256]{3,2,1,0:T(8,128)(2,1)S(1)} %bundle.4.refs_6_), channel_id=1, source_target_pairs={{0,2},{2,0},{4,6},{6,4},{1,3},{3,1},{5,7},{7,5},{8,10},{10,8},{12,... | collective-permute-start | bytes 3145736 | tf_op jit(solution)/shard_map/ppermute | solution.py:445
  47.8 3.7 %collective-permute-start.11 = (bf16[1,8,256,256]{3,2,1,0:T(8,128)(2,1)S(1)}, bf16[1,8,256,256]{3,2,1,0:T(8,128)(2,1)S(1)}, u32[]{:S(2)}, u32[]{:S(2)}) collective-permute-start(bf16[1,8,256,256]{3,2,1,0:T(8,128)(2,1)S(1)} %collective-permute-done.9.pure.refs_0_), channel_id=1, source_target_pairs={{0,2},{2,0},{4,6},{6,4},{1,3},{3,1},{5,7},{7,5},{8,10},{10,8},{12,... | collective-permute-start | bytes 3145736 | tf_op jit(solution)/shard_map/ppermute | solution.py:445
  48.3 4.4 %collective-permute-start.10 = (bf16[1,5,256,256]{3,2,1,0:T(8,128)(2,1)S(1)}, bf16[1,5,256,256]{3,2,1,0:T(8,128)(2,1)S(1)}, u32[]{:S(2)}, u32[]{:S(2)}) collective-permute-start(bf16[1,5,256,256]{3,2,1,0:T(8,128)(2,1)S(1)} %bundle.5.refs_5_), channel_id=1, source_target_pairs={{0,2},{2,0},{4,6},{6,4},{1,3},{3,1},{5,7},{7,5},{8,10},{10,8},{12,... | collective-permute-start | bytes 1966088 | tf_op jit(solution)/shard_map/ppermute | solution.py:445
  51.5 1.2 %copy-start.2 = (s32[1,13]{1,0:T(1,128)S(1)}, s32[1,13]{1,0:T(1,128)}, u32[]{:S(2)}) copy-start(s32[1,13]{1,0:T(1,128)} %keep.1) | copy-start | bytes 160

commit v9 on v8

--- a/solution.py
+++ b/solution.py
@@ -458,10 +458,11 @@
     diag, middle, outer, pure = pack(density)
     diag = fetch_diag(diag)
     middle = fetch(middle, 2)
-    outer = fetch(outer, 3)
     pure = swap(pure, "col", 2)
     sums = first(density, beside)
     far_middle = swap_layers(middle)
+    middle, outer = after(middle, outer)
+    outer = fetch(outer, 3)
     far_diag = swap_layers(cut(swap_kernel, SENT, diag))
     late_outer = after(outer, far_middle)[0]
     far_outer = swap_layers(cut(rest_kernel, OUTER, diag, late_outer))

time: 59.5 us -> 59.5 us (level)
  no operation moved by 1% of the time
where the time goes in v9:
time: 59.5 us; the launch traced here: 58.7 us
  waiting for transfers between devices  31 us (52%)
  starting transfers between devices  15.6 us (26%)
  Pallas kernels  10.5 us (18%)
  local copies, waits for them, and re-layouts  1.47 us (2%)
    ppermute x2, waiting for transfers between devices, fetch(): return lax.ppermute(array, axes, pairs)  16.2 us
    ppermute x1, waiting for transfers between devices, fetch_diag(): return lax.ppermute(array, ('row', 'col'), pairs)  9.57 us
    ppermute x6, starting transfers between devices, swap(): lax.ppermute(array, axis, [(peer, peer ^ distance) for peer in range(peer...  8.23 us
    pallas_call x1, Pallas kernels, last(): call(last_kernel, 'last', shape, [SCALARS] + [VECTOR] * 13, ANYWHERE, [pl...  5.96 us
    ppermute x2, starting transfers between devices, fetch(): return lax.ppermute(array, axes, pairs)  5.1 us
    ppermute x6, waiting for transfers between devices, swap(): lax.ppermute(array, axis, [(peer, peer ^ distance) for peer in range(peer...  2.61 us
    ppermute x3, waiting for transfers between devices, swap_layers(): return lax.ppermute(array, ('col', 'layer'), pairs)  2.54 us
    ppermute x3, starting transfers between devices, swap_layers(): return lax.ppermute(array, ('col', 'layer'), pairs)  1.9 us
  transfers between devices with their start and end apart: 12, of which 6 were waited for; matrix products, arithmetic and copies ran while one was open for 0% of the time, Pallas kernels for 8%

profile of v9, /device:TPU:0, one launch (start us, length us, event | category | flops | bytes accessed | tf_op | source)
XLA Modules:
  0.0 58.7 jit_solution(15928910003644506147)
XLA Ops:
  0.0 0.0 copy-start
  0.0 1.5 %copy-done = bf16[1,13,256,256]{3,2,1,0:T(8,128)(2,1)S(1)} copy-done((bf16[1,13,256,256]{3,2,1,0:T(8,128)(2,1)S(1)}, bf16[1,13,256,256]{3,2,1,0:T(8,128)(2,1)}, u32[]{:S(2)}) %copy-start) | copy-done | bytes 1703960
  1.5 0.2 pack.1
  1.6 5.1 %collective-permute-start.1 = (bf16[1,4,256,256]{3,2,1,0:T(8,128)(2,1)S(1)}, bf16[1,4,256,256]{3,2,1,0:T(8,128)(2,1)S(1)}, u32[]{:S(2)}, u32[]{:S(2)}) collective-permute-start(bf16[1,4,256,256]{3,2,1,0:T(8,128)(2,1)S(1)} %get-tuple-element.19), channel_id=1, source_target_pairs={{0,24},{1,9},{2,10},{3,27},{4,28},{5,13},{6,14},{7,31},{8,0},{9,17... | collective-permute-start | bytes 1572872 | tf_op jit(solution)/shard_map/ppermute | solution.py:434
  6.7 1.5 %collective-permute-start.9 = (bf16[1,8,256,256]{3,2,1,0:T(8,128)(2,1)S(1)}, bf16[1,8,256,256]{3,2,1,0:T(8,128)(2,1)S(1)}, u32[]{:S(2)}, u32[]{:S(2)}) collective-permute-start(bf16[1,8,256,256]{3,2,1,0:T(8,128)(2,1)S(1)} %get-tuple-element.26), channel_id=1, source_target_pairs={{0,4},{2,6},{4,0},{6,2},{1,5},{3,7},{5,1},{7,3},{8,12},{10,14},{12... | collective-permute-start | bytes 3145736 | tf_op jit(solution)/shard_map/ppermute | solution.py:445
  8.2 0.4 collective-permute-start.2
  8.6 0.0 collective-permute-start
  8.6 13.1 %collective-permute-done.1.refs_0_ = bf16[1,4,256,256]{3,2,1,0:T(8,128)(2,1)S(1)} collective-permute-done((bf16[1,4,256,256]{3,2,1,0:T(8,128)(2,1)S(1)}, bf16[1,4,256,256]{3,2,1,0:T(8,128)(2,1)S(1)}, u32[]{:S(2)}, u32[]{:S(2)}) %collective-permute-start.1) | collective-permute-done | bytes 524320 | tf_op jit(solution)/shard_map/ppermute | solution.py:434
  21.7 0.0 collective-permute-start.3
  21.8 0.0 collective-permute-start.4
  21.8 9.6 %collective-permute-done.2.refs_1_.diag = bf16[1,4,256,256]{3,2,1,0:T(8,128)(2,1)S(1)} collective-permute-done((bf16[1,4,256,256]{3,2,1,0:T(8,128)(2,1)S(1)}, bf16[1,4,256,256]{3,2,1,0:T(8,128)(2,1)S(1)}, u32[]{:S(2)}, u32[]{:S(2)}) %collective-permute-start.2) | collective-permute-done | bytes 524320 | tf_op jit(solution)/shard_map/ppermute | solution.py:441
  31.4 0.1 collective-permute-start.8
  31.4 3.1 %collective-permute-done.4.refs_1_.refs_2_.outer = bf16[1,2,256,256]{3,2,1,0:T(8,128)(2,1)S(1)} collective-permute-done((bf16[1,2,256,256]{3,2,1,0:T(8,128)(2,1)S(1)}, bf16[1,2,256,256]{3,2,1,0:T(8,128)(2,1)S(1)}, u32[]{:S(2)}, u32[]{:S(2)}) %collective-permute-start.4) | collective-permute-done | bytes 262176 | tf_op jit(solution)/shard_map/ppermute | solution.py:434
  34.5 0.0 collective-permute-done.3.refs_0_.other_far
  34.6 1.8 %collective-permute-start.7 = (bf16[1,2,256,256]{3,2,1,0:T(8,128)(2,1)S(1)}, bf16[1,2,256,256]{3,2,1,0:T(8,128)(2,1)S(1)}, u32[]{:S(2)}, u32[]{:S(2)}) collective-permute-start(bf16[1,2,256,256]{3,2,1,0:T(8,128)(2,1)S(1)} %cut.2), channel_id=1, source_target_pairs={{0,3},{1,2},{2,1},{3,0},{4,7},{5,6},{6,5},{7,4},{8,11},{9,10},{10,... | collective-permute-start | bytes 786440 | tf_op jit(solution)/shard_map/ppermute | solution.py:455
  36.4 0.1 bundle.3.near.refs_1_
  36.5 0.0 copy-start.1
  36.5 4.8 %collective-permute-start.6 = (bf16[1,8,256,256]{3,2,1,0:T(8,128)(2,1)S(1)}, bf16[1,8,256,256]{3,2,1,0:T(8,128)(2,1)S(1)}, u32[]{:S(2)}, u32[]{:S(2)}) collective-permute-start(bf16[1,8,256,256]{3,2,1,0:T(8,128)(2,1)S(1)} %bundle.3.near.refs_1_), channel_id=1, source_target_pairs={{0,2},{2,0},{4,6},{6,4},{1,3},{3,1},{5,7},{7,5},{8,10},{10,8},{12,... | collective-permute-start | bytes 3145736 | tf_op jit(solution)/shard_map/ppermute | solution.py:445
  41.3 0.1 bundle.4.refs_6_
  41.3 0.9 %collective-permute-done.8.refs_0_ = bf16[1,3,256,256]{3,2,1,0:T(8,128)(2,1)S(1)} collective-permute-done((bf16[1,3,256,256]{3,2,1,0:T(8,128)(2,1)S(1)}, bf16[1,3,256,256]{3,2,1,0:T(8,128)(2,1)S(1)}, u32[]{:S(2)}, u32[]{:S(2)}) %collective-permute-start.8) | collective-permute-done | bytes 393248 | tf_op jit(solution)/shard_map/ppermute | solution.py:455
  42.2 1.3 %collective-permute-start.5 = (bf16[1,8,256,256]{3,2,1,0:T(8,128)(2,1)S(1)}, bf16[1,8,256,256]{3,2,1,0:T(8,128)(2,1)S(1)}, u32[]{:S(2)}, u32[]{:S(2)}) collective-permute-start(bf16[1,8,256,256]{3,2,1,0:T(8,128)(2,1)S(1)} %bundle.4.refs_6_), channel_id=1, source_target_pairs={{0,2},{2,0},{4,6},{6,4},{1,3},{3,1},{5,7},{7,5},{8,10},{10,8},{12,... | collective-permute-start | bytes 3145736 | tf_op jit(solution)/shard_map/ppermute | solution.py:445
  43.6 2.6 %collective-permute-done.9.pure.refs_0_ = bf16[1,8,256,256]{3,2,1,0:T(8,128)(2,1)S(1)} collective-permute-done((bf16[1,8,256,256]{3,2,1,0:T(8,128)(2,1)S(1)}, bf16[1,8,256,256]{3,2,1,0:T(8,128)(2,1)S(1)}, u32[]{:S(2)}, u32[]{:S(2)}) %collective-permute-start.9) | collective-permute-done | bytes 1048608 | tf_op jit(solution)/shard_map/ppermute | solution.py:445
  46.2 1.7 %collective-permute-done.7.refs_1_ = bf16[1,2,256,256]{3,2,1,0:T(8,128)(2,1)S(1)} collective-permute-done((bf16[1,2,256,256]{3,2,1,0:T(8,128)(2,1)S(1)}, bf16[1,2,256,256]{3,2,1,0:T(8,128)(2,1)S(1)}, u32[]{:S(2)}, u32[]{:S(2)}) %collective-permute-start.7) | collective-permute-done | bytes 262176 | tf_op jit(solution)/shard_map/ppermute | solution.py:455
  47.8 0.4 collective-permute-start.11
  48.3 0.1 collective-permute-start.10
  48.5 0.0 collective-permute-done.beside
  48.5 0.0 copy-done.1
  48.5 1.7 %first.1.before = f32[13,256,256]{2,1,0:T(8,128)S(1)} custom-call(bf16[1,13,256,256]{3,2,1,0:T(8,128)(2,1)S(1)} %copy-done.1, bf16[1,13,256,256]{3,2,1,0:T(8,128)(2,1)S(1)} %collective-permute-done.beside), custom_call_target="tpu_custom_call" | custom-call | flops 1543503872 | bytes 4194304 | tf_op jit(solution)/shard_map/first/pallas_call | solution.py:357
  50.2 0.0 collective-permute-done.6.other_near.refs_4_
  50.2 0.0 collective-permute-done.5.far.refs_7_
  50.2 1.3 %second.1 = (f32[13,256,256]{2,1,0:T(8,128)S(1)}, bf16[16,256,256]{2,1,0:T(8,128)(2,1)S(1)}) custom-call(bf16[1,13,256,256]{3,2,1,0:T(8,128)(2,1)S(1)} %copy-done.1, bf16[1,8,256,256]{3,2,1,0:T(8,128)(2,1)S(1)} %bundle.3.near.refs_1_, bf16[1,8,256,256]{3,2,1,0:T(8,128)(2,1)S(1)} %collective-permute-done.5.far.refs_7_, ...), custom_call_target="tpu_custom_call" | custom-call | flops 1006632960 | bytes 4194304 | tf_op jit(solution)/shard_map/second/pallas_call | solution.py:377
  51.5 0.0 collective-permute-done.11.other_pure.refs_3_
  51.5 0.0 copy-start.2
  51.5 1.2 %third.1 = (f32[13,256,256]{2,1,0:T(8,128)S(1)}, bf16[1,256,256]{2,1,0:T(8,128)(2,1)S(1)}) custom-call(bf16[1,13,256,256]{3,2,1,0:T(8,128)(2,1)S(1)} %copy-done.1, bf16[1,8,256,256]{3,2,1,0:T(8,128)(2,1)S(1)} %collective-permute-done.9.pure.refs_0_, bf16[1,8,256,256]{3,2,1,0:T(8,128)(2,1)S(1)} %collective-permute-done.11.other_pure.refs_3_, ...), custom_call_target="tpu_custom_call" | custom-call | flops 1006632960 | bytes 4194304 | tf_op jit(solution)/shard_map/third/pallas_call | solution.py:392
  52.7 0.0 collective-permute-done.10.refs_2_
  52.7 0.0 copy-done.2
  52.7 6.0 %last.1 = f32[1,13,256,128]{3,2,1,0:T(8,128)} custom-call(s32[1,13]{1,0:T(1,128)S(1)} %copy-done.2, bf16[1,13,256,256]{3,2,1,0:T(8,128)(2,1)S(1)} %copy-done.1, bf16[1,13,256,256]{3,2,1,0:T(8,128)(2,1)S(1)} %collective-permute-done.beside, bf16[16,256,256]{2,1,0:T(8,128)(2,1)S(1)} %get-tuple-element.24.middle, ...), custom_call_target="tpu_custom_call" | custom-call | flops 4026531840 | bytes 4194304 | tf_op jit(solution)/shard_map/last/pallas_call | solution.py:400
  (3 shorter events, 0.1 us)
Async XLA Ops:
  0.0 1.5 %copy-start = (bf16[1,13,256,256]{3,2,1,0:T(8,128)(2,1)S(1)}, bf16[1,13,256,256]{3,2,1,0:T(8,128)(2,1)}, u32[]{:S(2)}) copy-start(bf16[1,13,256,256]{3,2,1,0:T(8,128)(2,1)} %own.7) | copy-start | bytes 5111812
  1.6 20.1 %collective-permute-start.1 = (bf16[1,4,256,256]{3,2,1,0:T(8,128)(2,1)S(1)}, bf16[1,4,256,256]{3,2,1,0:T(8,128)(2,1)S(1)}, u32[]{:S(2)}, u32[]{:S(2)}) collective-permute-start(bf16[1,4,256,256]{3,2,1,0:T(8,128)(2,1)S(1)} %get-tuple-element.19), channel_id=1, source_target_pairs={{0,24},{1,9},{2,10},{3,27},{4,28},{5,13},{6,14},{7,31},{8,0},{9,17... | collective-permute-start | bytes 1572872 | tf_op jit(solution)/shard_map/ppermute | solution.py:434
  6.7 39.4 %collective-permute-start.9 = (bf16[1,8,256,256]{3,2,1,0:T(8,128)(2,1)S(1)}, bf16[1,8,256,256]{3,2,1,0:T(8,128)(2,1)S(1)}, u32[]{:S(2)}, u32[]{:S(2)}) collective-permute-start(bf16[1,8,256,256]{3,2,1,0:T(8,128)(2,1)S(1)} %get-tuple-element.26), channel_id=1, source_target_pairs={{0,4},{2,6},{4,0},{6,2},{1,5},{3,7},{5,1},{7,3},{8,12},{10,14},{12... | collective-permute-start | bytes 3145736 | tf_op jit(solution)/shard_map/ppermute | solution.py:445
  8.2 23.1 %collective-permute-start.2 = (bf16[1,4,256,256]{3,2,1,0:T(8,128)(2,1)S(1)}, bf16[1,4,256,256]{3,2,1,0:T(8,128)(2,1)S(1)}, u32[]{:S(2)}, u32[]{:S(2)}) collective-permute-start(bf16[1,4,256,256]{3,2,1,0:T(8,128)(2,1)S(1)} %get-tuple-element.22), channel_id=1, source_target_pairs={{0,28},{2,30},{4,8},{6,10},{8,4},{10,6},{12,16},{14,18},{16,12},{1... | collective-permute-start | bytes 1572872 | tf_op jit(solution)/shard_map/ppermute | solution.py:441
  8.6 39.8 %collective-permute-start = (bf16[1,13,256,256]{3,2,1,0:T(8,128)(2,1)S(1)}, bf16[1,13,256,256]{3,2,1,0:T(8,128)(2,1)S(1)}, u32[]{:S(2)}, u32[]{:S(2)}) collective-permute-start(bf16[1,13,256,256]{3,2,1,0:T(8,128)(2,1)S(1)} %copy-done), channel_id=1, source_target_pairs={{0,2},{2,0},{4,6},{6,4},{1,3},{3,1},{5,7},{7,5},{8,10},{10,8},{12,... | collective-permute-start | bytes 5111816 | tf_op jit(solution)/shard_map/ppermute | solution.py:445
  21.7 12.8 %collective-permute-start.3 = (bf16[1,4,256,256]{3,2,1,0:T(8,128)(2,1)S(1)}, bf16[1,4,256,256]{3,2,1,0:T(8,128)(2,1)S(1)}, u32[]{:S(2)}, u32[]{:S(2)}) collective-permute-start(bf16[1,4,256,256]{3,2,1,0:T(8,128)(2,1)S(1)} %collective-permute-done.1.refs_0_), channel_id=1, source_target_pairs={{0,3},{1,2},{2,1},{3,0},{4,7},{5,6},{6,5},{7,4},{8,11},{9,10},{10,... | collective-permute-start | bytes 1572872 | tf_op jit(solution)/shard_map/ppermute | solution.py:455
  21.8 12.8 %collective-permute-start.4 = (bf16[1,2,256,256]{3,2,1,0:T(8,128)(2,1)S(1)}, bf16[1,2,256,256]{3,2,1,0:T(8,128)(2,1)S(1)}, u32[]{:S(2)}, u32[]{:S(2)}) collective-permute-start(bf16[1,2,256,256]{3,2,1,0:T(8,128)(2,1)S(1)} %get-tuple-element.23), channel_id=1, source_target_pairs={{0,20},{1,13},{2,14},{3,23},{4,24},{5,17},{6,18},{7,27},{8,28},{9,... | collective-permute-start | bytes 786440 | tf_op jit(solution)/shard_map/ppermute | solution.py:434
  31.4 10.9 %collective-permute-start.8 = (bf16[1,3,256,256]{3,2,1,0:T(8,128)(2,1)S(1)}, bf16[1,3,256,256]{3,2,1,0:T(8,128)(2,1)S(1)}, u32[]{:S(2)}, u32[]{:S(2)}) collective-permute-start(bf16[1,3,256,256]{3,2,1,0:T(8,128)(2,1)S(1)} %cut.3), channel_id=1, source_target_pairs={{0,3},{1,2},{2,1},{3,0},{4,7},{5,6},{6,5},{7,4},{8,11},{9,10},{10,... | collective-permute-start | bytes 1179656 | tf_op jit(solution)/shard_map/ppermute | solution.py:455
  34.6 13.3 %collective-permute-start.7 = (bf16[1,2,256,256]{3,2,1,0:T(8,128)(2,1)S(1)}, bf16[1,2,256,256]{3,2,1,0:T(8,128)(2,1)S(1)}, u32[]{:S(2)}, u32[]{:S(2)}) collective-permute-start(bf16[1,2,256,256]{3,2,1,0:T(8,128)(2,1)S(1)} %cut.2), channel_id=1, source_target_pairs={{0,3},{1,2},{2,1},{3,0},{4,7},{5,6},{6,5},{7,4},{8,11},{9,10},{10,... | collective-permute-start | bytes 786440 | tf_op jit(solution)/shard_map/ppermute | solution.py:455
  36.5 12.0 %copy-start.1 = (bf16[1,13,256,256]{3,2,1,0:T(8,128)(2,1)S(1)}, bf16[1,13,256,256]{3,2,1,0:T(8,128)(2,1)}, u32[]{:S(2)}) copy-start(bf16[1,13,256,256]{3,2,1,0:T(8,128)(2,1)} %own.7) | copy-start | bytes 5111812
  36.5 13.7 %collective-permute-start.6 = (bf16[1,8,256,256]{3,2,1,0:T(8,128)(2,1)S(1)}, bf16[1,8,256,256]{3,2,1,0:T(8,128)(2,1)S(1)}, u32[]{:S(2)}, u32[]{:S(2)}) collective-permute-start(bf16[1,8,256,256]{3,2,1,0:T(8,128)(2,1)S(1)} %bundle.3.near.refs_1_), channel_id=1, source_target_pairs={{0,2},{2,0},{4,6},{6,4},{1,3},{3,1},{5,7},{7,5},{8,10},{10,8},{12,... | collective-permute-start | bytes 3145736 | tf_op jit(solution)/shard_map/ppermute | solution.py:445
  42.2 8.0 %collective-permute-start.5 = (bf16[1,8,256,256]{3,2,1,0:T(8,128)(2,1)S(1)}, bf16[1,8,256,256]{3,2,1,0:T(8,128)(2,1)S(1)}, u32[]{:S(2)}, u32[]{:S(2)}) collective-permute-start(bf16[1,8,256,256]{3,2,1,0:T(8,128)(2,1)S(1)} %bundle.4.refs_6_), channel_id=1, source_target_pairs={{0,2},{2,0},{4,6},{6,4},{1,3},{3,1},{5,7},{7,5},{8,10},{10,8},{12,... | collective-permute-start | bytes 3145736 | tf_op jit(solution)/shard_map/ppermute | solution.py:445
  47.8 3.7 %collective-permute-start.11 = (bf16[1,8,256,256]{3,2,1,0:T(8,128)(2,1)S(1)}, bf16[1,8,256,256]{3,2,1,0:T(8,128)(2,1)S(1)}, u32[]{:S(2)}, u32[]{:S(2)}) collective-permute-start(bf16[1,8,256,256]{3,2,1,0:T(8,128)(2,1)S(1)} %collective-permute-done.9.pure.refs_0_), channel_id=1, source_target_pairs={{0,2},{2,0},{4,6},{6,4},{1,3},{3,1},{5,7},{7,5},{8,10},{10,8},{12,... | collective-permute-start | bytes 3145736 | tf_op jit(solution)/shard_map/ppermute | solution.py:445
  48.3 4.4 %collective-permute-start.10 = (bf16[1,5,256,256]{3,2,1,0:T(8,128)(2,1)S(1)}, bf16[1,5,256,256]{3,2,1,0:T(8,128)(2,1)S(1)}, u32[]{:S(2)}, u32[]{:S(2)}) collective-permute-start(bf16[1,5,256,256]{3,2,1,0:T(8,128)(2,1)S(1)} %bundle.5.refs_5_), channel_id=1, source_target_pairs={{0,2},{2,0},{4,6},{6,4},{1,3},{3,1},{5,7},{7,5},{8,10},{10,8},{12,... | collective-permute-start | bytes 1966088 | tf_op jit(solution)/shard_map/ppermute | solution.py:445
  51.5 1.2 %copy-start.2 = (s32[1,13]{1,0:T(1,128)S(1)}, s32[1,13]{1,0:T(1,128)}, u32[]{:S(2)}) copy-start(s32[1,13]{1,0:T(1,128)} %keep.1) | copy-start | bytes 160
